TPU v7x, 32 devices: a whole 2x2x4 slice. The times are simulated.
32 devices in a mesh: tok: 4 (over z), mod: 2 (over core), head: 4 (over y, x).
Axes of the slice: x: 2, y: 2, z: 4, core: 2. Of those that a mesh axis runs over, the one named last changes fastest.
Arguments:
- latents: bfloat16 [16, 128, 768], P('mod'), may hold values from -6 to 6
- video_tokens: bfloat16 [16, 6272, 768], P('mod', 'tok'), may hold values from -6 to 6
- text_tokens: bfloat16 [16, 40, 768], P('mod'), may hold values from -6 to 6
- frame_counts: int32 [16], P('mod'), may hold values from 4 to 16, as said below
- text_lengths: int32 [16], P('mod'), may hold values from 8 to 40
- drop_mask: int32 [16], P('mod'), may hold values from 0 to 1, as said below
- cotangent: bfloat16 [16, 128, 768], P('mod'), may hold values from -6 to 6
- norm_latent_gain: float32 [768], replicated, may hold values from 0.5 to 1.5
- norm_latent_bias: float32 [768], replicated, may hold values from -1.75 to 1.75
- norm_input_gain: float32 [768], replicated, may hold values from 0.5 to 1.5
- norm_input_bias: float32 [768], replicated, may hold values from -0.125 to 0.125
- cross_query: bfloat16 [768, 768], P(None, 'head'), may hold values from -0.21875 to 0.21875
- cross_key: bfloat16 [768, 768], P(None, 'head'), may hold values from -0.21875 to 0.21875
- cross_value: bfloat16 [768, 768], P(None, 'head'), may hold values from -0.21875 to 0.21875
- cross_output: bfloat16 [768, 768], P('head'), may hold values from -10 to 10
- norm_cross_gain: float32 [768], replicated, may hold values from 0.5 to 1.5
- norm_cross_bias: float32 [768], replicated, may hold values from -1.75 to 1.75
- cross_up: bfloat16 [768, 3072], P(None, 'head'), may hold values from -0.21875 to 0.21875
- cross_down: bfloat16 [3072, 768], P('head'), may hold values from -0.15625 to 0.15625
- norm_self_gain: float32 [768], replicated, may hold values from 0.5 to 1.5
- norm_self_bias: float32 [768], replicated, may hold values from -0.3125 to 0.3125
- self_query: bfloat16 [768, 768], P(None, 'head'), may hold values from -0.21875 to 0.21875
- self_key: bfloat16 [768, 768], P(None, 'head'), may hold values from -0.21875 to 0.21875
- self_value: bfloat16 [768, 768], P(None, 'head'), may hold values from -0.21875 to 0.21875
- self_output: bfloat16 [768, 768], P('head'), may hold values from -1.5 to 1.5
- norm_ffn_gain: float32 [768], replicated, may hold values from 0.5 to 1.5
- norm_ffn_bias: float32 [768], replicated, may hold values from -1.75 to 1.75
- self_up: bfloat16 [768, 3072], P(None, 'head'), may hold values from -0.21875 to 0.21875
- self_down: bfloat16 [3072, 768], P('head'), may hold values from -0.15625 to 0.15625
Outputs:
- latents_out: bfloat16 [16, 128, 768], P('mod')
- grad_latents: bfloat16 [16, 128, 768], P('mod')
- grad_video: bfloat16 [16, 6272, 768], P('mod', 'tok')
- grad_text: bfloat16 [16, 40, 768], P('mod')
- grad_norm_latent_gain: float32 [768], replicated
- grad_norm_latent_bias: float32 [768], replicated
- grad_norm_input_gain: float32 [768], replicated
- grad_norm_input_bias: float32 [768], replicated
- grad_cross_query: float32 [768, 768], P(None, 'head')
- grad_cross_key: float32 [768, 768], P(None, 'head')
- grad_cross_value: float32 [768, 768], P(None, 'head')
- grad_cross_output: float32 [768, 768], P('head')
- grad_norm_cross_gain: float32 [768], replicated
- grad_norm_cross_bias: float32 [768], replicated
- grad_cross_up: float32 [768, 3072], P(None, 'head')
- grad_cross_down: float32 [3072, 768], P('head')
- grad_norm_self_gain: float32 [768], replicated
- grad_norm_self_bias: float32 [768], replicated
- grad_self_query: float32 [768, 768], P(None, 'head')
- grad_self_key: float32 [768, 768], P(None, 'head')
- grad_self_value: float32 [768, 768], P(None, 'head')
- grad_self_output: float32 [768, 768], P('head')
- grad_norm_ffn_gain: float32 [768], replicated
- grad_norm_ffn_bias: float32 [768], replicated
- grad_self_up: float32 [768, 3072], P(None, 'head')
- grad_self_down: float32 [3072, 768], P('head')
Inputs may be any that keep to these rules, and one draw needn't show every extreme that they name: `frame_counts`: the clips form two halves, the first 8 and the rest; in each half one clip, drawn at random, has 16 frames, 40 text tokens and is never dropped. `drop_mask`: in each half of the clips at least one clip is dropped.
All inputs are finite; a program needn't handle non-finite values.
Results may differ from a plain program's by a relative error of at most 0.035.
Values may be sent and summed in bfloat16 or wider, within the bound.
No kernel may reach another device: no remote copies, remote signals or barrier semaphores. Data moves between devices by JAX's collectives and lax.ppermute only.
A program may use at most 256 MiB of HBM per device.

v0:
```python
import jax
import jax.numpy as jnp
from jax import lax
from jax.sharding import PartitionSpec as P

HEAD = 64
PATCH = 392


EPSILON = 1e-05
NEGATIVE = -1e30


def combined_all(x, axis, combine):
    everything = jax.tree.map(
        lambda part, kind: lax.all_gather(part.astype(kind), axis),
        x,
        (jnp.bfloat16, jnp.bfloat16, jnp.bfloat16),
    )

    def take(k):
        return jax.tree.map(lambda part, own: part[k].astype(own.dtype), everything, x)

    return lax.fori_loop(
        1, lax.axis_size(axis), lambda k, so_far: combine(so_far, take(k)), take(0)
    )


def normalize(rows):
    mean = jnp.mean(rows, -1, keepdims=True)
    centered = rows - mean
    rstd = lax.rsqrt(jnp.mean(centered * centered, -1, keepdims=True) + EPSILON)
    return (centered * rstd, rstd)


def norm_back(grad_out, normed, rstd, gain):
    scaled = grad_out * gain
    grad_in = rstd * (
        scaled
        - jnp.mean(scaled, -1, keepdims=True)
        - normed * jnp.mean(scaled * normed, -1, keepdims=True)
    )
    leading = tuple(range(grad_out.ndim - 1))
    return (grad_in, jnp.sum(grad_out * normed, leading), jnp.sum(grad_out, leading))


def project(rows, weight):
    return jnp.einsum("...d,df->...f", rows, weight, preferred_element_type=jnp.float32)


def project_back(grad, weight):
    return jnp.einsum("...f,df->...d", grad, weight, preferred_element_type=jnp.float32)


def flatten_rows(rows):
    return rows.reshape(-1, rows.shape[-1])


def weight_grad(rows, grad):
    return lax.dot_general(
        flatten_rows(rows),
        flatten_rows(grad),
        (((0,), (0,)), ((), ())),
        preferred_element_type=jnp.float32,
    )


def split_heads(rows):
    return rows.reshape(rows.shape[:-1] + (rows.shape[-1] // HEAD, HEAD))


def head_rows(partial_rows):
    return lax.psum(partial_rows.astype(jnp.bfloat16), "head").astype(jnp.float32)


def head_grads(partial_rows):
    return lax.psum(partial_rows.astype(jnp.bfloat16), "head").astype(jnp.float32)


def attend_part(queries, keys, values, valid):
    scale = HEAD ** (-0.5)
    scores = (
        jnp.einsum("clhe,cnhe->clhn", queries, keys, preferred_element_type=jnp.float32) * scale
    )
    mask = valid[:, None, None, :]
    masked = jnp.where(mask, scores, NEGATIVE)
    peak = jnp.max(masked, -1)
    weights = jnp.where(mask, jnp.exp(masked - peak[..., None]), 0.0)
    total = jnp.sum(weights, -1)
    summed = jnp.einsum(
        "clhn,cnhe->clhe", weights.astype(jnp.bfloat16), values, preferred_element_type=jnp.float32
    )
    return (peak, total, summed)


def combine_parts(former, latter):
    top = jnp.maximum(former[0], latter[0])
    first_factor = jnp.exp(former[0] - top)
    second_factor = jnp.exp(latter[0] - top)
    total = former[1] * first_factor + latter[1] * second_factor
    summed = former[2] * first_factor[..., None] + latter[2] * second_factor[..., None]
    return (top, total, summed)


def attend_back(queries, keys, values, valid, log_total, d_attended, delta):
    scale = HEAD ** (-0.5)
    scores = (
        jnp.einsum("clhe,cnhe->clhn", queries, keys, preferred_element_type=jnp.float32) * scale
    )
    probs = jnp.where(valid[:, None, None, :], jnp.exp(scores - log_total[..., None]), 0.0)
    d_probs = jnp.einsum("clhe,cnhe->clhn", d_attended, values, preferred_element_type=jnp.float32)
    d_scores = (probs * (d_probs - delta[..., None])).astype(jnp.bfloat16)
    d_query = (
        jnp.einsum("clhn,cnhe->clhe", d_scores, keys, preferred_element_type=jnp.float32) * scale
    )
    d_key = (
        jnp.einsum("clhn,clhe->cnhe", d_scores, queries, preferred_element_type=jnp.float32) * scale
    )
    d_value = jnp.einsum(
        "clhn,clhe->cnhe",
        probs.astype(jnp.bfloat16),
        d_attended,
        preferred_element_type=jnp.float32,
    )
    return (d_query, d_key, d_value)


def gelu_exact(values):
    return jax.nn.gelu(values, approximate=False)


def feed_forward(rows, gain, bias, upper, lower):
    normed, rstd = normalize(rows)
    inner = (normed * gain + bias).astype(jnp.bfloat16)
    pre = project(inner, upper)
    hidden = gelu_exact(pre).astype(jnp.bfloat16)
    return (head_rows(project(hidden, lower)), (normed, rstd, inner, pre, hidden))


def feed_back(grad_rows, saved, gain, upper, lower):
    normed, rstd, inner, pre, hidden = saved
    grad_low = grad_rows.astype(jnp.bfloat16)
    d_hidden = project_back(grad_low, lower)
    unused, gelu_pull = jax.vjp(gelu_exact, pre)
    d_pre = gelu_pull(d_hidden)[0].astype(jnp.bfloat16)
    d_inner = head_grads(project_back(d_pre, upper))
    d_rows, d_gain, d_bias = norm_back(d_inner, normed, rstd, gain)
    return (grad_rows + d_rows, d_gain, d_bias, (inner, d_pre, hidden, grad_low))


def token_side(
    video_in,
    text_in,
    d_video_pair,
    d_text_pair,
    key_value,
    video_normed,
    video_rstd,
    text_normed,
    text_rstd,
    input_gain,
    first_shard,
):
    pair_partial = weight_grad(video_in, d_video_pair) + first_shard * weight_grad(
        text_in, d_text_pair
    )
    d_video_in, d_text_in = (
        lax.psum(project_back(d_video_pair, key_value).astype(jnp.bfloat16), "head").astype(
            jnp.float32
        ),
        lax.psum(project_back(d_text_pair, key_value).astype(jnp.bfloat16), "head").astype(
            jnp.float32
        ),
    )
    d_video, video_gain_grad, video_bias_grad = norm_back(
        d_video_in, video_normed, video_rstd, input_gain
    )
    d_text, text_gain_grad, text_bias_grad = norm_back(
        d_text_in, text_normed, text_rstd, input_gain
    )
    pair_sum, gain_sum, bias_sum = lax.psum(
        (
            pair_partial,
            video_gain_grad + first_shard * text_gain_grad,
            video_bias_grad + first_shard * text_bias_grad,
        ),
        ("tok", "mod"),
    )
    return (d_video, d_text, pair_sum, gain_sum, bias_sum)


def on_device(
    latents,
    video_tokens,
    text_tokens,
    frame_counts,
    text_lengths,
    drop_mask,
    cotangent,
    norm_latent_gain,
    norm_latent_bias,
    norm_input_gain,
    norm_input_bias,
    cross_query,
    cross_key,
    cross_value,
    cross_output,
    norm_cross_gain,
    norm_cross_bias,
    cross_up,
    cross_down,
    norm_self_gain,
    norm_self_bias,
    self_query,
    self_key,
    self_value,
    self_output,
    norm_ffn_gain,
    norm_ffn_bias,
    self_up,
    self_down,
):
    clips, lat_rows, width = latents.shape
    span = video_tokens.shape[1]
    text_span = text_tokens.shape[1]
    half_width = cross_key.shape[1]
    self_width = self_query.shape[1]
    keep_clip = (1 - drop_mask).astype(jnp.float32)
    keep = keep_clip[:, None, None]
    positions = lax.axis_index("tok") * span + jnp.arange(span)
    video_valid = positions[None, :] // PATCH < frame_counts[:, None]
    text_valid = jnp.arange(text_span)[None, :] < text_lengths[:, None]
    first_shard = (lax.axis_index("tok") == 0).astype(jnp.float32)
    state = latents.astype(jnp.float32)
    latent_normed, latent_rstd = normalize(state)
    queries_in = (latent_normed * norm_latent_gain + norm_latent_bias).astype(jnp.bfloat16)
    query_heads = split_heads(project(queries_in, cross_query).astype(jnp.bfloat16))
    video_normed, video_rstd = normalize(video_tokens.astype(jnp.float32))
    text_normed, text_rstd = normalize(text_tokens.astype(jnp.float32))
    video_in = (video_normed * norm_input_gain + norm_input_bias).astype(jnp.bfloat16)
    text_in = (text_normed * norm_input_gain + norm_input_bias).astype(jnp.bfloat16)
    key_value = jnp.concatenate([cross_key, cross_value], axis=1)
    video_pair = project(video_in, key_value).astype(jnp.bfloat16)
    text_pair = project(text_in, key_value).astype(jnp.bfloat16)
    video_keys = split_heads(video_pair[..., :half_width])
    video_values = split_heads(video_pair[..., half_width:])
    text_keys = split_heads(text_pair[..., :half_width])
    text_values = split_heads(text_pair[..., half_width:])
    triple = jnp.concatenate([self_query, self_key, self_value], axis=1)
    peak, total, summed = attend_part(query_heads, video_keys, video_values, video_valid)
    peak, total, summed = combined_all((peak, total, summed), "tok", combine_parts)
    peak, total, summed = combine_parts(
        (peak, total, summed), attend_part(query_heads, text_keys, text_values, text_valid)
    )
    cross_attended = summed / total[..., None]
    cross_log_total = peak + jnp.log(total)
    cross_low = cross_attended.reshape(clips, lat_rows, -1).astype(jnp.bfloat16)
    first = state + keep * head_rows(project(cross_low, cross_output))
    cross_mlp, cross_saved = feed_forward(
        first, norm_cross_gain, norm_cross_bias, cross_up, cross_down
    )
    second = first + cross_mlp
    self_normed, self_rstd = normalize(second)
    self_in = (self_normed * norm_self_gain + norm_self_bias).astype(jnp.bfloat16)
    triple_rows = project(self_in, triple).astype(jnp.bfloat16)
    self_q = split_heads(triple_rows[..., :self_width])
    self_k = split_heads(triple_rows[..., self_width : 2 * self_width])
    self_v = split_heads(triple_rows[..., 2 * self_width :])
    all_valid = jnp.ones((clips, lat_rows), dtype=bool)
    self_peak, self_total, self_summed = attend_part(self_q, self_k, self_v, all_valid)
    self_attended = self_summed / self_total[..., None]
    self_log_total = self_peak + jnp.log(self_total)
    self_low = self_attended.reshape(clips, lat_rows, -1).astype(jnp.bfloat16)
    third = second + head_rows(project(self_low, self_output))
    self_mlp, self_saved = feed_forward(third, norm_ffn_gain, norm_ffn_bias, self_up, self_down)
    latents_out = (third + self_mlp).astype(jnp.bfloat16)
    grad = cotangent.astype(jnp.float32)
    grad_third, ffn_gain_grad, ffn_bias_grad, self_ffn_pairs = feed_back(
        grad, self_saved, norm_ffn_gain, self_up, self_down
    )
    self_branch = grad_third.astype(jnp.bfloat16)
    d_self_att = split_heads(project_back(self_branch, self_output).astype(jnp.bfloat16))
    self_delta = jnp.sum(d_self_att.astype(jnp.float32) * self_attended, -1)
    dq_self, dk_self, dv_self = attend_back(
        self_q, self_k, self_v, all_valid, self_log_total, d_self_att, self_delta
    )
    d_triple = jnp.concatenate(
        [
            dq_self.reshape(clips, lat_rows, -1),
            dk_self.reshape(clips, lat_rows, -1),
            dv_self.reshape(clips, lat_rows, -1),
        ],
        axis=-1,
    ).astype(jnp.bfloat16)
    d_self_in = head_grads(project_back(d_triple, triple))
    d_second, self_gain_grad, self_bias_grad = norm_back(
        d_self_in, self_normed, self_rstd, norm_self_gain
    )
    grad_second = grad_third + d_second
    grad_first, cross_gain_grad, cross_bias_grad, cross_ffn_pairs = feed_back(
        grad_second, cross_saved, norm_cross_gain, cross_up, cross_down
    )
    cross_branch = (keep * grad_first).astype(jnp.bfloat16)
    d_cross_att = split_heads(project_back(cross_branch, cross_output).astype(jnp.bfloat16))
    cross_delta = jnp.sum(d_cross_att.astype(jnp.float32) * cross_attended, -1)
    dq_video, dk_video, dv_video = attend_back(
        query_heads,
        video_keys,
        video_values,
        video_valid,
        cross_log_total,
        d_cross_att,
        cross_delta,
    )
    dq_text, dk_text, dv_text = attend_back(
        query_heads, text_keys, text_values, text_valid, cross_log_total, d_cross_att, cross_delta
    )
    d_query = (
        (lax.psum(dq_video.astype(jnp.bfloat16), "tok").astype(jnp.float32) + dq_text)
        .reshape(clips, lat_rows, -1)
        .astype(jnp.bfloat16)
    )
    d_queries_in = head_grads(project_back(d_query, cross_query))
    d_latent, latent_gain_grad, latent_bias_grad = norm_back(
        d_queries_in, latent_normed, latent_rstd, norm_latent_gain
    )
    grad_latents = (grad_first + d_latent).astype(jnp.bfloat16)
    cross_inner, cross_d_pre, cross_hidden, cross_grad_low = cross_ffn_pairs
    self_inner, self_d_pre, self_hidden, self_grad_low = self_ffn_pairs
    shares = (
        lax.psum_scatter(
            weight_grad(queries_in, d_query).astype(jnp.bfloat16),
            "mod",
            scatter_dimension=0,
            tiled=True,
        ).astype(jnp.float32),
        lax.psum_scatter(
            weight_grad(cross_low, cross_branch).astype(jnp.bfloat16),
            "mod",
            scatter_dimension=0,
            tiled=True,
        ).astype(jnp.float32),
        lax.psum_scatter(
            weight_grad(cross_inner, cross_d_pre).astype(jnp.bfloat16),
            "mod",
            scatter_dimension=0,
            tiled=True,
        ).astype(jnp.float32),
        lax.psum_scatter(
            weight_grad(cross_hidden, cross_grad_low).astype(jnp.bfloat16),
            "mod",
            scatter_dimension=0,
            tiled=True,
        ).astype(jnp.float32),
        lax.psum_scatter(
            weight_grad(self_in, d_triple).astype(jnp.bfloat16),
            "mod",
            scatter_dimension=0,
            tiled=True,
        ).astype(jnp.float32),
        lax.psum_scatter(
            weight_grad(self_low, self_branch).astype(jnp.bfloat16),
            "mod",
            scatter_dimension=0,
            tiled=True,
        ).astype(jnp.float32),
        lax.psum_scatter(
            weight_grad(self_inner, self_d_pre).astype(jnp.bfloat16),
            "mod",
            scatter_dimension=0,
            tiled=True,
        ).astype(jnp.float32),
        lax.psum_scatter(
            weight_grad(self_hidden, self_grad_low).astype(jnp.bfloat16),
            "mod",
            scatter_dimension=0,
            tiled=True,
        ).astype(jnp.float32),
        lax.psum_scatter(
            latent_gain_grad.astype(jnp.bfloat16), "mod", scatter_dimension=0, tiled=True
        ).astype(jnp.float32),
        lax.psum_scatter(
            latent_bias_grad.astype(jnp.bfloat16), "mod", scatter_dimension=0, tiled=True
        ).astype(jnp.float32),
        lax.psum_scatter(
            cross_gain_grad.astype(jnp.bfloat16), "mod", scatter_dimension=0, tiled=True
        ).astype(jnp.float32),
        lax.psum_scatter(
            cross_bias_grad.astype(jnp.bfloat16), "mod", scatter_dimension=0, tiled=True
        ).astype(jnp.float32),
        lax.psum_scatter(
            self_gain_grad.astype(jnp.bfloat16), "mod", scatter_dimension=0, tiled=True
        ).astype(jnp.float32),
        lax.psum_scatter(
            self_bias_grad.astype(jnp.bfloat16), "mod", scatter_dimension=0, tiled=True
        ).astype(jnp.float32),
        lax.psum_scatter(
            ffn_gain_grad.astype(jnp.bfloat16), "mod", scatter_dimension=0, tiled=True
        ).astype(jnp.float32),
        lax.psum_scatter(
            ffn_bias_grad.astype(jnp.bfloat16), "mod", scatter_dimension=0, tiled=True
        ).astype(jnp.float32),
    )
    summed_grads = (
        lax.all_gather(shares[0].astype(jnp.bfloat16), "mod", axis=0, tiled=True).astype(
            jnp.float32
        ),
        lax.all_gather(shares[1].astype(jnp.bfloat16), "mod", axis=0, tiled=True).astype(
            jnp.float32
        ),
        lax.all_gather(shares[2].astype(jnp.bfloat16), "mod", axis=0, tiled=True).astype(
            jnp.float32
        ),
        lax.all_gather(shares[3].astype(jnp.bfloat16), "mod", axis=0, tiled=True).astype(
            jnp.float32
        ),
        lax.all_gather(shares[4].astype(jnp.bfloat16), "mod", axis=0, tiled=True).astype(
            jnp.float32
        ),
        lax.all_gather(shares[5].astype(jnp.bfloat16), "mod", axis=0, tiled=True).astype(
            jnp.float32
        ),
        lax.all_gather(shares[6].astype(jnp.bfloat16), "mod", axis=0, tiled=True).astype(
            jnp.float32
        ),
        lax.all_gather(shares[7].astype(jnp.bfloat16), "mod", axis=0, tiled=True).astype(
            jnp.float32
        ),
        lax.all_gather(shares[8].astype(jnp.bfloat16), "mod", axis=0, tiled=True).astype(
            jnp.float32
        ),
        lax.all_gather(shares[9].astype(jnp.bfloat16), "mod", axis=0, tiled=True).astype(
            jnp.float32
        ),
        lax.all_gather(shares[10].astype(jnp.bfloat16), "mod", axis=0, tiled=True).astype(
            jnp.float32
        ),
        lax.all_gather(shares[11].astype(jnp.bfloat16), "mod", axis=0, tiled=True).astype(
            jnp.float32
        ),
        lax.all_gather(shares[12].astype(jnp.bfloat16), "mod", axis=0, tiled=True).astype(
            jnp.float32
        ),
        lax.all_gather(shares[13].astype(jnp.bfloat16), "mod", axis=0, tiled=True).astype(
            jnp.float32
        ),
        lax.all_gather(shares[14].astype(jnp.bfloat16), "mod", axis=0, tiled=True).astype(
            jnp.float32
        ),
        lax.all_gather(shares[15].astype(jnp.bfloat16), "mod", axis=0, tiled=True).astype(
            jnp.float32
        ),
    )
    d_video_pair = jnp.concatenate(
        [dk_video.reshape(clips, span, -1), dv_video.reshape(clips, span, -1)], axis=-1
    ).astype(jnp.bfloat16)
    d_text_pair = jnp.concatenate(
        [dk_text.reshape(clips, text_span, -1), dv_text.reshape(clips, text_span, -1)], axis=-1
    ).astype(jnp.bfloat16)
    d_video, d_text, pair_sum, input_gain_grad, input_bias_grad = token_side(
        video_in,
        text_in,
        d_video_pair,
        d_text_pair,
        key_value,
        video_normed,
        video_rstd,
        text_normed,
        text_rstd,
        norm_input_gain,
        first_shard,
    )
    triple_grad = summed_grads[4]
    return (
        latents_out,
        grad_latents,
        d_video.astype(jnp.bfloat16),
        d_text.astype(jnp.bfloat16),
        summed_grads[8],
        summed_grads[9],
        input_gain_grad,
        input_bias_grad,
        summed_grads[0],
        pair_sum[:, :half_width],
        pair_sum[:, half_width:],
        summed_grads[1],
        summed_grads[10],
        summed_grads[11],
        summed_grads[2],
        summed_grads[3],
        summed_grads[12],
        summed_grads[13],
        triple_grad[:, :self_width],
        triple_grad[:, self_width : 2 * self_width],
        triple_grad[:, 2 * self_width :],
        summed_grads[5],
        summed_grads[14],
        summed_grads[15],
        summed_grads[6],
        summed_grads[7],
    )


def solution(mesh):
    in_specs = (
        P("mod", None, None),
        P("mod", "tok", None),
        P("mod", None, None),
        P("mod"),
        P("mod"),
        P("mod"),
        P("mod", None, None),
        P(),
        P(),
        P(),
        P(),
        P(None, "head"),
        P(None, "head"),
        P(None, "head"),
        P("head", None),
        P(),
        P(),
        P(None, "head"),
        P("head", None),
        P(),
        P(),
        P(None, "head"),
        P(None, "head"),
        P(None, "head"),
        P("head", None),
        P(),
        P(),
        P(None, "head"),
        P("head", None),
    )
    out_specs = (
        P("mod", None, None),
        P("mod", None, None),
        P("mod", "tok", None),
        P("mod", None, None),
        P(),
        P(),
        P(),
        P(),
        P(None, "head"),
        P(None, "head"),
        P(None, "head"),
        P("head", None),
        P(),
        P(),
        P(None, "head"),
        P("head", None),
        P(),
        P(),
        P(None, "head"),
        P(None, "head"),
        P(None, "head"),
        P("head", None),
        P(),
        P(),
        P(None, "head"),
        P("head", None),
    )
    return jax.shard_map(
        on_device, mesh=mesh, in_specs=in_specs, out_specs=out_specs, check_vma=False
    )
```

profile of v0, /device:TPU:0, one launch (start us, length us, event | category | flops | bytes accessed | tf_op | source)
XLA Modules:
  0.0 1418.8 jit_solution(13390788692598591794)
XLA Ops:
  30.7 15.8 %fusion.39 = bf16[8,1568,384]{2,1,0:T(8,128)(2,1)S(1)} fusion(bf16[8,1568,768]{2,1,0:T(8,128)(2,1)} %param.32, f32[768]{0:T(1024)S(1)} %copy-done.138, f32[768]{0:T(1024)S(1)} %copy-done.89, f32[8,1568]{1,0:T(8,128)S(1)} %add_rsqrt_fusion, f32[8,1568]{1,0:T(8,128)S(1)} %broadcast_multiply_fusion.2, bf16[768,192]{1,0:T(8,128)(2,1)S(1)} %copy.198, ...), kind=kOutput, calls=%fused_computation.53 | convolution fusion | flops 7462551552 | bytes 29597696 | tf_op jit(solution)/shard_map/...d,df->...f/dot_general | solution.py:48
  53.1 8.3 copy.202
  61.4 8.4 copy.199
  71.9 8.8 fusion.22
  87.6 8.5 fusion.131
  96.1 12.0 all-reduce.21.cloned.1.call-start
  115.1 8.3 fusion.25
  123.5 14.0 all-gather.1
  137.4 11.9 all-gather
  155.4 35.5 %while.19 = (s32[]{:T(128)}, f32[8,128,3]{1,0,2:T(8,128)}, f32[8,128,3]{1,0,2:T(8,128)}, f32[8,128,3,64]{3,2,1,0:T(4,128)}, bf16[4,8,128,3]{2,1,0,3:T(8,128)(2,1...) while((s32[]{:T(128)}, f32[8,128,3]{1,0,2:T(8,128)}, ...), condition=%wide.region_7.8_spmd, body=%wide.region_6.7_spmd.sunk | while | flops 811013 | bytes 3698831 | solution.py:24
  200.2 59.4 %all-reduce.21.cloned.1.call-done = bf16[8,128,768]{2,1,0:T(8,128)(2,1)} async-done(((bf16[8,128,768]{2,1,0:T(8,128)(2,1)}), bf16[8,128,768]{2,1,0:T(8,128)(2,1)}) %all-reduce.21.cloned.1.call-update) | async-done | bytes 1572880 | tf_op jit(solution)/shard_map/psum | solution.py:73
  265.6 7.9 multiply_convert_fusion.3
  277.2 61.0 %all-reduce.23.cloned.1.call-done = bf16[8,128,768]{2,1,0:T(8,128)(2,1)} async-done(((bf16[8,128,768]{2,1,0:T(8,128)(2,1)}), bf16[8,128,768]{2,1,0:T(8,128)(2,1)}) %all-reduce.23.cloned.1.call-update) | async-done | bytes 1572880 | tf_op jit(solution)/shard_map/psum | solution.py:73
  350.1 60.8 %all-reduce.25.cloned.1.call-done = bf16[8,128,768]{2,1,0:T(8,128)(2,1)} async-done(((bf16[8,128,768]{2,1,0:T(8,128)(2,1)}), bf16[8,128,768]{2,1,0:T(8,128)(2,1)}) %all-reduce.25.cloned.1.call-update) | async-done | bytes 1572880 | tf_op jit(solution)/shard_map/psum | solution.py:73
  431.4 59.8 %all-reduce.27.cloned.1.call-done = bf16[8,128,768]{2,1,0:T(8,128)(2,1)} async-done(((bf16[8,128,768]{2,1,0:T(8,128)(2,1)}), bf16[8,128,768]{2,1,0:T(8,128)(2,1)}) %all-reduce.27.cloned.1.call-update) | async-done | bytes 1572880 | tf_op jit(solution)/shard_map/psum | solution.py:77
  507.0 61.0 %all-reduce.29.cloned.1.call-done = bf16[8,128,768]{2,1,0:T(8,128)(2,1)} async-done(((bf16[8,128,768]{2,1,0:T(8,128)(2,1)}), bf16[8,128,768]{2,1,0:T(8,128)(2,1)}) %all-reduce.29.cloned.1.call-update) | async-done | bytes 1572880 | tf_op jit(solution)/shard_map/psum | solution.py:77
  593.7 51.0 %all-reduce.31.cloned.1.call-done = bf16[8,128,768]{2,1,0:T(8,128)(2,1)} async-done(((bf16[8,128,768]{2,1,0:T(8,128)(2,1)}), bf16[8,128,768]{2,1,0:T(8,128)(2,1)}) %all-reduce.31.cloned.1.call-update) | async-done | bytes 1572880 | tf_op jit(solution)/shard_map/psum | solution.py:77
  654.6 14.9 %fusion.19 = bf16[8,128,3,1568]{1,3,2,0:T(8,128)(2,1)} fusion(f32[8,3,1568,128]{3,2,1,0:T(8,128)} %copy-done.3, f32[8,128,3]{1,2,0:T(4,128)S(1)} %multiply_reduce_fusion.3, f32[8,128,3]{1,2,0:T(4,128)S(1)} %copy.220, pred[8,1568]{1,0:T(8,128)(4,1)S(1)} %broadcast_compare_fusion, bf16[8,1568,3,64]{1,3,2,0:T(8,128)(2,1)} %bitcast.285, ...), kind=kOutput, calls=%fused_computation.31 | convolution fusion | flops 645464064 | bytes 34148608 | tf_op jit(solution)/shard_map/clhe,cnhe->clhn/dot_general | solution.py:111
  669.5 8.1 fusion.134
  698.7 10.8 fusion.42
  709.6 8.1 copy.225
  717.7 9.3 multiply_convert_fusion
  727.0 8.1 copy.224
  740.4 20.0 %fusion.101 = f32[768,384]{1,0:T(8,128)} fusion(bf16[8,1568,192]{2,1,0:T(8,128)(2,1)} %copy.225, bf16[8,1568,192]{2,1,0:T(8,128)(2,1)} %copy.224, bf16[8,1568,768]{2,1,0:T(8,128)(2,1)} %param.32, f32[768]{0:T(1024)S(1)} %copy-done.139, f32[768]{0:T(1024)S(1)} %copy-done.90, f32[8,1568]{1,0:T(8,128)S(1)} %copy-done.50, f32[8,1568]{1,0:T(8,128)S(1)} %copy-done.46), kind=kOutput, calls=%fused_computation.186 | convolution fusion | flops 7475822592 | bytes 30187520 | tf_op jit(solution)/shard_map/dot_general | solution.py:60
  775.2 17.7 %convolution_convert_fusion = bf16[8,1568,768]{2,1,0:T(8,128)(2,1)} fusion(bf16[8,1568,192]{2,1,0:T(8,128)(2,1)} %copy.225, bf16[8,1568,192]{2,1,0:T(8,128)(2,1)} %copy.224, bf16[768,192]{1,0:T(8,128)(2,1)} %copy-done.55, bf16[768,192]{1,0:T(8,128)(2,1)S(1)} %copy-done.54), kind=kOutput, calls=%fused_computation.39 | convolution fusion | flops 7428833280 | bytes 29491200 | tf_op jit(solution)/shard_map/...f,df->...d/dot_general | solution.py:52
  819.6 41.8 %all-reduce.35.cloned.1.call-done = f32[768,384]{1,0:T(8,128)} async-done(((f32[768,384]{1,0:T(8,128)}), f32[768,384]{1,0:T(8,128)}) %all-reduce.35.cloned.1.call-update) | async-done | bytes 1179664 | tf_op jit(solution)/shard_map/psum | solution.py:181
  874.9 8.0 all-gather.19.cloned.1.call-done
  885.7 9.2 all-gather.17.cloned.1.call-done
  897.7 413.0 %all-reduce.37.cloned.1.call-done = (bf16[8,128,768]{2,1,0:T(8,128)(2,1)}, bf16[8,128,768]{2,1,0:T(8,128)(2,1)}, bf16[8,1568,768]{2,1,0:T(8,128)(2,1)}, bf16[8,40,768]{2,1,0:T(8,128)(2,1)}) async-done(((bf16[8,128,768]{2,1,0:T(8,128)(2,1)}, bf16[8,128,768]{2,1,0:T(8,128)(2,1)}, bf16[8,1568,768]{2,1,0:T(8,128)(2,1)}, bf16[8,40,768]{2,1,0:T(8,128)(2,1)}), (bf16[8,128,768]{2,1,0:T(8,128)(2,1)}, ...) | async-done | bytes 22904848 | tf_op jit(solution)/shard_map/psum | solution.py:73
  1342.9 21.3 %fusion.17 = (f32[768]{0:T(1024)S(1)}, f32[8,1568]{1,0:T(8,128)S(1)}, f32[8,1568]{1,0:T(8,128)S(1)}, f32[768]{0:T(1024)S(1)}) fusion(bf16[8,1568,768]{2,1,0:T(8,128)(2,1)} %param.32, bf16[8,1568,768]{2,1,0:T(8,128)(2,1)} %get-tuple-element.414, f32[8,1568]{1,0:T(8,128)S(1)} %copy-done.50, f32[8,1568]{1,0:T(8,128)S(1)} %copy-done.46, f32[768]{0:T(1024)S(1)} %copy-done.90), kind=kLoop, calls=%fused_computation.28 | loop fusion | flops 105945088 | bytes 38745088 | tf_op jit(solution)/shard_map/reduce_sum | solution.py:44
  1367.5 17.6 %all-reduce.8 = (f32[768]{0:T(1024)}, f32[768]{0:T(1024)}) all-reduce(f32[768]{0:T(1024)S(1)} %multiply_add_fusion.1, f32[768]{0:T(1024)S(1)} %multiply_add_fusion), channel_id=1, replica_groups=mesh['tok'=4,'mod'=2,'head'=4] {'tok','mod'}, use_global_device_ids=true, to_apply=%region_51.52 | all-reduce | flops 1536 | bytes 12288 | tf_op jit(solution)/shard_map/psum | solution.py:181
  1385.1 26.6 %fusion.14 = bf16[8,1568,768]{2,1,0:T(8,128)(2,1)} fusion(bf16[8,1568,768]{2,1,0:T(8,128)(2,1)} %param.32, bf16[8,1568,768]{2,1,0:T(8,128)(2,1)} %get-tuple-element.414, f32[8,1568]{1,0:T(8,128)S(1)} %broadcast_multiply_fusion, f32[8,1568]{1,0:T(8,128)S(1)} %broadcast_multiply_fusion.1, f32[768]{0:T(1024)S(1)} %copy-done.90, f32[8,1568]{1,0:T(8,128)S(1)} %copy-done.50, ...), kind=kLoop, calls=%fused_computation.25 | loop fusion | flops 96337920 | bytes 58006528 | tf_op jit(solution)/shard_map/convert_element_type | solution.py:477
  (552 shorter events, 310.2 us)
Async XLA Ops:
  7.2 406.9 %copy-start = (bf16[768,768]{1,0:T(8,128)(2,1)S(1)}, bf16[768,768]{1,0:T(8,128)(2,1)}, u32[]{:S(2)}) copy-start(bf16[768,768]{1,0:T(8,128)(2,1)} %param.58) | copy-start | bytes 3538948
  7.2 145.3 %all-gather.25.cloned.1.call-start = ((), (), s32[]{:S(2)}) async-start(), calls=%async_computation.26 | async-start | bytes 1966080 | tf_op jit(solution)/shard_map/all_gather | solution.py:16
  71.9 77.5 %copy-start.22 = (bf16[8,128,192]{1,2,0:T(8,128)(2,1)}, bf16[8,128,192]{1,2,0:T(8,128)(2,1)S(1)}, u32[]{:S(2)}) copy-start(bf16[8,128,192]{1,2,0:T(8,128)(2,1)S(1)} %convolution_convert_fusion.14) | copy-start | bytes 1179652
  96.1 163.5 %all-reduce.21.cloned.1.call-start = ((), (), s32[]{:S(2)}) async-start(), calls=%async_computation.8 | async-start | bytes 3145728 | tf_op jit(solution)/shard_map/psum | solution.py:73
  200.1 138.1 %all-reduce.23.cloned.1.call-start = ((), (), s32[]{:S(2)}) async-start(), calls=%async_computation.9 | async-start | bytes 3145728 | tf_op jit(solution)/shard_map/psum | solution.py:73
  200.2 138.0 %copy-start.103 = (f32[8]{0:T(128)}, f32[8]{0:T(128)S(1)}, u32[]{:S(2)}) copy-start(f32[8]{0:T(128)S(1)} %subtract_convert_fusion) | copy-start | bytes 100
  277.2 133.7 %all-reduce.25.cloned.1.call-start = ((), (), s32[]{:S(2)}) async-start(), calls=%async_computation.10 | async-start | bytes 3145728 | tf_op jit(solution)/shard_map/psum | solution.py:73
  349.8 141.4 %all-reduce.27.cloned.1.call-start = ((), (), s32[]{:S(2)}) async-start(), calls=%async_computation.11 | async-start | bytes 3145728 | tf_op jit(solution)/shard_map/psum | solution.py:77
  430.1 65.7 %copy-start.85 = (f32[8,128]{1,0:T(8,128)S(1)}, f32[8,128]{1,0:T(8,128)}, u32[]{:S(2)}) copy-start(f32[8,128]{1,0:T(8,128)} %copy-done.84) | copy-start | bytes 12292
  430.1 65.7 %copy-start.101 = (f32[8,128]{1,0:T(8,128)S(1)}, f32[8,128]{1,0:T(8,128)}, u32[]{:S(2)}) copy-start(f32[8,128]{1,0:T(8,128)} %copy-done.100) | copy-start | bytes 12292
  430.1 65.7 %copy-start.113 = (f32[768]{0:T(1024)S(1)}, f32[768]{0:T(1024)}, u32[]{:S(2)}) copy-start(f32[768]{0:T(1024)} %param.56) | copy-start | bytes 9220
  430.2 137.8 %all-reduce.29.cloned.1.call-start = ((), (), s32[]{:S(2)}) async-start(), calls=%async_computation.12 | async-start | bytes 3145728 | tf_op jit(solution)/shard_map/psum | solution.py:77
  431.4 68.8 %copy-start.71 = (f32[8,128,3]{1,2,0:T(4,128)}, f32[8,128,3]{1,2,0:T(4,128)S(1)}, u32[]{:S(2)}) copy-start(f32[8,128,3]{1,2,0:T(4,128)S(1)} %log_add_fusion) | copy-start | bytes 36868
  504.3 63.7 %copy-start.77 = (f32[8,128]{1,0:T(8,128)S(1)}, f32[8,128]{1,0:T(8,128)}, u32[]{:S(2)}) copy-start(f32[8,128]{1,0:T(8,128)} %copy-done.76) | copy-start | bytes 12292
  504.3 63.7 %copy-start.95 = (f32[8,128]{1,0:T(8,128)S(1)}, f32[8,128]{1,0:T(8,128)}, u32[]{:S(2)}) copy-start(f32[8,128]{1,0:T(8,128)} %copy-done.94) | copy-start | bytes 12292
  507.0 137.7 %all-reduce.31.cloned.1.call-start = ((), (), s32[]{:S(2)}) async-start(), calls=%async_computation.13 | async-start | bytes 3145728 | tf_op jit(solution)/shard_map/psum | solution.py:77
  583.6 114.0 %reduce-scatter.21.cloned.1.call-start = ((), (), s32[]{:S(2)}) async-start(), calls=%async_computation.22 | async-start | bytes 1769472 | tf_op jit(solution)/shard_map/reduce_scatter | solution.py:367
  589.1 109.1 %reduce-scatter.23.cloned.1.call-start = ((), (), s32[]{:S(2)}) async-start(), calls=%async_computation.24 | async-start | bytes 1769472 | tf_op jit(solution)/shard_map/reduce_scatter | solution.py:373
  589.2 65.4 %copy-start.62 = (f32[8,128,3]{1,2,0:T(4,128)}, f32[8,128,3]{1,2,0:T(4,128)S(1)}, u32[]{:S(2)}) copy-start(f32[8,128,3]{1,2,0:T(4,128)S(1)} %copy.220) | copy-start | bytes 36868
  593.6 171.7 %all-reduce.33.cloned.1.call-start = ((), (), s32[]{:S(2)}) async-start(), calls=%async_computation.14 | async-start | bytes 786432 | tf_op jit(solution)/shard_map/psum | solution.py:319
  677.7 91.0 %reduce-scatter.17.cloned.1.call-start = ((), (), s32[]{:S(2)}) async-start(), calls=%async_computation.19 | async-start | bytes 1769472 | tf_op jit(solution)/shard_map/reduce_scatter | solution.py:349
  682.6 92.4 %reduce-scatter.15.cloned.1.call-start = ((), (), s32[]{:S(2)}) async-start(), calls=%async_computation.17 | async-start | bytes 1769472 | tf_op jit(solution)/shard_map/reduce_scatter | solution.py:343
  687.8 110.5 %reduce-scatter.19.cloned.1.call-start = ((), (), s32[]{:S(2)}) async-start(), calls=%async_computation.21 | async-start | bytes 442368 | tf_op jit(solution)/shard_map/reduce_scatter | solution.py:361
  691.0 112.0 %reduce-scatter.27.cloned.1.call-start = ((), (), s32[]{:S(2)}) async-start(), calls=%async_computation.28 | async-start | bytes 1474560
  697.5 111.5 %all-gather.21.cloned.1.call-start = ((), (), s32[]{:S(2)}) async-start(), calls=%async_computation.23 | async-start | bytes 1769472 | tf_op jit(solution)/shard_map/all_gather | solution.py:423
  698.1 113.8 %all-gather.23.cloned.1.call-start = ((), (), s32[]{:S(2)}) async-start(), calls=%async_computation.25 | async-start | bytes 1769472 | tf_op jit(solution)/shard_map/all_gather | solution.py:426
  698.7 117.8 %reduce-scatter.13.cloned.1.call-start = ((), (), s32[]{:S(2)}) async-start(), calls=%async_computation.16 | async-start | bytes 442368 | tf_op jit(solution)/shard_map/reduce_scatter | solution.py:337
  739.9 121.5 %all-reduce.35.cloned.1.call-start = ((), (), s32[]{:S(2)}) async-start(), calls=%async_computation.15 | async-start | bytes 2359296 | tf_op jit(solution)/shard_map/psum | solution.py:181
  765.3 105.7 %reduce-scatter.25.cloned.1.call-start = ((), (), s32[]{:S(2)}) async-start(), calls=%async_computation.27 | async-start | bytes 589824
  768.6 114.3 %all-gather.19.cloned.1.call-start = ((), (), s32[]{:S(2)}) async-start(), calls=%async_computation.20 | async-start | bytes 1769472 | tf_op jit(solution)/shard_map/all_gather | solution.py:414
  769.2 125.7 %all-gather.17.cloned.1.call-start = ((), (), s32[]{:S(2)}) async-start(), calls=%async_computation.18 | async-start | bytes 1769472 | tf_op jit(solution)/shard_map/all_gather | solution.py:411
  775.0 535.8 %all-reduce.37.cloned.1.call-start = ((), (), s32[]{:S(2)}) async-start(), calls=%async_computation.29 | async-start | bytes 45809664 | tf_op jit(solution)/shard_map/psum | solution.py:73
  (137 other events, 1411.9 us)
Sparse Core Ops, SparseCore 0:
  96.3 40.1 all-gather.24
  200.2 59.3 all-reduce.20
  277.3 60.8 all-reduce.22
  350.0 60.8 all-reduce.24
  430.3 60.8 all-reduce.26
  507.1 60.8 all-reduce.28
  583.7 60.8 all-reduce.30
  646.9 8.6 reduce-scatter.20
  658.5 9.8 reduce-scatter.22
  677.8 37.3 all-reduce.32
  718.1 8.2 reduce-scatter.16
  729.1 9.8 reduce-scatter.14
  741.3 8.8 reduce-scatter.18
  753.0 9.6 reduce-scatter.26
  764.1 10.3 all-gather.20
  775.9 10.3 all-gather.22
  789.0 8.8 reduce-scatter.12
  800.6 60.6 all-reduce.34
  864.2 6.7 reduce-scatter.24
  872.4 10.3 all-gather.18
  884.5 10.3 all-gather.16
  900.0 410.7 all-reduce.36
where the time goes:
time: 1420 us
  waiting for transfers between devices  831 us (59%)
  matrix products  196 us (14%)
  other arithmetic  181 us (13%)
  local copies, waits for them, and re-layouts  109 us (8%)
  blocking collectives  70.5 us (5%)
  between operations  17.3 us (1%)
  starting transfers between devices  14.4 us (1%)
    psum x4, waiting for transfers between devices, head_rows(): lax.psum(partial_rows.astype(jnp.bfloat16), 'head').astype(jnp.float32)  594 us
    psum x3, waiting for transfers between devices, head_grads(): lax.psum(partial_rows.astype(jnp.bfloat16), 'head').astype(jnp.float32)  172 us
    dot_general x10, matrix products, weight_grad(): lax.dot_general(flatten_rows(rows), flatten_rows(grad), (((0,), (0,)), ((...  54.1 us
    psum x1, waiting for transfers between devices, token_side(): lax.psum((pair_partial, video_gain_grad + first_shard * text_gain_grad, v...  41.8 us
    reduce_sum x6, other arithmetic, norm_back(): jnp.sum(grad_out * normed, leading)  38.4 us
    unnamed x319, local copies, waits for them, and re-layouts  38.3 us
    dot_general x10, matrix products, project(): jnp.einsum('...d,df->...f', rows, weight, preferred_element_type=jnp.floa...  36.4 us
    dot_general x10, matrix products, project_back(): jnp.einsum('...f,df->...d', grad, weight, preferred_element_type=jnp.floa...  34.1 us
  transfers between devices with their start and end apart: 22, of which 11 were waited for; matrix products, arithmetic and copies ran while one was open for 14% of the time, Pallas kernels for 0%

commit v1 on v0

v1 whole, which is shorter than its diff:
```python
import jax
import jax.numpy as jnp
from jax import lax
from jax.experimental import pallas as pl
from jax.experimental.pallas import tpu as pltpu
from jax.sharding import PartitionSpec as P

HEAD = 64
PATCH = 392
EPSILON = 1e-05
NEGATIVE = -1e30
LOG2E = 1.4426950408889634
STAT = 16
BF = jnp.bfloat16
F32 = jnp.float32
VMEM_LIMIT = 60 * 2**20


def dot(a, b):
    return jnp.dot(a, b, preferred_element_type=F32)


def dot_tn(a, b):
    return lax.dot_general(a, b, (((0,), (0,)), ((), ())), preferred_element_type=F32)


def dot_nt(a, b):
    return lax.dot_general(a, b, (((1,), (1,)), ((), ())), preferred_element_type=F32)


def normalize(rows):
    mean = jnp.mean(rows, -1, keepdims=True)
    centered = rows - mean
    rstd = lax.rsqrt(jnp.mean(centered * centered, -1, keepdims=True) + EPSILON)
    return centered * rstd, rstd


def normed_rows(rows, gain, bias):
    return (normalize(rows)[0] * gain + bias).astype(BF)


def norm_back(grad_out, rows, gain):
    normed, rstd = normalize(rows)
    scaled = grad_out * gain
    grad_in = rstd * (
        scaled
        - jnp.mean(scaled, -1, keepdims=True)
        - normed * jnp.mean(scaled * normed, -1, keepdims=True)
    )
    return grad_in, jnp.sum(grad_out * normed, 0, keepdims=True), jnp.sum(grad_out, 0, keepdims=True)


def row_sums(a):
    n, width = a.shape
    if n % 8:
        a = jnp.concatenate([a, jnp.zeros((8 - n % 8, width), a.dtype)], 0)
    return jnp.sum(a.reshape(-1, 8, width), 0)


def erf(x):
    x = jnp.clip(x, -4.0, 4.0)
    s = x * x
    top = -2.72614225801306e-10
    for c in (
        2.77068142495902e-08,
        -2.10102402082508e-06,
        -5.69250639462346e-05,
        -7.34990630326855e-04,
        -2.95459980854025e-03,
        -1.60960333262415e-02,
    ):
        top = top * s + c
    low = -1.45660718464996e-05
    for c in (
        -2.13374055278905e-04,
        -1.68282697438203e-03,
        -7.37332916720468e-03,
        -1.42647390514189e-02,
    ):
        low = low * s + c
    return x * top / low


def gelu_share(x):
    return 0.5 * (1.0 + erf(x * 0.7071067811865476))


def gelu_slope(x):
    return gelu_share(x) + x * (0.3989422804014327 * jnp.exp(-0.5 * x * x))


def parts_of(value, count):
    parts = []
    for _ in range(count):
        part = value.astype(BF).astype(F32)
        parts.append(part)
        value = value - part
    return parts


def stat_tile(rows, height):
    place = lax.broadcasted_iota(jnp.int32, (height, rows[0].shape[1]), 0)
    tile = jnp.zeros(place.shape, F32)
    for k, row in enumerate(rows):
        tile = jnp.where(place == k, row, tile)
    return tile.astype(BF)


def diagonal(rows, row_block, column_block, count):
    shape = (row_block * count, column_block * count)
    r = lax.broadcasted_iota(jnp.int32, shape, 0) // row_block
    c = lax.broadcasted_iota(jnp.int32, shape, 1) // column_block
    return jnp.where(r == c, rows, 0.0).astype(BF)


def blocks_down(rows, count):
    return diagonal(jnp.concatenate([rows] * count, 0), rows.shape[0], HEAD, count)


def blocks_across(rows_t, count):
    return diagonal(jnp.concatenate([rows_t] * count, 1), HEAD, rows_t.shape[1], count)


def diagonal_parts(table, lat, count):
    return [
        table[HEAD * h : HEAD * (h + 1), lat * h : lat * (h + 1)] for h in range(count)
    ]


def kernel_call(body, outs, *args, name, scalars=()):
    spec = pl.BlockSpec(memory_space=pltpu.VMEM)
    smem = pl.BlockSpec(memory_space=pltpu.SMEM)
    return pl.pallas_call(
        body,
        out_shape=[jax.ShapeDtypeStruct(s, t) for s, t in outs],
        in_specs=[smem] * len(scalars) + [spec] * len(args),
        out_specs=[spec] * len(outs),
        compiler_params=pltpu.CompilerParams(vmem_limit_bytes=VMEM_LIMIT),
        name=name,
    )(*scalars, *args)


def tokens_forward_kernel(
    clip_ref, count_ref, text_count_ref,
    video_ref, text_ref, latents_ref, lat_gain_ref, lat_bias_ref, gain_ref, bias_ref,
    key_ref, value_ref, query_t_ref,
    out_ref, rows_t_ref,
    blocks, peak, total, summed,
):
    place, j = pl.program_id(0), pl.program_id(1)
    rows = video_ref.shape[1]
    lat = latents_ref.shape[1]
    width = key_ref.shape[1]
    heads = width // HEAD
    count = count_ref[place] - j * rows

    @pl.when(j == 0)
    def _():
        queries_in = normed_rows(latents_ref[0].astype(F32), lat_gain_ref[...], lat_bias_ref[...])
        rows_t = dot_nt(query_t_ref[...], queries_in).astype(BF).astype(F32) * HEAD**-0.5
        rows_t_ref[0] = rows_t.astype(BF)
        blocks[...] = blocks_across(rows_t, heads)
        peak[...] = jnp.full_like(peak, NEGATIVE).astype(BF).astype(F32)
        total[...] = jnp.zeros_like(total)
        summed[...] = jnp.zeros_like(summed)

    def block(x, limit):
        inputs_in = normed_rows(x.astype(F32), gain_ref[...], bias_ref[...])
        key = dot(inputs_in, key_ref[...]).astype(BF)
        value = dot(inputs_in, value_ref[...]).astype(BF)
        mask = lax.broadcasted_iota(jnp.int32, (x.shape[0], 1), 0) < limit
        scores = jnp.where(mask, dot(key, blocks[...]) * LOG2E, NEGATIVE)
        before = peak[...]
        top = jnp.maximum(before, jnp.max(scores, 0, keepdims=True)).astype(BF).astype(F32)
        weights = jnp.exp2(scores - top)
        factor = jnp.exp2(before - top)
        peak[...] = top
        total[...] = total[...] * factor + jnp.sum(weights, 0, keepdims=True)
        table = dot_tn(value, weights.astype(BF))
        for h, part in enumerate(diagonal_parts(table, lat, heads)):
            r = slice(HEAD * h, HEAD * (h + 1))
            summed[r] = summed[r] * factor[:, lat * h : lat * (h + 1)] + part

    @pl.when(count > 0)
    def _():
        block(video_ref[0], count)

    @pl.when((j == 0) & (text_count_ref[place] > 0))
    def _():
        block(text_ref[0], text_count_ref[place])

    @pl.when(j == pl.num_programs(1) - 1)
    def _():
        out_ref[0, :width] = summed[...].astype(BF)
        of = [slice(lat * h, lat * (h + 1)) for h in range(heads)]
        totals = [parts_of(total[:, c], 2) for c in of]
        stats = [peak[:, c] for c in of] + [t[0] for t in totals] + [t[1] for t in totals]
        out_ref[0, width:] = stat_tile(stats, STAT)


def tokens_forward(clip_of, count, text_count, video, text, latents, params, rows):
    clips, span, width = video.shape
    lat = latents.shape[1]
    own = params[-1].shape[0]
    full = lambda a: pl.BlockSpec(a.shape, lambda s, j, *_: (0,) * a.ndim)
    out = lambda height: pl.BlockSpec((1, height, lat), lambda s, j, *_: (s, 0, 0))
    clip_spec = lambda a: pl.BlockSpec((1,) + a.shape[1:], lambda s, j, c, *_: (c[s], 0, 0))
    return pl.pallas_call(
        tokens_forward_kernel,
        grid_spec=pltpu.PrefetchScalarGridSpec(
            num_scalar_prefetch=3,
            grid=(clips, span // rows),
            in_specs=[
                pl.BlockSpec((1, rows, width), lambda s, j, c, *_: (c[s], j, 0)),
                clip_spec(text),
                clip_spec(latents),
            ]
            + [full(a) for a in params],
            out_specs=[out(own + STAT), out(own)],
            scratch_shapes=[
                pltpu.VMEM((own, own // HEAD * lat), BF),
                pltpu.VMEM((1, own // HEAD * lat), F32),
                pltpu.VMEM((1, own // HEAD * lat), F32),
                pltpu.VMEM((own, lat), F32),
            ],
        ),
        out_shape=[
            jax.ShapeDtypeStruct((clips, own + STAT, lat), BF),
            jax.ShapeDtypeStruct((clips, own, lat), BF),
        ],
        compiler_params=pltpu.CompilerParams(
            vmem_limit_bytes=VMEM_LIMIT, dimension_semantics=("arbitrary", "arbitrary")
        ),
        name="tokens_forward",
    )(clip_of, count, text_count, video, text, latents, *params)


GROUP = 4


def tokens_back_kernel(
    clip_ref, query_place_ref, count_ref, text_count_ref, text_share_ref,
    video_ref, text_ref, latents_ref, lat_gain_ref, lat_bias_ref, gain_ref, bias_ref,
    pair_ref, pair_t_ref, q0, q1, q2, q3, d0, d1, d2, d3,
    d_video_ref, d_text_ref, weights_ref, d_query_ref,
    q_down, q_across, d_down, d_across, lse, delta, d_query,
):
    place, j = pl.program_id(0), pl.program_id(1)
    rows, width = video_ref.shape[1:]
    own, lat = q0.shape[1:]
    own_heads = own // HEAD
    groups = width // (GROUP * HEAD)
    count = count_ref[place] - j * rows
    text_count = text_count_ref[place]
    alive = text_count > 0

    @pl.when((place == 0) & (j == 0))
    def _():
        weights_ref[...] = jnp.zeros_like(weights_ref)

    @pl.when(j == 0)
    def _():
        d_query[...] = jnp.zeros_like(d_query)

    @pl.when((j == 0) & alive)
    def _():
        mine = lax.rem(place, 2) == 0
        first = [jnp.where(mine, a[0, :own].astype(F32), b[0, own : 2 * own].astype(F32)) for a, b in ((d0, d2), (d1, d3))]
        second = [jnp.where(mine, a[0, own : 2 * own].astype(F32), b[0, :own].astype(F32)) for a, b in ((d0, d2), (d1, d3))]
        for pieces, down, across in (
            ([q[0].astype(F32) for q in (q0, q1, q2, q3)], q_down, q_across),
            (first + second, d_down, d_across),
        ):
            rows_t = jnp.concatenate(pieces, 0)
            natural = rows_t.T
            for g in range(groups):
                cut = slice(GROUP * HEAD * g, GROUP * HEAD * (g + 1))
                down[g] = blocks_down(natural[:, cut], GROUP)
                across[g] = blocks_across(rows_t[cut], GROUP)
        tiles = [d[0, 2 * own :].astype(F32) for d in (d0, d1, d2, d3)]
        n = 2 * own_heads
        for kind, first_row, count_of in ((delta, 0, 2), (lse, 2 * n, 3)):
            for shard in range(4):
                a, b = tiles[shard % 2], tiles[2 + shard % 2]
                for h in range(own_heads):
                    at_a = first_row + h + own_heads * (shard // 2)
                    at_b = first_row + h + own_heads * (1 - shard // 2)
                    row = sum(
                        jnp.where(mine, a[at_a + n * i : at_a + n * i + 1], b[at_b + n * i : at_b + n * i + 1])
                        for i in range(count_of)
                    )
                    head = shard * own_heads + h
                    kind[:, lat * head : lat * (head + 1)] = row

    def block(x, limit, out_ref, share):
        counted = (lambda a: a) if share is None else (lambda a: a * share)
        normed, rstd = normalize(x.astype(F32))
        inputs_in = (normed * gain_ref[...] + bias_ref[...]).astype(BF)
        key = dot(inputs_in, pair_ref[:, :width]).astype(BF)
        value = dot(inputs_in, pair_ref[:, width:]).astype(BF)
        mask = lax.broadcasted_iota(jnp.int32, (x.shape[0], 1), 0) < limit
        d_keys, d_values = [], []
        for g in range(groups):
            cut = slice(GROUP * HEAD * g, GROUP * HEAD * (g + 1))
            lanes = slice(GROUP * lat * g, GROUP * lat * (g + 1))
            scores = dot(key[:, cut], q_across[g])
            d_probs = dot(value[:, cut], d_across[g])
            probs = jnp.where(mask, jnp.exp2(scores * LOG2E - lse[:, lanes]), 0.0)
            d_scores = (probs * (d_probs - delta[:, lanes])).astype(BF)
            d_values.append(dot(probs.astype(BF), d_down[g]).astype(BF))
            d_keys.append(dot(d_scores, q_down[g]).astype(BF))
            if g == 0:
                table = dot_tn(key[:, cut], d_scores)
                for h, part in enumerate(diagonal_parts(table, lat, own_heads)):
                    d_query[HEAD * h : HEAD * (h + 1)] += counted(part)
        d_key, d_value = jnp.concatenate(d_keys, 1), jnp.concatenate(d_values, 1)
        d_in = dot(d_key, pair_t_ref[:width]) + dot(d_value, pair_t_ref[width:])
        weights_ref[:own] += counted(dot_tn(d_keys[0], inputs_in)[:own])
        weights_ref[own : 2 * own] += counted(dot_tn(d_values[0], inputs_in)[:own])
        weights_ref[3 * own : 3 * own + 8] += counted(row_sums(d_in * normed))
        weights_ref[3 * own + 8 : 3 * own + 16] += counted(row_sums(d_in))
        scaled = d_in * gain_ref[...]
        d_x = rstd * (
            scaled
            - jnp.mean(scaled, -1, keepdims=True)
            - normed * jnp.mean(scaled * normed, -1, keepdims=True)
        )
        out_ref[0] = d_x.astype(BF)

    @pl.when(count > 0)
    def _():
        block(video_ref[0], count, d_video_ref, None)

    @pl.when(count <= 0)
    def _():
        d_video_ref[...] = jnp.zeros_like(d_video_ref)

    @pl.when((j == 0) & alive)
    def _():
        block(text_ref[0], text_count, d_text_ref, text_share_ref[0].astype(F32))

    @pl.when((j == 0) & jnp.logical_not(alive))
    def _():
        d_text_ref[...] = jnp.zeros_like(d_text_ref)

    @pl.when(j == pl.num_programs(1) - 1)
    def _():
        d_rows = (d_query[...] * HEAD**-0.5).astype(BF)
        d_query_ref[0] = d_rows

        @pl.when(alive)
        def _():
            queries_in = normed_rows(
                latents_ref[0].astype(F32), lat_gain_ref[...], lat_bias_ref[...]
            )
            weights_ref[2 * own : 3 * own] += dot(d_rows, queries_in)


WEIGHT_ROWS = 32


def tokens_back(scalars, video, text, latents, params, queries, d_attended, rows):
    clips, span, width = video.shape
    own, lat = queries[0].shape[1:]
    groups = width // (GROUP * HEAD)
    full = lambda a: pl.BlockSpec(
        a.shape, lambda s, j, *_: (0,) * a.ndim, pipeline_mode=pl.Buffered(1)
    )
    clip_spec = lambda a: pl.BlockSpec((1,) + a.shape[1:], lambda s, j, c, *_: (c[s], 0, 0))
    video_spec = pl.BlockSpec((1, rows, width), lambda s, j, c, *_: (c[s], j, 0))
    query_spec = pl.BlockSpec((1, own, lat), lambda s, j, c, q, *_: (q[s], 0, 0))
    d_spec = pl.BlockSpec((1,) + d_attended[0].shape[1:], lambda s, j, *_: (s // 2, 0, 0))
    weight_shape = (3 * own + WEIGHT_ROWS, width)
    return pl.pallas_call(
        tokens_back_kernel,
        grid_spec=pltpu.PrefetchScalarGridSpec(
            num_scalar_prefetch=len(scalars),
            grid=(clips, span // rows),
            in_specs=[video_spec, clip_spec(text), clip_spec(latents)]
            + [full(a) for a in params]
            + [query_spec] * 4
            + [d_spec] * 4,
            out_specs=[
                video_spec,
                clip_spec(text),
                pl.BlockSpec(weight_shape, lambda s, j, *_: (0, 0)),
                pl.BlockSpec((1, own, lat), lambda s, j, *_: (s, 0, 0)),
            ],
            scratch_shapes=[
                pltpu.VMEM((groups, GROUP * lat, GROUP * HEAD), BF),
                pltpu.VMEM((groups, GROUP * HEAD, GROUP * lat), BF),
                pltpu.VMEM((groups, GROUP * lat, GROUP * HEAD), BF),
                pltpu.VMEM((groups, GROUP * HEAD, GROUP * lat), BF),
                pltpu.VMEM((1, groups * GROUP * lat), F32),
                pltpu.VMEM((1, groups * GROUP * lat), F32),
                pltpu.VMEM((own, lat), F32),
            ],
        ),
        out_shape=[
            jax.ShapeDtypeStruct(video.shape, BF),
            jax.ShapeDtypeStruct(text.shape, BF),
            jax.ShapeDtypeStruct(weight_shape, F32),
            jax.ShapeDtypeStruct((clips, own, lat), BF),
        ],
        compiler_params=pltpu.CompilerParams(
            vmem_limit_bytes=VMEM_LIMIT, dimension_semantics=("arbitrary", "arbitrary")
        ),
        name="tokens_back",
    )(*scalars, video, text, latents, *params, *queries, *d_attended)


def combine_kernel(side_ref, *refs):
    parts, mine_ref, other_ref = refs[:-2], refs[-2], refs[-1]
    own = parts[0].shape[1] - STAT
    lat = parts[0].shape[2]
    heads = own // HEAD
    results = []
    for y in range(2):
        tiles = [p[y, own:].astype(F32) for p in parts]
        attended, logs = [], []
        for h in range(heads):
            peaks = [t[h : h + 1] for t in tiles]
            top = peaks[0]
            for p in peaks[1:]:
                top = jnp.maximum(top, p)
            total = jnp.zeros((1, lat), F32)
            summed = jnp.zeros((HEAD, lat), F32)
            for p, t, peak in zip(parts, tiles, peaks):
                factor = jnp.exp2(peak - top)
                a = t[heads + h : heads + h + 1] + t[2 * heads + h : 2 * heads + h + 1]
                total = total + a * factor
                summed = summed + p[y, HEAD * h : HEAD * (h + 1)].astype(F32) * factor
            some = total > 0.0
            safe = jnp.where(some, total, 1.0)
            attended.append(jnp.where(some, summed / safe, 0.0))
            logs.append(parts_of(jnp.where(some, top + jnp.log2(safe), 0.0), 3))
        stats = [logs[h][i] for i in range(3) for h in range(heads)]
        results.append((jnp.concatenate(attended, 0), stat_tile(stats, STAT).astype(F32)))
    first = side_ref[0] == 0
    for ref, (a, b) in ((mine_ref, results), (other_ref, results[::-1])):
        ref[:own] = jnp.where(first, a[0], b[0]).astype(BF)
        ref[own:] = jnp.where(first, a[1], b[1]).astype(BF)


def cross_forward_kernel(
    a0, a1, a2, a3, o0, o1, o2, o3, latents_ref, keep_ref, gain_ref, bias_ref,
    up0, up1, down0, down1,
    first_ref, inner_ref, pre_ref, hidden_ref, part_ref,
):
    own = o0.shape[0]
    branch = sum(dot_tn(a[:own], o[...]) for a, o in ((a0, o0), (a1, o1), (a2, o2), (a3, o3)))
    first = latents_ref[...].astype(F32) + keep_ref[...] * branch
    first_ref[...] = first
    inner = normed_rows(first, gain_ref[...], bias_ref[...])
    inner_ref[...] = inner
    out = None
    for k, (up, down) in enumerate(((up0, down0), (up1, down1))):
        pre = dot(inner, up[...])
        pre_ref[k] = pre
        hidden = (pre * gelu_share(pre)).astype(BF)
        hidden_ref[k] = hidden
        term = dot(hidden, down[...])
        out = term if out is None else out + term
    part_ref[...] = out.astype(BF)


def self_forward_kernel(
    first_ref, part0, part1, gain_ref, bias_ref, w0, w1, wt0, wt1, o0, o1,
    second_ref, inner_ref, rows_ref, query_t_ref, attended_ref, lse_ref, part_ref,
):
    second = first_ref[...] + (part0[...].astype(F32) + part1[...].astype(F32))
    second_ref[...] = second
    inner = normed_rows(second, gain_ref[...], bias_ref[...])
    inner_ref[...] = inner
    lat = inner.shape[0]
    out = None
    for k, (w, wt, o) in enumerate(((w0, wt0, o0), (w1, wt1, o1))):
        own = w.shape[2]
        heads = own // HEAD
        query = (dot(inner, w[0]).astype(BF).astype(F32) * HEAD**-0.5).astype(BF)
        key = dot(inner, w[1]).astype(BF)
        value = dot(inner, w[2]).astype(BF)
        for i, a in enumerate((query, key, value)):
            rows_ref[k, i] = a
        query_t = dot_nt(wt[...], inner).astype(BF).astype(F32) * HEAD**-0.5
        query_t_ref[k] = query_t.astype(BF)
        scores = dot(key, blocks_across(query_t, heads)) * LOG2E
        top = jnp.max(scores, 0, keepdims=True)
        weights = jnp.exp2(scores - top)
        total = jnp.sum(weights, 0, keepdims=True)
        table = dot_tn(value, weights.astype(BF))
        attended = jnp.concatenate(
            [
                part / total[:, lat * h : lat * (h + 1)]
                for h, part in enumerate(diagonal_parts(table, lat, heads))
            ],
            0,
        )
        attended_ref[k] = attended
        lse_ref[k] = top + jnp.log2(total)
        term = dot_tn(attended.astype(BF), o[...])
        out = term if out is None else out + term
    part_ref[...] = out.astype(BF)


def hidden_back(grad_low, pre, inner_parts, up, down):
    d_hidden = dot_nt(grad_low, down[...])
    d_pre = (d_hidden * gelu_slope(pre)).astype(BF)
    return d_pre, dot_nt(d_pre, up[...])


def last_back_kernel(
    second_ref, part0, part1, cotangent_ref, gain_ref, bias_ref, up0, up1, down0, down1,
    third_ref, inner_ref, hidden_ref, d_pre_ref, part_ref,
):
    third = second_ref[...] + (part0[...].astype(F32) + part1[...].astype(F32))
    third_ref[...] = third
    inner = normed_rows(third, gain_ref[...], bias_ref[...])
    inner_ref[...] = inner
    grad_low = cotangent_ref[...]
    out = None
    for k, (up, down) in enumerate(((up0, down0), (up1, down1))):
        pre = dot(inner, up[...])
        hidden_ref[k] = (pre * gelu_share(pre)).astype(BF)
        d_pre, term = hidden_back(grad_low, pre, None, up, down)
        d_pre_ref[k] = d_pre
        out = term if out is None else out + term
    part_ref[...] = out.astype(BF)


def down_kernel(hidden_ref, down0, down1, part_ref):
    part_ref[...] = (dot(hidden_ref[0], down0[...]) + dot(hidden_ref[1], down1[...])).astype(BF)


def self_back_kernel(
    cotangent_ref, third_ref, part0, part1, gain_ref,
    rows_ref, query_t_ref, attended_ref, lse_ref, w0, w1, o0, o1,
    grad_ref, sums_ref, branch_ref, d_rows_ref, low_ref, part_ref,
):
    d_inner = part0[...].astype(F32) + part1[...].astype(F32)
    d_x, d_gain, d_bias = norm_back(d_inner, third_ref[...], gain_ref[...])
    grad = cotangent_ref[...].astype(F32) + d_x
    grad_ref[...] = grad
    sums_ref[0:1] = d_gain
    sums_ref[1:2] = d_bias
    branch = grad.astype(BF)
    branch_ref[...] = branch
    lat = grad.shape[0]
    out = None
    for k, (w, o) in enumerate(((w0, o0), (w1, o1))):
        own = w.shape[2]
        heads = own // HEAD
        query, key, value = rows_ref[k, 0], rows_ref[k, 1], rows_ref[k, 2]
        d_att = dot_nt(branch, o[...]).astype(BF).astype(F32)
        d_att_t = dot_nt(o[...], branch).astype(BF).astype(F32)
        attended = attended_ref[k]
        low_ref[k] = attended.astype(BF)
        product = d_att_t * attended
        delta = jnp.concatenate(
            [
                jnp.sum(product[HEAD * h : HEAD * (h + 1)], 0, keepdims=True)
                for h in range(heads)
            ],
            1,
        )
        scores = dot(key, blocks_across(query_t_ref[k].astype(F32), heads))
        d_probs = dot(value, blocks_across(d_att_t, heads))
        probs = jnp.exp2(scores * LOG2E - lse_ref[k])
        d_scores = (probs * (d_probs - delta)).astype(BF)
        d_value = dot(probs.astype(BF), blocks_down(d_att, heads)).astype(BF)
        d_key = dot(d_scores, blocks_down(query.astype(F32), heads)).astype(BF)
        table = dot_tn(d_scores, key)
        column = lax.broadcasted_iota(jnp.int32, (lat, own), 1) // HEAD
        d_query = sum(
            jnp.where(column == h, table[lat * h : lat * (h + 1)], 0.0) for h in range(heads)
        )
        d_query = (d_query * HEAD**-0.5).astype(BF)
        for i, a in enumerate((d_query, d_key, d_value)):
            d_rows_ref[k, i] = a
            term = dot_nt(a, w[i])
            out = term if out is None else out + term
    part_ref[...] = out.astype(BF)


def cross_back_kernel(
    grad_ref, second_ref, part0, part1, gain_ref, pre_ref, up0, up1, down0, down1,
    out_ref, sums_ref, low_ref, d_pre_ref, part_ref,
):
    d_inner = part0[...].astype(F32) + part1[...].astype(F32)
    d_x, d_gain, d_bias = norm_back(d_inner, second_ref[...], gain_ref[...])
    grad = grad_ref[...] + d_x
    out_ref[...] = grad
    sums_ref[0:1] = d_gain
    sums_ref[1:2] = d_bias
    grad_low = grad.astype(BF)
    low_ref[...] = grad_low
    out = None
    for k, (up, down) in enumerate(((up0, down0), (up1, down1))):
        d_pre, term = hidden_back(grad_low, pre_ref[k], None, up, down)
        d_pre_ref[k] = d_pre
        out = term if out is None else out + term
    part_ref[...] = out.astype(BF)


def attended_back_kernel(
    grad_ref, first_ref, part0, part1, gain_ref, keep_ref, a0, a2, o0, o2,
    out_ref, sums_ref, branch_ref, packed_ref,
):
    d_inner = part0[...].astype(F32) + part1[...].astype(F32)
    d_x, d_gain, d_bias = norm_back(d_inner, first_ref[...], gain_ref[...])
    grad = grad_ref[...] + d_x
    out_ref[...] = grad
    sums_ref[0:1] = d_gain
    sums_ref[1:2] = d_bias
    branch = (keep_ref[...] * grad).astype(BF)
    branch_ref[...] = branch
    own = o0.shape[0]
    heads = own // HEAD
    deltas, logs = [], []
    for k, (a, o) in enumerate(((a0, o0), (a2, o2))):
        d_att_t = dot_nt(o[...], branch).astype(BF)
        packed_ref[own * k : own * (k + 1)] = d_att_t
        product = d_att_t.astype(F32) * a[:own].astype(F32)
        tile = a[own:].astype(F32)
        for h in range(heads):
            deltas.append(
                parts_of(jnp.sum(product[HEAD * h : HEAD * (h + 1)], 0, keepdims=True), 2)
            )
            logs.append([tile[heads * i + h : heads * i + h + 1] for i in range(3)])
    rows = [d[i] for i in range(2) for d in deltas] + [g[i] for i in range(3) for g in logs]
    packed_ref[2 * own :] = stat_tile(rows, 2 * STAT)


def latent_back_kernel(
    grad_ref, latents_ref, gain_ref, d0, d1, d2, d3, query_t_ref, out_ref, sums_ref
):
    own = d0.shape[0]
    d_in = sum(
        dot_tn(d[...], query_t_ref[own * k : own * (k + 1)]) for k, d in enumerate((d0, d1, d2, d3))
    )
    d_x, d_gain, d_bias = norm_back(d_in, latents_ref[...].astype(F32), gain_ref[...])
    out_ref[...] = (grad_ref[...] + d_x).astype(BF)
    sums_ref[0:1] = d_gain
    sums_ref[1:2] = d_bias


def weight_grads_kernel(*refs):
    count = len(refs) // 5
    for k in range(count):
        a0, b0, a1, b1 = refs[4 * k : 4 * k + 4]
        refs[4 * count + k][...] = (dot_tn(a0[...], b0[...]) + dot_tn(a1[...], b1[...])).astype(BF)


def weight_grads(pairs, name):
    outs = [((a0.shape[1], b0.shape[1]), BF) for a0, b0, a1, b1 in pairs]
    return kernel_call(
        weight_grads_kernel, outs, *[a for pair in pairs for a in pair], name=name
    )


def head_move(x, k):
    n = lax.axis_size("head")
    return lax.ppermute(x, "head", [(i, i ^ k) for i in range(n)])


def mod_move(x):
    return lax.ppermute(x, "mod", [(0, 1), (1, 0)])


def tok_move(x, shift):
    n = lax.axis_size("tok")
    return lax.ppermute(x, "tok", [(i, (i - shift) % n) for i in range(n)])


def after(x, *earlier):
    return lax.optimization_barrier((x, *earlier))[0]


def shared_head_move(x, k, axis):
    mod = lax.axis_index("mod")
    half = x.shape[axis] // 2
    part = head_move(lax.dynamic_slice_in_dim(x, mod * half, half, axis), k)
    other = mod_move(part)
    low = jnp.where(mod == 0, part, other)
    high = jnp.where(mod == 0, other, part)
    return jnp.concatenate([low, high], axis), part


def gather_latent_rows(rows, side_x):
    stages = jnp.stack([rows] + [tok_move(rows, k) for k in range(1, 4)])
    same, up, across = (head_move(stages, k) for k in (1, 2, 3))
    pick = lambda a, b: jnp.where(side_x == 0, a, b)
    mine = jnp.stack([pick(stages, same), pick(same, stages)], 1)
    other = jnp.stack([pick(up, across), pick(across, up)], 1)
    return jnp.stack([mine, other], 1)


def sum_over_tok_mod(x):
    n = lax.axis_size("tok")
    mod, tok = lax.axis_index("mod"), lax.axis_index("tok")
    half = x.shape[1] // 2
    low, high = x[:, :half], x[:, half:]
    own = jnp.where(mod == 0, low, high)
    own = own + mod_move(jnp.where(mod == 0, high, low).astype(BF)).astype(F32)
    if n != 4:
        own = lax.psum(own.astype(BF), "tok")
    else:
        step = x.shape[0] // n
        cut = lambda k: lax.dynamic_slice_in_dim(own, lax.rem(tok + k, n) * step, step, 0)
        received = [tok_move(cut(n - k).astype(BF), k) for k in range(1, n)]
        share = (cut(0) + sum(r.astype(F32) for r in received)).astype(BF)
        shares = [share] + [tok_move(share, k) for k in range(1, n)]
        own = jnp.zeros((x.shape[0], half), BF)
        for k, s in enumerate(shares):
            own = lax.dynamic_update_slice_in_dim(own, s, lax.rem(tok + k, n) * step, 0)
    other = mod_move(own)
    low = jnp.where(mod == 0, own, other)
    high = jnp.where(mod == 0, other, own)
    return jnp.concatenate([low, high], 1).astype(F32)


def on_device(
    latents,
    video_tokens,
    text_tokens,
    frame_counts,
    text_lengths,
    drop_mask,
    cotangent,
    norm_latent_gain,
    norm_latent_bias,
    norm_input_gain,
    norm_input_bias,
    cross_query,
    cross_key,
    cross_value,
    cross_output,
    norm_cross_gain,
    norm_cross_bias,
    cross_up,
    cross_down,
    norm_self_gain,
    norm_self_bias,
    self_query,
    self_key,
    self_value,
    self_output,
    norm_ffn_gain,
    norm_ffn_bias,
    self_up,
    self_down,
):
    clips, lat, width = latents.shape
    span = video_tokens.shape[1]
    own = cross_key.shape[1]
    shards = lax.axis_size("tok")
    zones = clips // 2
    tok, mod, head = lax.axis_index("tok"), lax.axis_index("mod"), lax.axis_index("head")
    zone = lax.rem(tok, zones)
    side_x, side_y = lax.rem(head, 2), head // 2
    rows = 784 if span % 784 == 0 else span
    row = lambda v: v[None]

    numbers = jnp.arange(clips, dtype=jnp.int32)
    live = 1 - drop_mask
    sort_key = drop_mask * clips + numbers
    rank = jnp.sum((sort_key[None, :] < sort_key[:, None]).astype(jnp.int32), 1)
    order = jnp.sum(jnp.where(rank[None, :] == numbers[:, None], numbers[None, :], 0), 1)
    pick = lambda table, at: jnp.sum(
        jnp.where(at[:, None] == numbers[None, :], table[None, :], 0), 1
    ).astype(jnp.int32)
    zone_of_place = lax.rem(zone + numbers // 2, zones)
    clip_plain = pick(order, 2 * zone_of_place + numbers % 2)
    query_place = 2 * (numbers // 2) + (numbers % 2 + side_y) % 2
    clip_place = pick(clip_plain, query_place)
    place_of_clip = jnp.sum(
        jnp.where(clip_place[None, :] == numbers[:, None], numbers[None, :], 0), 1
    )
    my_clip = clip_place[0]
    video_count = jnp.clip(frame_counts * PATCH - tok * span, 0, span) * live
    text_count = text_lengths * live
    last = (tok == shards - 1).astype(jnp.int32)

    my_latents = lax.dynamic_index_in_dim(latents, my_clip, 0, False)
    my_cotangent = lax.dynamic_index_in_dim(cotangent, my_clip, 0, False)
    other_cotangent = lax.dynamic_index_in_dim(cotangent, clip_place[1], 0, False)
    keep = lax.dynamic_index_in_dim(live, my_clip, 0, False).astype(F32) * jnp.ones((1, width), F32)

    outputs = [cross_output] + [head_move(cross_output, k) for k in (1, 2, 3)]
    cross_up_y, sent = shared_head_move(after(cross_up, *outputs), 2, 1)
    cross_down_y, sent = shared_head_move(after(cross_down, sent), 2, 0)
    self_w = jnp.stack([self_query, self_key, self_value])
    self_w_y, sent = shared_head_move(after(self_w, sent), 2, 1)
    self_output_y, sent = shared_head_move(after(self_output, sent), 2, 1)
    self_up_y, sent = shared_head_move(after(self_up, sent), 2, 1)
    self_down_y, sent = shared_head_move(after(self_down, sent), 2, 0)
    tables_t = jnp.stack([cross_key.T, cross_value.T, cross_query.T])
    others = []
    for k in (1, 2, 3):
        moved, sent = shared_head_move(after(tables_t, sent), k, 2)
        others.append(moved)
    tables = jnp.concatenate([tables_t] + others, 1)
    pair_t = tables[:2].reshape(2 * width, width)
    pair = pair_t.T
    all_query_t = tables[2]

    partial, query_t = tokens_forward(
        clip_plain, pick(video_count, clip_plain), pick(text_count, clip_plain) * last,
        video_tokens, text_tokens, latents,
        (row(norm_latent_gain), row(norm_latent_bias), row(norm_input_gain), row(norm_input_bias),
         cross_key, cross_value, cross_query.T),
        rows,
    )
    partial = partial.reshape(zones, 2, *partial.shape[1:])
    received = [tok_move(partial[(-k) % zones], k) for k in range(1, shards)]
    mine, other = kernel_call(
        combine_kernel, [(partial.shape[2:], BF)] * 2, partial[0], *received,
        name="combine", scalars=(side_y.reshape(1),),
    )
    attended = [mine, head_move(mine, 1), head_move(other, 2), head_move(other, 3)]
    queries = [query_t] + [head_move(after(query_t, attended[3]), k) for k in (1, 2, 3)]

    lw = (lat, width)
    first, inner1, pre1, hidden1, part = kernel_call(
        cross_forward_kernel,
        [(lw, F32), (lw, BF), ((2,) + lw, F32), ((2,) + lw, BF), (lw, BF)],
        *attended, *outputs, my_latents, keep, row(norm_cross_gain), row(norm_cross_bias),
        cross_up, cross_up_y, cross_down, cross_down_y, name="cross_forward",
    )
    heads = own // HEAD
    second, self_in, self_rows, self_query_t, self_attended, self_lse, part = kernel_call(
        self_forward_kernel,
        [(lw, F32), (lw, BF), ((2, 3, lat, own), BF), ((2, own, lat), BF), ((2, own, lat), F32),
         ((2, 1, heads * lat), F32), (lw, BF)],
        first, part, head_move(part, 1), row(norm_self_gain), row(norm_self_bias),
        self_w, self_w_y, self_query.T, self_w_y[0].T, self_output, self_output_y,
        name="self_forward",
    )
    third, inner2, hidden2, d_pre2, part = kernel_call(
        last_back_kernel,
        [(lw, F32), (lw, BF), ((2,) + lw, BF), ((2,) + lw, BF), (lw, BF)],
        second, part, head_move(part, 1), my_cotangent, row(norm_ffn_gain), row(norm_ffn_bias),
        self_up, self_up_y, self_down, self_down_y, name="last_back",
    )
    received = head_move(part, 1)
    (out_part,) = kernel_call(
        down_kernel, [(lw, BF)], after(hidden2, part), self_down, self_down_y, name="down"
    )
    grad_third, ffn_sums, self_branch, self_d_rows, self_low, part = kernel_call(
        self_back_kernel,
        [(lw, F32), ((2, width), F32), (lw, BF), ((2, 3, lat, own), BF), ((2, own, lat), BF), (lw, BF)],
        my_cotangent, third, part, received, row(norm_ffn_gain),
        self_rows, self_query_t, self_attended, self_lse, self_w, self_w_y, self_output, self_output_y,
        name="self_back",
    )
    grad_second, self_sums, low1, d_pre1, part = kernel_call(
        cross_back_kernel,
        [(lw, F32), ((2, width), F32), (lw, BF), ((2,) + lw, BF), (lw, BF)],
        grad_third, second, part, head_move(part, 1), row(norm_self_gain), pre1,
        cross_up, cross_up_y, cross_down, cross_down_y, name="cross_back",
    )
    grad_first, cross_sums, cross_branch, packed = kernel_call(
        attended_back_kernel,
        [(lw, F32), ((2, width), F32), (lw, BF), ((2 * own + 2 * STAT, lat), BF)],
        grad_second, first, part, head_move(part, 1), row(norm_cross_gain), keep,
        attended[0], attended[2], outputs[0], outputs[2], name="attended_back",
    )

    stages = jnp.stack([packed] + [tok_move(packed, k) for k in range(1, 4)])
    d_attended = [stages] + [head_move(stages, k) for k in (1, 2, 3)]
    d_video, d_text, token_weights, d_query_t = tokens_back(
        (clip_place, query_place, pick(video_count, clip_place), pick(text_count, clip_place),
         last.reshape(1)),
        video_tokens, text_tokens, latents,
        (row(norm_latent_gain), row(norm_latent_bias), row(norm_input_gain), row(norm_input_bias),
         pair, pair_t),
        queries, d_attended, rows,
    )

    out_rows = third + (out_part.astype(F32) + head_move(out_part, 1).astype(F32))
    half_of = lambda a: lax.dynamic_slice_in_dim(a, side_x * (lat // 2), lat // 2, 0)
    in_clip_order = lambda a: jnp.take(a.reshape(clips, lat, width), place_of_clip, axis=0)
    latents_out = in_clip_order(gather_latent_rows(half_of(out_rows).astype(BF), side_x))

    move_y = lambda a: head_move(a, 2)
    up2, down2 = weight_grads(
        [(inner2, d_pre2[0], move_y(inner2), move_y(d_pre2[1])),
         (hidden2[0], my_cotangent, move_y(hidden2[1]), other_cotangent)], "last_weights",
    )
    self_in_y, branch_y = move_y(self_in), move_y(self_branch)
    d_rows_y, low_y = move_y(self_d_rows[1]), move_y(self_low[1])
    wq, wk, wv, wo = weight_grads(
        [(self_in, self_d_rows[0, i], self_in_y, d_rows_y[i]) for i in range(3)]
        + [(self_low[0].T, self_branch, low_y.T, branch_y)], "self_weights",
    )
    up1, down1, co = weight_grads(
        [(inner1, d_pre1[0], move_y(inner1), move_y(d_pre1[1])),
         (hidden1[0], low1, move_y(hidden1[1]), move_y(low1)),
         (mine[:own].T, cross_branch, other[:own].T, move_y(cross_branch))], "cross_weights",
    )
    if shards > zones:
        counts = tok < zones
        up1, down1, co, wq, wk, wv, wo, up2, down2 = (
            jnp.where(counts, a, 0) for a in (up1, down1, co, wq, wk, wv, wo, up2, down2)
        )
    both = ("tok", "mod")
    up2, down2 = lax.psum((up2, down2), both)
    wq, wk, wv, wo = lax.psum(after((wq, wk, wv, wo), up2), both)
    up1, down1, co = lax.psum(after((up1, down1, co), wq), both)

    d_query_t = d_query_t.reshape(zones, 2, own, lat)
    received = [tok_move(d_query_t[(-k) % zones], k) for k in range(1, shards)]
    d_query = (d_query_t[0].astype(F32) + sum(r.astype(F32) for r in received)).astype(BF)
    d_queries = [d_query[0], head_move(d_query[0], 1), head_move(d_query[1], 2), head_move(d_query[1], 3)]
    my_grad, latent_sums = kernel_call(
        latent_back_kernel, [(lw, BF), ((2, width), F32)],
        grad_first, my_latents, row(norm_latent_gain), *d_queries, all_query_t, name="latent_back",
    )
    norm_sums = jnp.concatenate(
        [latent_sums, cross_sums, self_sums, ffn_sums, jnp.zeros((8, width), F32)], 0
    )
    gathered = gather_latent_rows(
        jnp.concatenate([half_of(my_grad), norm_sums.astype(BF)], 0), side_x
    )
    grad_latents = in_clip_order(gathered[:, :, :, : lat // 2])
    norm_sums = jnp.sum(gathered[:, :, 0, lat // 2 : lat // 2 + 8].astype(F32), (0, 1))
    norm_sums = norm_sums + mod_move(norm_sums)
    token_weights = sum_over_tok_mod(token_weights)
    input_sums = jnp.sum(token_weights[3 * own : 3 * own + 16].reshape(2, 8, width), 1)
    f32 = lambda a: a.astype(F32)
    return (
        latents_out,
        grad_latents,
        d_video,
        d_text,
        norm_sums[0],
        norm_sums[1],
        input_sums[0],
        input_sums[1],
        token_weights[2 * own : 3 * own].T,
        token_weights[:own].T,
        token_weights[own : 2 * own].T,
        f32(co),
        norm_sums[2],
        norm_sums[3],
        f32(up1),
        f32(down1),
        norm_sums[4],
        norm_sums[5],
        f32(wq),
        f32(wk),
        f32(wv),
        f32(wo),
        norm_sums[6],
        norm_sums[7],
        f32(up2),
        f32(down2),
    )


def solution(mesh):
    in_specs = (
        P("mod", None, None),
        P("mod", "tok", None),
        P("mod", None, None),
        P("mod"),
        P("mod"),
        P("mod"),
        P("mod", None, None),
        P(),
        P(),
        P(),
        P(),
        P(None, "head"),
        P(None, "head"),
        P(None, "head"),
        P("head", None),
        P(),
        P(),
        P(None, "head"),
        P("head", None),
        P(),
        P(),
        P(None, "head"),
        P(None, "head"),
        P(None, "head"),
        P("head", None),
        P(),
        P(),
        P(None, "head"),
        P("head", None),
    )
    out_specs = (
        P("mod", None, None),
        P("mod", None, None),
        P("mod", "tok", None),
        P("mod", None, None),
        P(),
        P(),
        P(),
        P(),
        P(None, "head"),
        P(None, "head"),
        P(None, "head"),
        P("head", None),
        P(),
        P(),
        P(None, "head"),
        P("head", None),
        P(),
        P(),
        P(None, "head"),
        P(None, "head"),
        P(None, "head"),
        P("head", None),
        P(),
        P(),
        P(None, "head"),
        P("head", None),
    )
    return jax.shard_map(
        on_device, mesh=mesh, in_specs=in_specs, out_specs=out_specs, check_vma=False
    )
```

time: 1420 us -> 558 us (0.39)
  waiting for transfers between devices: 831 us -> 129 us
  matrix products: 196 us -> 0 us
  Pallas kernels: 0 us -> 157 us
  other arithmetic: 181 us -> 56.5 us
  starting transfers between devices: 14.4 us -> 127 us
  blocking collectives: 70.5 us -> 0 us
  local copies, waits for them, and re-layouts: 109 us -> 73.3 us
    psum x9 -> x3, waiting for transfers between devices: 808 us -> 30.5 us  [the longest x2 30.5 us: on_device(): wq, wk, wv, wo = lax.psum(after((wq, wk, wv, wo), up2), both)]
    dot_general x48 -> x0, matrix products: 196 us -> none  [the longest x10 54.1 us: weight_grad(): lax.dot_general(flatten_rows(rows), flatten_rows(grad), (((0,), (0,)), ((...]
    pallas_call x0 -> x14, Pallas kernels: none -> 157 us  [the longest x1 80.5 us: tokens_back(): pl.pallas_call(tokens_back_kernel, grid_spec=pltpu.PrefetchScalarGridSpec...]
    ppermute x0 -> x81, starting transfers between devices: none -> 127 us  [the longest x48 58.1 us: head_move(): return lax.ppermute(x, 'head', [(i, i ^ k) for i in range(n)])]
    ppermute x0 -> x81, waiting for transfers between devices: none -> 98.5 us  [the longest x48 73.1 us: head_move(): return lax.ppermute(x, 'head', [(i, i ^ k) for i in range(n)])]
    reduce_sum x27 -> x7, other arithmetic: 85.7 us -> 1.5 us  [the longest x3 1.15 us: on_device(): jnp.sum(jnp.where(at[:, None] == numbers[None, :], table[None, :], 0), 1)]
    convert_element_type x25 -> x9, other arithmetic: 65 us -> 14.6 us  [the longest x6 10.3 us: on_device(): f32 = lambda a: a.astype(F32)]
    all_gather x14 -> x0, blocking collectives: 49.4 us -> none  [the longest x2 25.8 us: combined_all(): lax.all_gather(part.astype(kind), axis)]
  transfers between devices with their start and end apart: 22 -> 84, of which waited for: 11 -> 24; matrix products, arithmetic and copies ran while one was open for 14% -> 20% of each run, Pallas kernels for 0% -> 28%
where the time goes in v1:
time: 558 us; the launch traced here: 562 us
  Pallas kernels  157 us (28%)
  waiting for transfers between devices  129 us (23%)
  starting transfers between devices  127 us (23%)
  local copies, waits for them, and re-layouts  73.3 us (13%)
  other arithmetic  56.5 us (10%)
  between operations  19.6 us (4%)
    pallas_call x1, Pallas kernels, tokens_back(): pl.pallas_call(tokens_back_kernel, grid_spec=pltpu.PrefetchScalarGridSpec...  80.5 us
    ppermute x48, waiting for transfers between devices, head_move(): return lax.ppermute(x, 'head', [(i, i ^ k) for i in range(n)])  73.1 us
    ppermute x48, starting transfers between devices, head_move(): return lax.ppermute(x, 'head', [(i, i ^ k) for i in range(n)])  58.1 us
    pallas_call x12, Pallas kernels, kernel_call(): pl.pallas_call(body, out_shape=[jax.ShapeDtypeStruct(s, t) for s, t in ou...  50.3 us
    ppermute x21, starting transfers between devices, tok_move(): return lax.ppermute(x, 'tok', [(i, (i - shift) % n) for i in range(n)])  34.7 us
    ppermute x12, starting transfers between devices, mod_move(): return lax.ppermute(x, 'mod', [(0, 1), (1, 0)])  34.1 us
    psum x2, waiting for transfers between devices, on_device(): wq, wk, wv, wo = lax.psum(after((wq, wk, wv, wo), up2), both)  30.5 us
    pallas_call x1, Pallas kernels, tokens_forward(): pl.pallas_call(tokens_forward_kernel, grid_spec=pltpu.PrefetchScalarGridS...  26.2 us
  transfers between devices with their start and end apart: 84, of which 24 were waited for; matrix products, arithmetic and copies ran while one was open for 20% of the time, Pallas kernels for 28%

profile of v1, /device:TPU:0, one launch (start us, length us, event | category | flops | bytes accessed | tf_op | source)
XLA Modules:
  0.0 562.5 jit_solution(5205960532530832272)
XLA Ops:
  7.2 3.0 collective-permute-start.6
  23.3 26.2 %tokens_forward.1 = (bf16[8,208,128]{2,1,0:T(8,128)(2,1)}, bf16[8,192,128]{2,1,0:T(8,128)(2,1)}) custom-call(s32[8]{0:T(128)} %copy-done.86, s32[8]{0:T(128)} %get-tuple-element.281.count_ref, s32[8]{0:T(128)} %broadcast_multiply_fusion.text_count_ref, bf16[8,1568,768]{2,1,0:T(8,128)(2,1)} %video_ref.3, bf16[8,40,768]{2,1,0:T(8,128)(2,1)} %text_ref.3, ...), custom_call_target="tpu_custom_call" | custom-call | tf_op jit(solution)/shard_map/tokens_forward/pallas_call | solution.py:208
  85.5 3.3 collective-permute-done.11
  95.1 9.6 %collective-permute-done.14 = bf16[3,384,192]{1,2,0:T(8,128)(2,1)S(1)} collective-permute-done((bf16[3,384,192]{1,2,0:T(8,128)(2,1)}, bf16[3,384,192]{1,2,0:T(8,128)(2,1)S(1)}, u32[]{:S(2)}, u32[]{:S(2)}) %collective-permute-start.14) | collective-permute-done | bytes 442400 | tf_op jit(solution)/shard_map/ppermute | solution.py:663
  116.4 5.7 %cross_forward.1 = (f32[128,768]{1,0:T(8,128)}, bf16[128,768]{1,0:T(8,128)(2,1)}, f32[2,128,768]{2,1,0:T(8,128)}, bf16[2,128,768]{2,1,0:T(8,128)(2,1)}, bf16[128,768]{1,0:T(8,128)(2,1)}) custom-call(bf16[208,128]{1,0:T(8,128)(2,1)} %get-tuple-element.97.a0, bf16[208,128]{1,0:T(8,128)(2,1)} %collective-permute-done.3.a1, bf16[208,128]{1,0:T(8,128)(2,1)} %copy-done.57, ...), custom_call_target="tpu_custom_call" | custom-call | tf_op jit(solution)/shard_map/cross_forward/pallas_call | solution.py:133
  133.9 9.3 %collective-permute-done.21 = bf16[384,768]{1,0:T(8,128)(2,1)} collective-permute-done((bf16[384,768]{1,0:T(8,128)(2,1)}, bf16[384,768]{1,0:T(8,128)(2,1)}, u32[]{:S(2)}, u32[]{:S(2)}) %collective-permute-start.21) | collective-permute-done | bytes 589856 | tf_op jit(solution)/shard_map/ppermute | solution.py:663
  150.1 4.8 self_forward.1
  163.2 5.8 %last_back.1 = (f32[128,768]{1,0:T(8,128)}, bf16[128,768]{1,0:T(8,128)(2,1)}, bf16[2,128,768]{2,1,0:T(8,128)(2,1)}, bf16[2,128,768]{2,1,0:T(8,128)(2,1)}, bf16[128,768]{1,0:T(8,128)(2,1)}) custom-call(f32[128,768]{1,0:T(8,128)} %get-tuple-element.105.second_ref, bf16[128,768]{1,0:T(8,128)(2,1)} %get-tuple-element.106.part0, bf16[128,768]{1,0:T(8,128)(2,1)} %copy-done.59, ...), custom_call_target="tpu_custom_call" | custom-call | tf_op jit(solution)/shard_map/last_back/pallas_call | solution.py:133
  169.5 3.0 down.1
  179.3 5.8 %self_back.1 = (f32[128,768]{1,0:T(8,128)}, f32[2,768]{1,0:T(2,128)}, bf16[128,768]{1,0:T(8,128)(2,1)}, bf16[2,3,128,192]{3,2,1,0:T(8,128)(2,1)}, bf16[2,192,128...) custom-call(bf16[128,768]{1,0:T(8,128)(2,1)} %get-tuple-element.294.cotangent_ref.refs_5_, ...), custom_call_target="tpu_custom_call" | custom-call | tf_op jit(solution)/shard_map/self_back/pallas_call | solution.py:133
  193.7 3.0 collective-permute-start.25
  196.7 3.9 last_weights.1
  203.5 3.0 collective-permute-done.24
  211.6 6.5 %collective-permute-start.29 = (bf16[4,64,768]{2,1,0:T(8,128)(2,1)}, bf16[4,64,768]{2,1,0:T(8,128)(2,1)}, u32[]{:S(2)}, u32[]{:S(2)}) collective-permute-start(bf16[4,64,768]{2,1,0:T(8,128)(2,1)} %pad_maximum_fusion.10), channel_id=1, source_target_pairs={{0,3},{1,2},{2,1},{3,0},{4,7},{5,6},{6,5},{7,4},{8,11},{9,10},{10,... | collective-permute-start | bytes 1179656 | tf_op jit(solution)/shard_map/ppermute | solution.py:663
  218.8 6.2 %cross_back.1 = (f32[128,768]{1,0:T(8,128)}, f32[2,768]{1,0:T(2,128)}, bf16[128,768]{1,0:T(8,128)(2,1)}, bf16[2,128,768]{2,1,0:T(8,128)(2,1)}, bf16[128,768]{1,0:T(8,128)(2,1)}) custom-call(f32[128,768]{1,0:T(8,128)} %get-tuple-element.117.grad_ref, f32[128,768]{1,0:T(8,128)} %get-tuple-element.105.second_ref, bf16[128,768]{1,0:T(8,128)(2,1)} %get-tuple-element.118.part0, ...), custom_call_target="tpu_custom_call" | custom-call | tf_op jit(solution)/shard_map/cross_back/pallas_call | solution.py:133
  227.9 3.4 self_weights.1
  232.1 7.0 %collective-permute-done.32.part1 = bf16[128,768]{1,0:T(8,128)(2,1)S(1)} collective-permute-done((bf16[128,768]{1,0:T(8,128)(2,1)}, bf16[128,768]{1,0:T(8,128)(2,1)S(1)}, u32[]{:S(2)}, u32[]{:S(2)}) %collective-permute-start.32) | collective-permute-done | bytes 196640 | tf_op jit(solution)/shard_map/ppermute | solution.py:663
  244.1 3.5 collective-permute-start.44
  271.4 3.7 collective-permute-done.70.refs_3_
  276.1 7.4 %collective-permute-done.72.refs_7_ = bf16[128,768]{1,0:T(8,128)(2,1)S(1)} collective-permute-done((bf16[128,768]{1,0:T(8,128)(2,1)S(1)}, bf16[128,768]{1,0:T(8,128)(2,1)S(1)}, u32[]{:S(2)}, u32[]{:S(2)}) %collective-permute-start.72) | collective-permute-done | bytes 196640 | tf_op jit(solution)/shard_map/ppermute | solution.py:663
  288.4 4.2 cross_weights.1
  292.6 30.5 %all-reduce.7.cloned.1.call-done = bf16[768,192]{1,0:T(8,128)(2,1)} async-done(((bf16[768,192]{1,0:T(8,128)(2,1)}), bf16[768,192]{1,0:T(8,128)(2,1)}) %all-reduce.7.cloned.1.call-update) | async-done | bytes 294928 | tf_op jit(solution)/shard_map/psum | solution.py:908
  332.8 10.3 %collective-permute-done.46.d2 = bf16[4,416,128]{2,1,0:T(8,128)(2,1)} collective-permute-done((bf16[4,416,128]{2,1,0:T(8,128)(2,1)}, bf16[4,416,128]{2,1,0:T(8,128)(2,1)}, u32[]{:S(2)}, u32[]{:S(2)}) %collective-permute-start.46) | collective-permute-done | bytes 426016 | tf_op jit(solution)/shard_map/ppermute | solution.py:663
  343.2 80.5 %tokens_back.1 = (bf16[8,1568,768]{2,1,0:T(8,128)(2,1)}, bf16[8,40,768]{2,1,0:T(8,128)(2,1)}, f32[608,768]{1,0:T(8,128)}, bf16[8,192,128]{2,1,0:T(8,128)(2,1)}) custom-call(s32[8]{0:T(128)} %copy-done.78, s32[8]{0:T(128)} %copy-done.87, s32[8]{0:T(128)} %get-tuple-element.282.count_ref, s32[8]{0:T(128)} %get-tuple-element.279.text_count_ref, ...), custom_call_target="tpu_custom_call" | custom-call | tf_op jit(solution)/shard_map/tokens_back/pallas_call | solution.py:374
  426.4 3.0 collective-permute-start.48
  431.8 33.2 %collective-permute-start.61 = (bf16[608,384]{1,0:T(8,128)(2,1)}, bf16[608,384]{1,0:T(8,128)(2,1)}, u32[]{:S(2)}, u32[]{:S(2)}) collective-permute-start(bf16[608,384]{1,0:T(8,128)(2,1)} %select_convert_fusion), channel_id=1, source_target_pairs={{0,4},{4,0},{1,5},{5,1},{2,6},{6,2},{3,7},{7,3},{8,12},{12,8},{9,1... | collective-permute-start | bytes 1400840 | tf_op jit(solution)/shard_map/ppermute | solution.py:667
  488.3 5.3 collective-permute-done.55
  494.1 6.1 %collective-permute-done.63 = bf16[152,384]{1,0:T(8,128)(2,1)S(1)} collective-permute-done((bf16[152,384]{1,0:T(8,128)(2,1)S(1)}, bf16[152,384]{1,0:T(8,128)(2,1)S(1)}, u32[]{:S(2)}, u32[]{:S(2)}) %collective-permute-start.63) | collective-permute-done | bytes 116768 | tf_op jit(solution)/shard_map/ppermute | solution.py:672
  501.8 3.4 collective-permute-start.65
  517.0 3.7 collective-permute-done.67
  522.6 11.5 %collective-permute-done.58 = bf16[4,80,768]{2,1,0:T(8,128)(2,1)S(1)} collective-permute-done((bf16[4,80,768]{2,1,0:T(8,128)(2,1)S(1)}, bf16[4,80,768]{2,1,0:T(8,128)(2,1)S(1)}, u32[]{:S(2)}, u32[]{:S(2)}) %collective-permute-start.58) | collective-permute-done | bytes 491552 | tf_op jit(solution)/shard_map/ppermute | solution.py:663
  537.7 3.5 broadcast_select_fusion
  (460 shorter events, 223.6 us)
Async XLA Ops:
  7.2 259.6 %all-reduce.5.cloned.1.call-start = ((), (), s32[]{:S(2)}) async-start(), calls=%async_computation | async-start | bytes 2359296 | tf_op jit(solution)/shard_map/psum | solution.py:907
  7.2 42.3 %collective-permute-start.6 = (bf16[192,768]{1,0:T(8,128)(2,1)}, bf16[192,768]{1,0:T(8,128)(2,1)S(1)}, u32[]{:S(2)}, u32[]{:S(2)}) collective-permute-start(bf16[192,768]{1,0:T(8,128)(2,1)} %o0.7), channel_id=1, source_target_pairs={{0,1},{1,0},{2,3},{3,2},{4,5},{5,4},{6,7},{7,6},{8,9},{9,8},{10,11... | collective-permute-start | bytes 884744 | tf_op jit(solution)/shard_map/ppermute | solution.py:663
  10.3 39.3 %collective-permute-start.7 = (bf16[192,768]{1,0:T(8,128)(2,1)}, bf16[192,768]{1,0:T(8,128)(2,1)S(1)}, u32[]{:S(2)}, u32[]{:S(2)}) collective-permute-start(bf16[192,768]{1,0:T(8,128)(2,1)} %o0.7), channel_id=1, source_target_pairs={{0,2},{1,3},{2,0},{3,1},{4,6},{5,7},{6,4},{7,5},{8,10},{9,11},{10,... | collective-permute-start | bytes 884744 | tf_op jit(solution)/shard_map/ppermute | solution.py:663
  11.8 37.8 %collective-permute-start.8 = (bf16[192,768]{1,0:T(8,128)(2,1)}, bf16[192,768]{1,0:T(8,128)(2,1)S(1)}, u32[]{:S(2)}, u32[]{:S(2)}) collective-permute-start(bf16[192,768]{1,0:T(8,128)(2,1)} %o0.7), channel_id=1, source_target_pairs={{0,3},{1,2},{2,1},{3,0},{4,7},{5,6},{6,5},{7,4},{8,11},{9,10},{10,... | collective-permute-start | bytes 884744 | tf_op jit(solution)/shard_map/ppermute | solution.py:663
  54.3 24.0 %collective-permute-start = (bf16[2,208,128]{2,1,0:T(8,128)(2,1)}, bf16[2,208,128]{2,1,0:T(8,128)(2,1)}, u32[]{:S(2)}, u32[]{:S(2)}) collective-permute-start(bf16[2,208,128]{2,1,0:T(8,128)(2,1)} %get-tuple-element.329), channel_id=1, source_target_pairs={{0,24},{8,0},{16,8},{24,16},{1,25},{9,1},{17,9},{25,17},{2,26},{10... | collective-permute-start | bytes 319496 | tf_op jit(solution)/shard_map/ppermute | solution.py:672
  57.0 21.3 %collective-permute-start.1 = (bf16[2,208,128]{2,1,0:T(8,128)(2,1)S(1)}, bf16[2,208,128]{2,1,0:T(8,128)(2,1)}, u32[]{:S(2)}, u32[]{:S(2)}) collective-permute-start(bf16[2,208,128]{2,1,0:T(8,128)(2,1)S(1)} %get-tuple-element.328), channel_id=1, source_target_pairs={{0,16},{8,24},{16,0},{24,8},{1,17},{9,25},{17,1},{25,9},{2,18},{10... | collective-permute-start | bytes 319496 | tf_op jit(solution)/shard_map/ppermute | solution.py:672
  80.2 35.6 %collective-permute-start.3 = (bf16[208,128]{1,0:T(8,128)(2,1)}, bf16[208,128]{1,0:T(8,128)(2,1)}, u32[]{:S(2)}, u32[]{:S(2)}) collective-permute-start(bf16[208,128]{1,0:T(8,128)(2,1)} %get-tuple-element.97.a0), channel_id=1, source_target_pairs={{0,1},{1,0},{2,3},{3,2},{4,5},{5,4},{6,7},{7,6},{8,9},{9,8},{10,11... | collective-permute-start | bytes 159752 | tf_op jit(solution)/shard_map/ppermute | solution.py:663
  93.1 22.7 %collective-permute-start.4 = (bf16[208,128]{1,0:T(8,128)(2,1)S(1)}, bf16[208,128]{1,0:T(8,128)(2,1)S(1)}, u32[]{:S(2)}, u32[]{:S(2)}) collective-permute-start(bf16[208,128]{1,0:T(8,128)(2,1)S(1)} %copy-done.73), channel_id=1, source_target_pairs={{0,2},{1,3},{2,0},{3,1},{4,6},{5,7},{6,4},{7,5},{8,10},{9,11},{10,... | collective-permute-start | bytes 159752 | tf_op jit(solution)/shard_map/ppermute | solution.py:663
  122.1 27.4 %collective-permute-start.13 = (bf16[128,768]{1,0:T(8,128)(2,1)}, bf16[128,768]{1,0:T(8,128)(2,1)S(1)}, u32[]{:S(2)}, u32[]{:S(2)}) collective-permute-start(bf16[128,768]{1,0:T(8,128)(2,1)} %get-tuple-element.102.part0), channel_id=1, source_target_pairs={{0,1},{1,0},{2,3},{3,2},{4,5},{5,4},{6,7},{7,6},{8,9},{9,8},{10,11... | collective-permute-start | bytes 589832 | tf_op jit(solution)/shard_map/ppermute | solution.py:663
  132.6 22.8 %collective-permute-start.20 = (bf16[768,384]{1,0:T(8,128)(2,1)}, bf16[768,384]{1,0:T(8,128)(2,1)}, u32[]{:S(2)}, u32[]{:S(2)}) collective-permute-start(bf16[768,384]{1,0:T(8,128)(2,1)} %collective-permute-done.19), channel_id=1, source_target_pairs={{0,4},{4,0},{1,5},{5,1},{2,6},{6,2},{3,7},{7,3},{8,12},{12,8},{9,1... | collective-permute-start | bytes 1769480 | tf_op jit(solution)/shard_map/ppermute | solution.py:667
  156.8 43.9 %collective-permute-start.34 = (bf16[3,192,384]{2,1,0:T(8,128)(2,1)}, bf16[3,192,384]{2,1,0:T(8,128)(2,1)}, u32[]{:S(2)}, u32[]{:S(2)}) collective-permute-start(bf16[3,192,384]{2,1,0:T(8,128)(2,1)} %collective-permute-done.33), channel_id=1, source_target_pairs={{0,4},{4,0},{1,5},{5,1},{2,6},{6,2},{3,7},{7,3},{8,12},{12,8},{9,1... | collective-permute-start | bytes 1327112 | tf_op jit(solution)/shard_map/ppermute | solution.py:667
  191.7 34.0 %collective-permute-start.74 = (bf16[128,768]{1,0:T(8,128)(2,1)S(1)}, bf16[128,768]{1,0:T(8,128)(2,1)S(1)}, u32[]{:S(2)}, u32[]{:S(2)}) collective-permute-start(bf16[128,768]{1,0:T(8,128)(2,1)S(1)} %copy-done.28), channel_id=1, source_target_pairs={{0,2},{1,3},{2,0},{3,1},{4,6},{5,7},{6,4},{7,5},{8,10},{9,11},{10,... | collective-permute-start | bytes 589832 | tf_op jit(solution)/shard_map/ppermute | solution.py:663
  200.6 122.4 %all-reduce.7.cloned.1.call-start = ((), (), s32[]{:S(2)}) async-start(), calls=%async_computation.1 | async-start | bytes 786432 | tf_op jit(solution)/shard_map/psum | solution.py:908
  211.2 32.2 %collective-permute-start.28 = (bf16[4,64,768]{2,1,0:T(8,128)(2,1)}, bf16[4,64,768]{2,1,0:T(8,128)(2,1)S(1)}, u32[]{:S(2)}, u32[]{:S(2)}) collective-permute-start(bf16[4,64,768]{2,1,0:T(8,128)(2,1)} %pad_maximum_fusion.10), channel_id=1, source_target_pairs={{0,2},{1,3},{2,0},{3,1},{4,6},{5,7},{6,4},{7,5},{8,10},{9,11},{10,... | collective-permute-start | bytes 1179656 | tf_op jit(solution)/shard_map/ppermute | solution.py:663
  211.6 31.9 %collective-permute-start.29 = (bf16[4,64,768]{2,1,0:T(8,128)(2,1)}, bf16[4,64,768]{2,1,0:T(8,128)(2,1)}, u32[]{:S(2)}, u32[]{:S(2)}) collective-permute-start(bf16[4,64,768]{2,1,0:T(8,128)(2,1)} %pad_maximum_fusion.10), channel_id=1, source_target_pairs={{0,3},{1,2},{2,1},{3,0},{4,7},{5,6},{6,5},{7,4},{8,11},{9,10},{10,... | collective-permute-start | bytes 1179656 | tf_op jit(solution)/shard_map/ppermute | solution.py:663
  225.7 41.2 %collective-permute-start.69 = (bf16[128,768]{1,0:T(8,128)(2,1)}, bf16[128,768]{1,0:T(8,128)(2,1)}, u32[]{:S(2)}, u32[]{:S(2)}) collective-permute-start(bf16[128,768]{1,0:T(8,128)(2,1)} %get-tuple-element.138.refs_0_), channel_id=1, source_target_pairs={{0,2},{1,3},{2,0},{3,1},{4,6},{5,7},{6,4},{7,5},{8,10},{9,11},{10,... | collective-permute-start | bytes 589832 | tf_op jit(solution)/shard_map/ppermute | solution.py:663
  225.8 23.0 %collective-permute-start.27 = (bf16[4,64,768]{2,1,0:T(8,128)(2,1)}, bf16[4,64,768]{2,1,0:T(8,128)(2,1)}, u32[]{:S(2)}, u32[]{:S(2)}) collective-permute-start(bf16[4,64,768]{2,1,0:T(8,128)(2,1)} %pad_maximum_fusion.10), channel_id=1, source_target_pairs={{0,1},{1,0},{2,3},{3,2},{4,5},{5,4},{6,7},{7,6},{8,9},{9,8},{10,11... | collective-permute-start | bytes 1179656 | tf_op jit(solution)/shard_map/ppermute | solution.py:663
  239.1 23.1 %collective-permute-start.37 = (bf16[3,192,384]{2,1,0:T(8,128)(2,1)S(1)}, bf16[3,192,384]{2,1,0:T(8,128)(2,1)}, u32[]{:S(2)}, u32[]{:S(2)}) collective-permute-start(bf16[3,192,384]{2,1,0:T(8,128)(2,1)S(1)} %constant_dynamic-slice_fusion.1), channel_id=1, source_target_pairs={{0,3},{1,2},{2,1},{3,0},{4,7},{5,6},{6,5},{7,4},{8,11},{9,10},{10,... | collective-permute-start | bytes 1327112 | tf_op jit(solution)/shard_map/ppermute | solution.py:663
  243.4 25.6 %collective-permute-start.36 = (bf16[3,192,384]{2,1,0:T(8,128)(2,1)}, bf16[3,192,384]{2,1,0:T(8,128)(2,1)}, u32[]{:S(2)}, u32[]{:S(2)}) collective-permute-start(bf16[3,192,384]{2,1,0:T(8,128)(2,1)} %collective-permute-done.35), channel_id=1, source_target_pairs={{0,4},{4,0},{1,5},{5,1},{2,6},{6,2},{3,7},{7,3},{8,12},{12,8},{9,1... | collective-permute-start | bytes 1327112 | tf_op jit(solution)/shard_map/ppermute | solution.py:667
  262.3 60.8 %collective-permute-start.38 = (bf16[3,192,384]{2,1,0:T(8,128)(2,1)}, bf16[3,192,384]{2,1,0:T(8,128)(2,1)S(1)}, u32[]{:S(2)}, u32[]{:S(2)}) collective-permute-start(bf16[3,192,384]{2,1,0:T(8,128)(2,1)} %collective-permute-done.37), channel_id=1, source_target_pairs={{0,4},{4,0},{1,5},{5,1},{2,6},{6,2},{3,7},{7,3},{8,12},{12,8},{9,1... | collective-permute-start | bytes 1327112 | tf_op jit(solution)/shard_map/ppermute | solution.py:667
  264.6 62.0 %collective-permute-start.39 = (bf16[8,192,128]{2,1,0:T(8,128)(2,1)}, bf16[8,192,128]{2,1,0:T(8,128)(2,1)}, u32[]{:S(2)}, u32[]{:S(2)}) collective-permute-start(bf16[8,192,128]{2,1,0:T(8,128)(2,1)} %get-tuple-element.127.q0), channel_id=1, source_target_pairs={{0,1},{1,0},{2,3},{3,2},{4,5},{5,4},{6,7},{7,6},{8,9},{9,8},{10,11... | collective-permute-start | bytes 1179656 | tf_op jit(solution)/shard_map/ppermute | solution.py:663
  266.8 278.2 %all-reduce.9.cloned.1.call-start = ((), (), s32[]{:S(2)}) async-start(), calls=%async_computation.2 | async-start | bytes 9830400 | tf_op jit(solution)/shard_map/psum | solution.py:908
  275.0 57.7 %collective-permute-start.40 = (bf16[8,192,128]{2,1,0:T(8,128)(2,1)}, bf16[8,192,128]{2,1,0:T(8,128)(2,1)}, u32[]{:S(2)}, u32[]{:S(2)}) collective-permute-start(bf16[8,192,128]{2,1,0:T(8,128)(2,1)} %get-tuple-element.127.q0), channel_id=1, source_target_pairs={{0,2},{1,3},{2,0},{3,1},{4,6},{5,7},{6,4},{7,5},{8,10},{9,11},{10,... | collective-permute-start | bytes 1179656 | tf_op jit(solution)/shard_map/ppermute | solution.py:663
  283.5 49.3 %collective-permute-start.41 = (bf16[8,192,128]{2,1,0:T(8,128)(2,1)}, bf16[8,192,128]{2,1,0:T(8,128)(2,1)}, u32[]{:S(2)}, u32[]{:S(2)}) collective-permute-start(bf16[8,192,128]{2,1,0:T(8,128)(2,1)} %get-tuple-element.127.q0), channel_id=1, source_target_pairs={{0,3},{1,2},{2,1},{3,0},{4,7},{5,6},{6,5},{7,4},{8,11},{9,10},{10,... | collective-permute-start | bytes 1179656 | tf_op jit(solution)/shard_map/ppermute | solution.py:663
  287.8 45.0 %collective-permute-start.45 = (bf16[4,416,128]{2,1,0:T(8,128)(2,1)}, bf16[4,416,128]{2,1,0:T(8,128)(2,1)}, u32[]{:S(2)}, u32[]{:S(2)}) collective-permute-start(bf16[4,416,128]{2,1,0:T(8,128)(2,1)} %pad_maximum_fusion.9.d0), channel_id=1, source_target_pairs={{0,1},{1,0},{2,3},{3,2},{4,5},{5,4},{6,7},{7,6},{8,9},{9,8},{10,11... | collective-permute-start | bytes 1277960 | tf_op jit(solution)/shard_map/ppermute | solution.py:663
  424.9 40.0 %collective-permute-start.50 = (bf16[2,192,128]{2,1,0:T(8,128)(2,1)S(1)}, bf16[2,192,128]{2,1,0:T(8,128)(2,1)S(1)}, u32[]{:S(2)}, u32[]{:S(2)}) collective-permute-start(bf16[2,192,128]{2,1,0:T(8,128)(2,1)S(1)} %get-tuple-element.343), channel_id=1, source_target_pairs={{0,8},{8,16},{16,24},{24,0},{1,9},{9,17},{17,25},{25,1},{2,10},{10... | collective-permute-start | bytes 294920 | tf_op jit(solution)/shard_map/ppermute | solution.py:672
  426.1 38.8 %collective-permute-start.49 = (bf16[2,192,128]{2,1,0:T(8,128)(2,1)S(1)}, bf16[2,192,128]{2,1,0:T(8,128)(2,1)S(1)}, u32[]{:S(2)}, u32[]{:S(2)}) collective-permute-start(bf16[2,192,128]{2,1,0:T(8,128)(2,1)S(1)} %get-tuple-element.344), channel_id=1, source_target_pairs={{0,16},{8,24},{16,0},{24,8},{1,17},{9,25},{17,1},{25,9},{2,18},{10... | collective-permute-start | bytes 294920 | tf_op jit(solution)/shard_map/ppermute | solution.py:672
  426.4 38.5 %collective-permute-start.48 = (bf16[2,192,128]{2,1,0:T(8,128)(2,1)S(1)}, bf16[2,192,128]{2,1,0:T(8,128)(2,1)S(1)}, u32[]{:S(2)}, u32[]{:S(2)}) collective-permute-start(bf16[2,192,128]{2,1,0:T(8,128)(2,1)S(1)} %get-tuple-element.342), channel_id=1, source_target_pairs={{0,24},{8,0},{16,8},{24,16},{1,25},{9,1},{17,9},{25,17},{2,26},{10... | collective-permute-start | bytes 294920 | tf_op jit(solution)/shard_map/ppermute | solution.py:672
  431.8 51.1 %collective-permute-start.61 = (bf16[608,384]{1,0:T(8,128)(2,1)}, bf16[608,384]{1,0:T(8,128)(2,1)}, u32[]{:S(2)}, u32[]{:S(2)}) collective-permute-start(bf16[608,384]{1,0:T(8,128)(2,1)} %select_convert_fusion), channel_id=1, source_target_pairs={{0,4},{4,0},{1,5},{5,1},{2,6},{6,2},{3,7},{7,3},{8,12},{12,8},{9,1... | collective-permute-start | bytes 1400840 | tf_op jit(solution)/shard_map/ppermute | solution.py:667
  493.7 27.7 %collective-permute-start.57 = (bf16[4,80,768]{2,1,0:T(8,128)(2,1)S(1)}, bf16[4,80,768]{2,1,0:T(8,128)(2,1)}, u32[]{:S(2)}, u32[]{:S(2)}) collective-permute-start(bf16[4,80,768]{2,1,0:T(8,128)(2,1)S(1)} %pad_maximum_fusion.8), channel_id=1, source_target_pairs={{0,1},{1,0},{2,3},{3,2},{4,5},{5,4},{6,7},{7,6},{8,9},{9,8},{10,11... | collective-permute-start | bytes 1474568 | tf_op jit(solution)/shard_map/ppermute | solution.py:663
  510.9 23.2 %collective-permute-start.58 = (bf16[4,80,768]{2,1,0:T(8,128)(2,1)S(1)}, bf16[4,80,768]{2,1,0:T(8,128)(2,1)S(1)}, u32[]{:S(2)}, u32[]{:S(2)}) collective-permute-start(bf16[4,80,768]{2,1,0:T(8,128)(2,1)S(1)} %pad_maximum_fusion.8), channel_id=1, source_target_pairs={{0,2},{1,3},{2,0},{3,1},{4,6},{5,7},{6,4},{7,5},{8,10},{9,11},{10,... | collective-permute-start | bytes 1474568 | tf_op jit(solution)/shard_map/ppermute | solution.py:663
  512.2 21.9 %collective-permute-start.59 = (bf16[4,80,768]{2,1,0:T(8,128)(2,1)S(1)}, bf16[4,80,768]{2,1,0:T(8,128)(2,1)S(1)}, u32[]{:S(2)}, u32[]{:S(2)}) collective-permute-start(bf16[4,80,768]{2,1,0:T(8,128)(2,1)S(1)} %pad_maximum_fusion.8), channel_id=1, source_target_pairs={{0,3},{1,2},{2,1},{3,0},{4,7},{5,6},{6,5},{7,4},{8,11},{9,10},{10,... | collective-permute-start | bytes 1474568 | tf_op jit(solution)/shard_map/ppermute | solution.py:663
  (140 other events, 1939.3 us)
Sparse Core Ops, SparseCore 0:
  200.8 58.9 all-reduce.4
  267.0 56.0 all-reduce.6
  326.9 114.4 all-reduce.8

commit v2 on v1

v2 whole, which is shorter than its diff:
```python
import functools

import jax
import jax.numpy as jnp
from jax import lax
from jax.experimental import pallas as pl
from jax.experimental.pallas import tpu as pltpu
from jax.sharding import PartitionSpec as P

HEAD = 64
PATCH = 392
EPSILON = 1e-05
NEGATIVE = -1e30
LOG2E = 1.4426950408889634
STAT = 16
BF = jnp.bfloat16
F32 = jnp.float32
VMEM_LIMIT = 60 * 2**20
SIDE_X, SIDE_Y, MOD = range(3)


def dot(a, b):
    return jnp.dot(a, b, preferred_element_type=F32)


def dot_tn(a, b):
    return lax.dot_general(a, b, (((0,), (0,)), ((), ())), preferred_element_type=F32)


def dot_nt(a, b):
    return lax.dot_general(a, b, (((1,), (1,)), ((), ())), preferred_element_type=F32)


def normalize(rows):
    mean = jnp.mean(rows, -1, keepdims=True)
    centered = rows - mean
    rstd = lax.rsqrt(jnp.mean(centered * centered, -1, keepdims=True) + EPSILON)
    return centered * rstd, rstd


def normed_rows(rows, gain, bias):
    return (normalize(rows)[0] * gain + bias).astype(BF)


def norm_back(grad_out, rows, gain):
    normed, rstd = normalize(rows)
    scaled = grad_out * gain
    grad_in = rstd * (
        scaled
        - jnp.mean(scaled, -1, keepdims=True)
        - normed * jnp.mean(scaled * normed, -1, keepdims=True)
    )
    return grad_in, jnp.sum(grad_out * normed, 0, keepdims=True), jnp.sum(grad_out, 0, keepdims=True)


def row_sums(a):
    n, width = a.shape
    if n % 8:
        a = jnp.concatenate([a, jnp.zeros((8 - n % 8, width), a.dtype)], 0)
    return jnp.sum(a.reshape(-1, 8, width), 0)


def erf(x):
    x = jnp.clip(x, -4.0, 4.0)
    s = x * x
    top = -2.72614225801306e-10
    for c in (
        2.77068142495902e-08,
        -2.10102402082508e-06,
        -5.69250639462346e-05,
        -7.34990630326855e-04,
        -2.95459980854025e-03,
        -1.60960333262415e-02,
    ):
        top = top * s + c
    low = -1.45660718464996e-05
    for c in (
        -2.13374055278905e-04,
        -1.68282697438203e-03,
        -7.37332916720468e-03,
        -1.42647390514189e-02,
    ):
        low = low * s + c
    return x * top / low


def gelu_share(x):
    return 0.5 * (1.0 + erf(x * 0.7071067811865476))


def gelu_slope(x):
    return gelu_share(x) + x * (0.3989422804014327 * jnp.exp(-0.5 * x * x))


def parts_of(value, count):
    parts = []
    for _ in range(count):
        part = value.astype(BF).astype(F32)
        parts.append(part)
        value = value - part
    return parts


def stat_tile(rows, height):
    place = lax.broadcasted_iota(jnp.int32, (height, rows[0].shape[1]), 0)
    tile = jnp.zeros(place.shape, F32)
    for k, row in enumerate(rows):
        tile = jnp.where(place == k, row, tile)
    return tile.astype(BF)


def diagonal(rows, row_block, column_block, count):
    shape = (row_block * count, column_block * count)
    r = lax.broadcasted_iota(jnp.int32, shape, 0) // row_block
    c = lax.broadcasted_iota(jnp.int32, shape, 1) // column_block
    return jnp.where(r == c, rows, 0.0).astype(BF)


def blocks_down(rows, count):
    return diagonal(jnp.concatenate([rows] * count, 0), rows.shape[0], HEAD, count)


def blocks_across(rows_t, count):
    return diagonal(jnp.concatenate([rows_t] * count, 1), HEAD, rows_t.shape[1], count)


def diagonal_parts(table, lat, count):
    return [
        table[HEAD * h : HEAD * (h + 1), lat * h : lat * (h + 1)] for h in range(count)
    ]


def cost_of(us):
    return pl.CostEstimate(flops=int(us * 1e9), bytes_accessed=0, transcendentals=0)


NO_COST = cost_of(0)


def kernel_call(body, outs, *args, name, scalars=(), scratch=(), deps=(), beside=0.0):
    spec = pl.BlockSpec(memory_space=pltpu.VMEM)
    smem = pl.BlockSpec(memory_space=pltpu.SMEM)
    first, count = len(scalars) + len(args), len(deps)
    return pl.pallas_call(
        lambda *refs: body(*refs[:first], *refs[first + count :]),
        out_shape=[jax.ShapeDtypeStruct(s, t) for s, t in outs],
        in_specs=[smem] * len(scalars)
        + [spec] * len(args)
        + [pl.BlockSpec(memory_space=pl.ANY)] * len(deps),
        out_specs=[spec] * len(outs),
        scratch_shapes=[pltpu.VMEM(s, t) for s, t in scratch],
        compiler_params=pltpu.CompilerParams(vmem_limit_bytes=VMEM_LIMIT),
        cost_estimate=cost_of(beside),
        name=name,
    )(*scalars, *args, *deps)


def tie(x, *deps):
    anywhere = pl.BlockSpec(memory_space=pl.ANY)
    return pl.pallas_call(
        lambda *refs: None,
        out_shape=jax.ShapeDtypeStruct(x.shape, x.dtype),
        in_specs=[anywhere] * (1 + len(deps)),
        out_specs=anywhere,
        input_output_aliases={0: 0},
        cost_estimate=NO_COST,
        name="tie",
    )(x, *deps)


def stack_kernel(*refs):
    for k, ref in enumerate(refs[:-1]):
        refs[-1][k] = ref[...]


def concat_kernel(*refs):
    row = 0
    for ref in refs[:-1]:
        refs[-1][row : row + ref.shape[0]] = ref[...]
        row += ref.shape[0]


def join_halves(target, part, other, mod, at, n):
    target[pl.ds(pl.multiple_of(mod * n, 16), n)] = part[at : at + n]
    target[pl.ds(pl.multiple_of((1 - mod) * n, 16), n)] = other[at : at + n]


def pack_kernel(plan, *refs, counts):
    outs = refs[-len(counts) :]
    at = 0
    for out, count in zip(outs, counts):
        row = 0
        for ref in refs[at : at + count]:
            out[row : row + ref.shape[0]] = ref[...]
            row += ref.shape[0]
        at += count


def pack_halves(at, plan, groups):
    arrays = [a for g in groups for a in g]
    spec = lambda a: pl.BlockSpec((a.shape[0] // 2, a.shape[1]), lambda i, p: (p[at.mod], 0))
    shapes = [(sum(a.shape[0] // 2 for a in g), g[0].shape[1]) for g in groups]
    return pl.pallas_call(
        functools.partial(pack_kernel, counts=[len(g) for g in groups]),
        grid_spec=pltpu.PrefetchScalarGridSpec(
            num_scalar_prefetch=1,
            grid=(1,),
            in_specs=[spec(a) for a in arrays],
            out_specs=[pl.BlockSpec(s, lambda i, m: (0, 0)) for s in shapes],
        ),
        out_shape=[jax.ShapeDtypeStruct(s, BF) for s in shapes],
        compiler_params=pltpu.CompilerParams(vmem_limit_bytes=VMEM_LIMIT),
        cost_estimate=NO_COST,
        name="pack_halves",
    )(plan, *arrays)


def tables_kernel(plan, gathered_ref, pair_ref, pair_t_ref, query_t_ref):
    parts, _, rows, width = gathered_ref.shape
    own = parts * rows // 3
    for k in range(4):
        x, y = lax.rem(plan[SIDE_X] + k % 2, 2), lax.rem(plan[SIDE_Y] + k // 2, 2)
        shard = 2 * y + x
        for i, (target, start) in enumerate(((pair_t_ref, 0), (pair_t_ref, width), (query_t_ref, 0))):
            for p in range(parts):
                low, high = max(own * i, rows * p), min(own * (i + 1), rows * (p + 1))
                if low < high:
                    to = start + own * k + low - own * i
                    target[to : to + high - low] = gathered_ref[
                        p, shard, low - rows * p : high - rows * p
                    ]
    for c in range(0, 2 * width, 256):
        pair_ref[:, c : c + 256] = pair_t_ref[c : c + 256].astype(F32).T.astype(BF)


class Plan:
    def __init__(self, clips, blocks):
        steps = clips * blocks
        self.clips, self.blocks, self.size = clips, blocks, 0
        for name, length in (
            ("side_x", 1), ("side_y", 1), ("mod", 1), ("share", 1), ("some", 2), ("keep", 1), ("tok", 1),
            ("clip_plain", clips), ("count_plain", clips), ("text_plain", clips),
            ("read_clip", steps), ("read_block", steps), ("zero_clip", steps), ("zero_block", steps),
            ("clip", clips), ("count", clips), ("text", clips),
            ("back_clip", steps), ("back_block", steps),
        ):
            setattr(self, name, self.size)
            self.size += length

    def calls(self):
        return ((0, 1), (1, self.clips - 1))


def plan_kernel(place_ref, frames_ref, lengths_ref, drop_ref, plan, order, *, at, rows, span):
    clips, blocks = at.clips, at.blocks
    zones = clips // 2
    tok, side_x, side_y, mod, last = (place_ref[i] for i in range(5))
    zone = lax.rem(tok, zones)
    plan[at.side_x], plan[at.side_y], plan[at.mod], plan[at.share] = side_x, side_y, mod, last
    plan[at.tok] = tok
    drops = [drop_ref[c] for c in range(clips)]
    for c in range(clips):
        rank = sum(
            (drops[o] < drops[c]).astype(jnp.int32)
            if o > c
            else (drops[o] <= drops[c]).astype(jnp.int32)
            for o in range(clips)
            if o != c
        )
        order[rank] = c

    def tables(side, clip_at, count_at, text_at, share):
        flags = []
        for p in range(clips):
            clip = order[2 * lax.rem(zone + p // 2, zones) + lax.rem(p + side, 2)]
            live = 1 - drop_ref[clip]
            count = jnp.clip(frames_ref[clip] * PATCH - tok * span, 0, span) * live
            plan[clip_at + p] = clip
            plan[count_at + p] = count
            plan[text_at + p] = lengths_ref[clip] * live * share
            flags += [((count > b * rows).astype(jnp.int32), clip, b) for b in range(blocks)]
        return flags

    def hold(flags, wanted, clip_at, block_at):
        clip, block = flags[0][1], jnp.int32(0)
        for flag, c, b in flags[::-1]:
            clip = jnp.where(flag == wanted, c, clip)
            block = jnp.where(flag == wanted, b, block)
        for i, (flag, c, b) in enumerate(flags):
            clip = jnp.where(flag == wanted, c, clip)
            block = jnp.where(flag == wanted, b, block)
            plan[clip_at + i] = clip
            plan[block_at + i] = block

    flags = tables(0, at.clip_plain, at.count_plain, at.text_plain, last)
    hold(flags, 1, at.read_clip, at.read_block)
    hold(flags, 0, at.zero_clip, at.zero_block)
    flags = tables(side_y, at.clip, at.count, at.text, 1)
    for i, (first, count) in enumerate(at.calls()):
        part = flags[first * blocks : (first + count) * blocks]
        hold(part, 1, at.back_clip + first * blocks, at.back_block + first * blocks)
        plan[at.some + i] = sum(f for f, _, _ in part)
    plan[at.keep] = 1 - drop_ref[plan[at.clip]]


def make_plan(at, places, frames, lengths, drops, rows, span):
    smem = pl.BlockSpec(memory_space=pltpu.SMEM)
    return pl.pallas_call(
        functools.partial(plan_kernel, at=at, rows=rows, span=span),
        out_shape=jax.ShapeDtypeStruct((at.size,), jnp.int32),
        in_specs=[smem] * 4,
        out_specs=smem,
        scratch_shapes=[pltpu.SMEM((at.clips,), jnp.int32)],
        cost_estimate=NO_COST,
        name="plan",
    )(places, frames, lengths, drops)


def own_rows_kernel(plan, latents, mine, other, latents_ref, mine_ref, other_ref, keep_ref, *, at):
    latents_ref[...] = latents[0]
    mine_ref[...] = mine[0]
    other_ref[...] = other[0]
    keep_ref[...] = jnp.full(keep_ref.shape, plan[at.keep].astype(F32))


def own_rows(at, plan, latents, cotangent):
    lat, width = latents.shape[1:]
    spec = lambda k: pl.BlockSpec((1, lat, width), lambda i, p: (p[at.clip + k], 0, 0))
    whole = lambda *shape: pl.BlockSpec(shape, lambda i, p: (0,) * len(shape))
    return pl.pallas_call(
        functools.partial(own_rows_kernel, at=at),
        grid_spec=pltpu.PrefetchScalarGridSpec(
            num_scalar_prefetch=1,
            grid=(1,),
            in_specs=[spec(0), spec(0), spec(1)],
            out_specs=[whole(lat, width)] * 3 + [whole(1, width)],
        ),
        out_shape=[
            *[jax.ShapeDtypeStruct((lat, width), BF)] * 3,
            jax.ShapeDtypeStruct((1, width), F32),
        ],
        cost_estimate=NO_COST,
        name="own_rows",
    )(plan, latents, cotangent, cotangent)


def tokens_forward_kernel(
    plan, video_ref, text_ref, latents_ref, norms_ref, key_t_ref, value_t_ref, query_t_ref,
    zero_ref, *refs, at,
):
    outs, (key_ref, value_ref, blocks, peak, total, summed) = refs[:-6], refs[-6:]
    place, j = pl.program_id(0), pl.program_id(1)
    rows = video_ref.shape[1]
    lat = latents_ref.shape[1]
    width = key_ref.shape[1]
    heads = width // HEAD
    clip_count = plan[at.count_plain + place]
    text_count = plan[at.text_plain + place]
    count = clip_count - j * rows
    lat_gain, lat_bias, gain, bias = (norms_ref[i : i + 1] for i in range(4))

    @pl.when((place == 0) & (j == 0))
    def _():
        key_ref[...] = key_t_ref[...].astype(F32).T.astype(BF)
        value_ref[...] = value_t_ref[...].astype(F32).T.astype(BF)

    @pl.when(count <= 0)
    def _():
        zero_ref[...] = jnp.zeros_like(zero_ref)

    @pl.when((j == 0) & ((clip_count > 0) | (text_count > 0)))
    def _():
        queries_in = normed_rows(latents_ref[0].astype(F32), lat_gain, lat_bias)
        rows_t = dot_nt(query_t_ref[...], queries_in).astype(BF).astype(F32) * HEAD**-0.5
        blocks[...] = blocks_across(rows_t, heads)

    @pl.when(j == 0)
    def _():
        peak[...] = jnp.full_like(peak, NEGATIVE).astype(BF).astype(F32)
        total[...] = jnp.zeros_like(total)
        summed[...] = jnp.zeros_like(summed)

    def block(x, limit):
        inputs_in = normed_rows(x.astype(F32), gain, bias)
        key = dot(inputs_in, key_ref[...]).astype(BF)
        value = dot(inputs_in, value_ref[...]).astype(BF)
        mask = lax.broadcasted_iota(jnp.int32, (x.shape[0], 1), 0) < limit
        scores = jnp.where(mask, dot(key, blocks[...]) * LOG2E, NEGATIVE)
        before = peak[...]
        top = jnp.maximum(before, jnp.max(scores, 0, keepdims=True)).astype(BF).astype(F32)
        weights = jnp.exp2(scores - top)
        factor = jnp.exp2(before - top)
        peak[...] = top
        total[...] = total[...] * factor + jnp.sum(weights, 0, keepdims=True)
        table = dot_tn(value, weights.astype(BF))
        for h, part in enumerate(diagonal_parts(table, lat, heads)):
            r = slice(HEAD * h, HEAD * (h + 1))
            summed[r] = summed[r] * factor[:, lat * h : lat * (h + 1)] + part

    @pl.when(count > 0)
    def _():
        block(video_ref[0], count)

    @pl.when((j == 0) & (text_count > 0))
    def _():
        block(text_ref[0], text_count)

    for zone, out_ref in enumerate(outs):

        @pl.when((j == pl.num_programs(1) - 1) & (place // 2 == zone))
        def _(out_ref=out_ref):
            out_ref[0, :width] = summed[...].astype(BF)
            of = [slice(lat * h, lat * (h + 1)) for h in range(heads)]
            totals = [parts_of(total[:, c], 2) for c in of]
            stats = [peak[:, c] for c in of] + [t[0] for t in totals] + [t[1] for t in totals]
            out_ref[0, width:] = stat_tile(stats, STAT)


def tokens_forward(at, plan, video, text, latents, params, rows):
    clips, span, width = video.shape
    lat = latents.shape[1]
    own = params[-1].shape[0]
    blocks = span // rows
    full = lambda a: pl.BlockSpec(a.shape, lambda s, j, *_: (0,) * a.ndim)
    clip_spec = lambda a: pl.BlockSpec(
        (1,) + a.shape[1:], lambda s, j, p: (p[at.clip_plain + s], 0, 0)
    )
    block_spec = lambda clip, block: pl.BlockSpec(
        (1, rows, width), lambda s, j, p: (p[clip + s * blocks + j], p[block + s * blocks + j], 0)
    )
    return pl.pallas_call(
        functools.partial(tokens_forward_kernel, at=at),
        grid_spec=pltpu.PrefetchScalarGridSpec(
            num_scalar_prefetch=1,
            grid=(clips, blocks),
            in_specs=[
                block_spec(at.read_clip, at.read_block),
                clip_spec(text),
                clip_spec(latents),
            ]
            + [full(a) for a in params],
            out_specs=[block_spec(at.zero_clip, at.zero_block)]
            + [
                pl.BlockSpec(
                    (1, own + STAT, lat), lambda s, j, p, z=z: (jnp.clip(s - 2 * z, 0, 1), 0, 0)
                )
                for z in range(clips // 2)
            ],
            scratch_shapes=[
                pltpu.VMEM((width, own), BF),
                pltpu.VMEM((width, own), BF),
                pltpu.VMEM((own, own // HEAD * lat), BF),
                pltpu.VMEM((1, own // HEAD * lat), F32),
                pltpu.VMEM((1, own // HEAD * lat), F32),
                pltpu.VMEM((own, lat), F32),
            ],
        ),
        out_shape=[jax.ShapeDtypeStruct(video.shape, BF)]
        + [jax.ShapeDtypeStruct((2, own + STAT, lat), BF)] * (clips // 2),
        compiler_params=pltpu.CompilerParams(
            vmem_limit_bytes=VMEM_LIMIT, dimension_semantics=("arbitrary", "arbitrary")
        ),
        cost_estimate=cost_of(30.0),
        name="tokens_forward",
    )(plan, video, text, latents, *params)


GROUP = 4


def tokens_back_kernel(
    plan, *refs, at, call, carried, extra,
):
    video_ref, text_ref, latents_ref, norms_ref, pair_ref, pair_t_ref, query_t_ref = refs[:7]
    d0, d1, d2, d3 = refs[7:11]
    refs = refs[13:]
    if carried:
        before_ref, refs = refs[0], refs[1:]
    refs = refs[extra:]
    d_video_ref, d_text_ref, weights_ref, d_query_ref = refs[:4]
    final = call == len(at.calls()) - 1
    if final:
        keep_ref, send_ref = refs[4:6]
        refs = refs[2:]
    q_down, q_across, d_down, d_across, lse, delta, d_query, queries = refs[4:]
    step, j = pl.program_id(0), pl.program_id(1)
    place = step + at.calls()[call][0]
    rows, width = video_ref.shape[1:]
    lat = latents_ref.shape[1]
    own = query_t_ref.shape[0] // 4
    own_heads = own // HEAD
    groups = width // (GROUP * HEAD)
    count = plan[at.count + place] - j * rows
    text_count = plan[at.text + place]
    alive = text_count > 0
    lat_gain, lat_bias, gain, bias = (norms_ref[i : i + 1] for i in range(4))

    @pl.when((step == 0) & (j == 0))
    def _():
        weights_ref[...] = before_ref[...] if carried else jnp.zeros_like(weights_ref)
        for ref in (q_down, q_across, d_down, d_across):
            ref[...] = jnp.zeros_like(ref)

    @pl.when(j == 0)
    def _():
        d_query[...] = jnp.zeros_like(d_query)

    @pl.when((j == 0) & alive)
    def _():
        mine = lax.rem(place, 2) == 0
        first = [jnp.where(mine, a[0, :own].astype(F32), b[0, own : 2 * own].astype(F32)) for a, b in ((d0, d2), (d1, d3))]
        second = [jnp.where(mine, a[0, own : 2 * own].astype(F32), b[0, :own].astype(F32)) for a, b in ((d0, d2), (d1, d3))]
        queries_in = normed_rows(latents_ref[0].astype(F32), lat_gain, lat_bias)
        queries[...] = queries_in
        query = dot_nt(queries_in, query_t_ref[...]).astype(BF).astype(F32) * HEAD**-0.5
        d_rows_t = jnp.concatenate(first + second, 0)
        column = lax.broadcasted_iota(jnp.int32, (lat, 2 * HEAD), 1) // HEAD
        for natural, rows_t, down, across in (
            (query, query.T, q_down, q_across),
            (d_rows_t.T, d_rows_t, d_down, d_across),
        ):
            for head in range(groups * GROUP):
                g, h = divmod(head, GROUP)
                across[g, HEAD * h : HEAD * (h + 1), lat * h : lat * (h + 1)] = rows_t[
                    HEAD * head : HEAD * (head + 1)
                ].astype(BF)
                pair = natural[:, 2 * HEAD * (head // 2) : 2 * HEAD * (head // 2 + 1)]
                at = 2 * HEAD * (h // 2)
                down[g, lat * h : lat * (h + 1), at : at + 2 * HEAD] = jnp.where(
                    column == h % 2, pair, 0.0
                ).astype(BF)
        tiles = [d[0, 2 * own : 2 * own + 2 * STAT].astype(F32) for d in (d0, d1, d2, d3)]
        n = 2 * own_heads
        for kind, first_row, count_of in ((delta, 0, 2), (lse, 2 * n, 3)):
            for shard in range(4):
                a, b = tiles[shard % 2], tiles[2 + shard % 2]
                for h in range(own_heads):
                    at_a = first_row + h + own_heads * (shard // 2)
                    at_b = first_row + h + own_heads * (1 - shard // 2)
                    row = sum(
                        jnp.where(mine, a[at_a + n * i : at_a + n * i + 1], b[at_b + n * i : at_b + n * i + 1])
                        for i in range(count_of)
                    )
                    head = shard * own_heads + h
                    kind[:, lat * head : lat * (head + 1)] = row

    def block(x, limit, out_ref, share):
        counted = (lambda a: a) if share is None else (lambda a: a * share)
        normed, rstd = normalize(x.astype(F32))
        inputs_in = (normed * gain + bias).astype(BF)
        key = dot(inputs_in, pair_ref[:, :width]).astype(BF)
        value = dot(inputs_in, pair_ref[:, width:]).astype(BF)
        mask = lax.broadcasted_iota(jnp.int32, (x.shape[0], 1), 0) < limit
        d_keys, d_values = [], []
        for g in range(groups):
            cut = slice(GROUP * HEAD * g, GROUP * HEAD * (g + 1))
            lanes = slice(GROUP * lat * g, GROUP * lat * (g + 1))
            scores = dot(key[:, cut], q_across[g])
            d_probs = dot(value[:, cut], d_across[g])
            probs = jnp.where(mask, jnp.exp2(scores * LOG2E - lse[:, lanes]), 0.0)
            d_scores = (probs * (d_probs - delta[:, lanes])).astype(BF)
            d_values.append(dot(probs.astype(BF), d_down[g]).astype(BF))
            d_keys.append(dot(d_scores, q_down[g]).astype(BF))
            if g == 0:
                table = dot_tn(key[:, cut], d_scores)
                for h, part in enumerate(diagonal_parts(table, lat, own_heads)):
                    d_query[HEAD * h : HEAD * (h + 1)] += counted(part)
        d_key, d_value = jnp.concatenate(d_keys, 1), jnp.concatenate(d_values, 1)
        d_in = dot(d_key, pair_t_ref[:width]) + dot(d_value, pair_t_ref[width:])
        weights_ref[:own] += counted(dot_tn(d_keys[0], inputs_in)[:own])
        weights_ref[own : 2 * own] += counted(dot_tn(d_values[0], inputs_in)[:own])
        weights_ref[3 * own : 3 * own + 8] += counted(row_sums(d_in * normed))
        weights_ref[3 * own + 8 : 3 * own + 16] += counted(row_sums(d_in))
        scaled = d_in * gain
        d_x = rstd * (
            scaled
            - jnp.mean(scaled, -1, keepdims=True)
            - normed * jnp.mean(scaled * normed, -1, keepdims=True)
        )
        out_ref[0] = d_x.astype(BF)

    @pl.when(count > 0)
    def _():
        block(video_ref[0], count, d_video_ref, None)

    @pl.when((plan[at.some + call] == 0) & (step == 0) & (j == 0))
    def _():
        d_video_ref[...] = jnp.zeros_like(d_video_ref)

    @pl.when((j == 0) & alive)
    def _():
        block(text_ref[0], text_count, d_text_ref, plan[at.share].astype(F32))

    @pl.when((j == 0) & jnp.logical_not(alive))
    def _():
        d_text_ref[...] = jnp.zeros_like(d_text_ref)

    @pl.when(j == pl.num_programs(1) - 1)
    def _():
        d_rows = (d_query[...] * HEAD**-0.5).astype(BF)
        d_query_ref[0] = d_rows

        @pl.when(alive)
        def _():
            weights_ref[2 * own : 3 * own] += dot(d_rows, queries[...])

        if final:

            @pl.when(step == pl.num_programs(0) - 1)
            def _():
                half = width // 2
                side = plan[at.mod]
                keep_ref[...] = weights_ref[:, pl.ds(pl.multiple_of(side * half, half), half)]
                send_ref[...] = weights_ref[
                    :, pl.ds(pl.multiple_of((1 - side) * half, half), half)
                ].astype(BF)


WEIGHT_ROWS = 64


def tokens_back(at, plan, call, video, text, latents, params, arrived, filled, before, rows, deps=()):
    first, steps = at.calls()[call]
    span, width = video.shape[1:]
    blocks = span // rows
    lat = latents.shape[1]
    own = params[-1].shape[0] // 4
    groups = width // (GROUP * HEAD)
    full = lambda a: pl.BlockSpec(
        a.shape, lambda s, j, *_: (0,) * a.ndim, pipeline_mode=pl.Buffered(1)
    )
    clip_spec = lambda a: pl.BlockSpec(
        (1,) + a.shape[1:], lambda s, j, p: (p[at.clip + first + s], 0, 0)
    )
    index = lambda p, table, s, j: p[table + (first + s) * blocks + j]
    video_spec = pl.BlockSpec(
        (1, rows, width),
        lambda s, j, p: (index(p, at.back_clip, s, j), index(p, at.back_block, s, j), 0),
    )
    weight_shape = (3 * own + WEIGHT_ROWS, width)
    half_shape = (weight_shape[0], width // 2)
    final = call == len(at.calls()) - 1
    operands = [video, text, latents, *params, *arrived]
    in_specs = [video_spec, clip_spec(text), clip_spec(latents)]
    in_specs += [full(a) for a in params]
    in_specs += [
        pl.BlockSpec(
            (1, 2 * own + 2 * STAT, lat), lambda s, j, *_: ((s + first) // 2 - first // 2, 0, 0)
        )
        for a in arrived
    ]
    start = 1 + len(operands)
    operands += filled
    in_specs += [pl.BlockSpec(memory_space=pl.ANY)] * 2
    if before is not None:
        operands += [before]
        in_specs += [full(before)]
    operands += deps
    in_specs += [pl.BlockSpec(memory_space=pl.ANY)] * len(deps)
    return pl.pallas_call(
        functools.partial(
            tokens_back_kernel, at=at, call=call, carried=before is not None, extra=len(deps)
        ),
        grid_spec=pltpu.PrefetchScalarGridSpec(
            num_scalar_prefetch=1,
            grid=(steps, blocks),
            in_specs=in_specs,
            out_specs=[
                video_spec,
                clip_spec(text),
                pl.BlockSpec(weight_shape, lambda s, j, *_: (0, 0)),
                pl.BlockSpec((1, own, lat), lambda s, j, *_: (s, 0, 0)),
            ]
            + [pl.BlockSpec(half_shape, lambda s, j, *_: (0, 0))] * (2 * final),
            scratch_shapes=[
                pltpu.VMEM((groups, GROUP * lat, GROUP * HEAD), BF),
                pltpu.VMEM((groups, GROUP * HEAD, GROUP * lat), BF),
                pltpu.VMEM((groups, GROUP * lat, GROUP * HEAD), BF),
                pltpu.VMEM((groups, GROUP * HEAD, GROUP * lat), BF),
                pltpu.VMEM((1, groups * GROUP * lat), F32),
                pltpu.VMEM((1, groups * GROUP * lat), F32),
                pltpu.VMEM((own, lat), F32),
                pltpu.VMEM((lat, width), BF),
            ],
        ),
        out_shape=[
            jax.ShapeDtypeStruct(video.shape, BF),
            jax.ShapeDtypeStruct(text.shape, BF),
            jax.ShapeDtypeStruct(weight_shape, F32),
            jax.ShapeDtypeStruct((steps, own, lat), BF),
        ]
        + [jax.ShapeDtypeStruct(half_shape, F32), jax.ShapeDtypeStruct(half_shape, BF)] * final,
        input_output_aliases={start: 0, start + 1: 1},
        compiler_params=pltpu.CompilerParams(
            vmem_limit_bytes=VMEM_LIMIT, dimension_semantics=("arbitrary", "arbitrary")
        ),
        cost_estimate=cost_of((25.0, 10.0)[call]),
        name="tokens_back",
    )(plan, *operands)


def combine_kernel(plan, output_ref, *refs):
    parts, (mine_ref, other_ref, low_ref, *branch_refs) = refs[:-5], refs[-5:]
    own = parts[0].shape[1] - STAT
    lat = parts[0].shape[2]
    heads = own // HEAD
    results = []
    for y in range(2):
        tiles = [p[y, own:].astype(F32) for p in parts]
        attended, logs = [], []
        for h in range(heads):
            peaks = [t[h : h + 1] for t in tiles]
            top = peaks[0]
            for p in peaks[1:]:
                top = jnp.maximum(top, p)
            total = jnp.zeros((1, lat), F32)
            summed = jnp.zeros((HEAD, lat), F32)
            for p, t, peak in zip(parts, tiles, peaks):
                factor = jnp.exp2(peak - top)
                a = t[heads + h : heads + h + 1] + t[2 * heads + h : 2 * heads + h + 1]
                total = total + a * factor
                summed = summed + p[y, HEAD * h : HEAD * (h + 1)].astype(F32) * factor
            some = total > 0.0
            safe = jnp.where(some, total, 1.0)
            attended.append(jnp.where(some, summed / safe, 0.0))
            logs.append(parts_of(jnp.where(some, top + jnp.log2(safe), 0.0), 3))
        stats = [logs[h][i] for i in range(3) for h in range(heads)]
        results.append((jnp.concatenate(attended, 0), stat_tile(stats, STAT).astype(F32)))
    first = plan[SIDE_Y] == 0
    for k, (ref, (a, b)) in enumerate(((mine_ref, results), (other_ref, results[::-1]))):
        low = jnp.where(first, a[0], b[0]).astype(BF)
        ref[:own] = low
        ref[own:] = jnp.where(first, a[1], b[1]).astype(BF)
        low_ref[k] = low
        branch_refs[k][...] = dot_tn(low, output_ref[...]).astype(BF)


def spread(norms_ref, row):
    return norms_ref[row : row + 1], norms_ref[row + 1 : row + 2]


def sum_of(terms):
    total = terms[0]
    for term in terms[1:]:
        total = total + term
    return total


def received_sum(part0, part1):
    return part0[...].astype(F32) + part1[...].astype(F32)


def cross_forward_kernel(
    plan, b0, b1, b2, b3, latents_ref, keep_ref, norms_ref, up0, down0, near, far,
    first_ref, inner_ref, pre_ref, hidden_ref, part_ref, up1, down1,
):
    join_mlp(near, far, plan[MOD], up1, down1)
    branch = received_sum(b0, b1) + received_sum(b2, b3)
    first = latents_ref[...].astype(F32) + keep_ref[...] * branch
    first_ref[...] = first
    inner = normed_rows(first, *spread(norms_ref, 4))
    inner_ref[...] = inner
    terms = []
    for k, (up, down) in enumerate(((up0, down0), (up1, down1))):
        pre = dot(inner, up[...])
        pre_ref[k] = pre
        hidden = (pre * gelu_share(pre)).astype(BF)
        hidden_ref[k] = hidden
        terms.append(dot(hidden, down[...]))
    part_ref[...] = sum_of(terms).astype(BF)


def join_mlp(near, far, mod, up, down):
    half = up.shape[0] // 2
    join_halves(up, near, far, mod, 0, half)
    join_halves(down, near, far, mod, half, half)


def join_self(near, far, mod, targets):
    half, start = targets.shape[1] // 2, targets.shape[2]
    for i in range(4):
        join_halves(targets.at[i], near, far, mod, start + half * i, half)


def self_forward_kernel(
    plan, first_ref, part0, part1, norms_ref, wq, wk, wv, wo, near, far,
    second_ref, inner_ref, rows_ref, query_t_ref, attended_ref, lse_ref, part_ref, joined,
):
    join_self(near, far, plan[MOD], joined)
    second = first_ref[...] + received_sum(part0, part1)
    second_ref[...] = second
    inner = normed_rows(second, *spread(norms_ref, 6))
    inner_ref[...] = inner
    lat = inner.shape[0]
    own = wq.shape[0]
    heads = own // HEAD
    terms = []
    for k, (q, w, v, o) in enumerate(((wq, wk, wv, wo), [joined.at[i] for i in range(4)])):
        query = (dot_nt(inner, q[...]).astype(BF).astype(F32) * HEAD**-0.5).astype(BF)
        key = dot_nt(inner, w[...]).astype(BF)
        value = dot_nt(inner, v[...]).astype(BF)
        for i, a in enumerate((query, key, value)):
            rows_ref[k, i] = a
        query_t = dot_nt(q[...], inner).astype(BF).astype(F32) * HEAD**-0.5
        query_t_ref[k] = query_t.astype(BF)
        scores = dot(key, blocks_across(query_t, heads)) * LOG2E
        top = jnp.max(scores, 0, keepdims=True)
        weights = jnp.exp2(scores - top)
        total = jnp.sum(weights, 0, keepdims=True)
        table = dot_tn(value, weights.astype(BF))
        attended = jnp.concatenate(
            [
                part / total[:, lat * h : lat * (h + 1)]
                for h, part in enumerate(diagonal_parts(table, lat, heads))
            ],
            0,
        )
        attended_ref[k] = attended
        lse_ref[k] = top + jnp.log2(total)
        terms.append(dot_tn(attended.astype(BF), o[...]))
    part_ref[...] = sum_of(terms).astype(BF)


def hidden_back(grad_low, pre, up, down):
    d_hidden = dot_nt(grad_low, down[...])
    d_pre = (d_hidden * gelu_slope(pre)).astype(BF)
    return d_pre, dot_nt(d_pre, up[...])


def last_back_kernel(
    plan, second_ref, part0, part1, cotangent_ref, norms_ref, up0, down0, near, far,
    third_ref, inner_ref, hidden_ref, d_pre_ref, part_ref, moving_ref, up1, down1,
):
    join_mlp(near, far, plan[MOD], up1, down1)
    third = second_ref[...] + received_sum(part0, part1)
    third_ref[...] = third
    inner = normed_rows(third, *spread(norms_ref, 8))
    inner_ref[...] = inner
    terms = []
    for k, (up, down) in enumerate(((up0, down0), (up1, down1))):
        pre = dot(inner, up[...])
        hidden_ref[k] = (pre * gelu_share(pre)).astype(BF)
        d_pre_ref[k], term = hidden_back(cotangent_ref[...], pre, up, down)
        terms.append(term)
    part_ref[...] = sum_of(terms).astype(BF)
    lat = inner.shape[0]
    for i, a in enumerate((inner, d_pre_ref[1], hidden_ref[1])):
        moving_ref[lat * i : lat * (i + 1)] = a


def down_kernel(plan, hidden_ref, down0, near, far, part_ref, down1):
    half = down1.shape[0] // 2
    join_halves(down1, near, far, plan[MOD], half, half)
    part_ref[...] = (dot(hidden_ref[0], down0[...]) + dot(hidden_ref[1], down1[...])).astype(BF)


def self_back_kernel(
    plan, cotangent_ref, third_ref, part0, part1, norms_ref,
    rows_ref, query_t_ref, attended_ref, lse_ref, wq, wk, wv, wo, near, far, self_in_ref,
    grad_ref, sums_ref, branch_ref, d_rows_ref, low_ref, part_ref, moving_ref, joined,
):
    join_self(near, far, plan[MOD], joined)
    d_inner = received_sum(part0, part1)
    d_x, d_gain, d_bias = norm_back(d_inner, third_ref[...], spread(norms_ref, 8)[0])
    grad = cotangent_ref[...].astype(F32) + d_x
    grad_ref[...] = grad
    sums_ref[0:1] = d_gain
    sums_ref[1:2] = d_bias
    branch = grad.astype(BF)
    branch_ref[...] = branch
    lat = grad.shape[0]
    own = wq.shape[0]
    heads = own // HEAD
    terms = []
    for k, weights in enumerate(((wq, wk, wv, wo), [joined.at[i] for i in range(4)])):
        o = weights[3]
        query, key, value = rows_ref[k, 0], rows_ref[k, 1], rows_ref[k, 2]
        d_att = dot_nt(branch, o[...]).astype(BF).astype(F32)
        d_att_t = dot_nt(o[...], branch).astype(BF).astype(F32)
        attended = attended_ref[k]
        low_ref[k] = attended.astype(BF)
        product = d_att_t * attended
        delta = jnp.concatenate(
            [
                jnp.sum(product[HEAD * h : HEAD * (h + 1)], 0, keepdims=True)
                for h in range(heads)
            ],
            1,
        )
        scores = dot(key, blocks_across(query_t_ref[k].astype(F32), heads))
        d_probs = dot(value, blocks_across(d_att_t, heads))
        probs = jnp.exp2(scores * LOG2E - lse_ref[k])
        d_scores = (probs * (d_probs - delta)).astype(BF)
        d_value = dot(probs.astype(BF), blocks_down(d_att, heads)).astype(BF)
        d_key = dot(d_scores, blocks_down(query.astype(F32), heads)).astype(BF)
        table = dot_tn(d_scores, key)
        column = lax.broadcasted_iota(jnp.int32, (lat, own), 1) // HEAD
        d_query = sum_of(
            [jnp.where(column == h, table[lat * h : lat * (h + 1)], 0.0) for h in range(heads)]
        )
        d_query = (d_query * HEAD**-0.5).astype(BF)
        for i, a in enumerate((d_query, d_key, d_value)):
            d_rows_ref[k, i] = a
            terms.append(dot(a, weights[i][...]))
            if k == 1:
                moving_ref[2 * lat :, own * i : own * (i + 1)] = a
    part_ref[...] = sum_of(terms).astype(BF)
    moving_ref[:lat] = self_in_ref[...]
    moving_ref[lat : 2 * lat] = branch
    moving_ref[2 * lat :, 3 * own :] = attended_ref[1].T.astype(BF)


def cross_back_kernel(
    plan, grad_ref, second_ref, part0, part1, norms_ref, pre_ref, up0, down0, near, far,
    inner_ref, hidden_ref,
    out_ref, sums_ref, low_ref, d_pre_ref, part_ref, moving_ref, up1, down1,
):
    join_mlp(near, far, plan[MOD], up1, down1)
    d_inner = received_sum(part0, part1)
    d_x, d_gain, d_bias = norm_back(d_inner, second_ref[...], spread(norms_ref, 6)[0])
    grad = grad_ref[...] + d_x
    out_ref[...] = grad
    sums_ref[0:1] = d_gain
    sums_ref[1:2] = d_bias
    grad_low = grad.astype(BF)
    low_ref[...] = grad_low
    terms = []
    for k, (up, down) in enumerate(((up0, down0), (up1, down1))):
        d_pre_ref[k], term = hidden_back(grad_low, pre_ref[k], up, down)
        terms.append(term)
    part_ref[...] = sum_of(terms).astype(BF)
    lat = grad.shape[0]
    for i, a in enumerate((inner_ref[...], d_pre_ref[1], hidden_ref[1], grad_low)):
        moving_ref[lat * i : lat * (i + 1)] = a


def attended_back_kernel(
    plan, grad_ref, first_ref, part0, part1, norms_ref, keep_ref, a0, a2, o0, near, far,
    branch_ref, packed_ref, first_grad_ref, sums_ref, o2,
):
    own, width = o0.shape
    join_halves(o2, near, far, plan[MOD], width + 2 * own, own // 2)
    d_inner = received_sum(part0, part1)
    d_x, d_gain, d_bias = norm_back(d_inner, first_ref[...], spread(norms_ref, 4)[0])
    grad = grad_ref[...] + d_x
    branch = (keep_ref[...] * grad).astype(BF)
    branch_ref[...] = branch
    own = o0.shape[0]
    heads = own // HEAD
    deltas, logs = [], []
    for k, (a, o) in enumerate(((a0, o0), (a2, o2))):
        d_att_t = dot_nt(o[...], branch).astype(BF)
        packed_ref[own * k : own * (k + 1)] = d_att_t
        product = d_att_t.astype(F32) * a[:own].astype(F32)
        tile = a[own:].astype(F32)
        for h in range(heads):
            deltas.append(
                parts_of(jnp.sum(product[HEAD * h : HEAD * (h + 1)], 0, keepdims=True), 2)
            )
            logs.append([tile[heads * i + h : heads * i + h + 1] for i in range(3)])
    rows = [d[i] for i in range(2) for d in deltas] + [g[i] for i in range(3) for g in logs]
    packed_ref[2 * own : 2 * own + 2 * STAT] = stat_tile(rows, 2 * STAT)
    first_grad_ref[...] = grad
    sums_ref[0:1] = d_gain
    sums_ref[1:2] = d_bias


def half_rows_kernel(plan, third_ref, out0, out1, out_ref, hold):
    half = out_ref.shape[0]
    hold[...] = third_ref[...] + received_sum(out0, out1)
    cut = pl.ds(pl.multiple_of(plan[SIDE_X] * half, half), half)
    out_ref[...] = hold[cut].astype(BF)


def latent_back_kernel(
    plan, grad_ref, latents_ref, norms_ref, d0, d1, d2, d3, query_t_ref,
    cross_sums, self_sums, ffn_sums, out_ref, hold,
):
    own, lat = d0.shape
    half = lat // 2
    d_in = sum_of(
        [dot_tn(d[...], query_t_ref[own * k : own * (k + 1)]) for k, d in enumerate((d0, d1, d2, d3))]
    )
    d_x, d_gain, d_bias = norm_back(
        d_in, latents_ref[...].astype(F32), spread(norms_ref, 0)[0]
    )
    hold[...] = grad_ref[...] + d_x
    cut = pl.ds(pl.multiple_of(plan[SIDE_X] * half, half), half)
    out_ref[:half] = hold[cut].astype(BF)
    sums = [d_gain, d_bias]
    sums += [ref[i : i + 1] for ref in (cross_sums, self_sums, ffn_sums) for i in range(2)]
    out_ref[half:] = stat_tile(sums, STAT)


def tail_pack_kernel(plan, keep_ref, arrived_ref, query_ref, own_ref, *outs, at):
    zones = len(outs) + 1
    own, lat = query_ref.shape[1:]
    step = own_ref.shape[0]
    for k in range(zones):
        cut = pl.ds(pl.multiple_of(lax.rem(plan[at.tok] + k, zones) * step, 16), step)
        total = keep_ref[cut] + arrived_ref[cut].astype(F32)
        if k == 0:
            own_ref[...] = total
            continue
        out = outs[k - 1]
        out[:own] = query_ref[2 * k - 1]
        out[own : 2 * own] = query_ref[2 * k]
        for c in range(total.shape[1] // lat):
            out[2 * own + step * c : 2 * own + step * (c + 1)] = total[
                :, lat * c : lat * (c + 1)
            ].astype(BF)


def tail_sum_kernel(first_ref, query_ref, own_ref, *refs):
    parts, (mine_ref, other_ref, share_ref) = refs[:-3], refs[-3:]
    own, lat = mine_ref.shape
    step = own_ref.shape[0]
    for i, (ref, near) in enumerate(((mine_ref, first_ref), (other_ref, query_ref))):
        cut = slice(own * i, own * (i + 1))
        ref[...] = (near[0].astype(F32) + sum_of([p[cut].astype(F32) for p in parts])).astype(BF)
    for c in range(own_ref.shape[1] // lat):
        lanes = slice(lat * c, lat * (c + 1))
        cut = slice(2 * own + step * c, 2 * own + step * (c + 1))
        total = own_ref[:, lanes] + sum_of([p[cut].astype(F32) for p in parts])
        share_ref[:, lanes] = total.astype(BF)


def token_weights_kernel(plan, mine_ref, other_ref, key_ref, value_ref, query_ref, sums_ref, whole, *, at):
    zones, step, half = mine_ref.shape
    own = key_ref.shape[0]
    side = plan[at.mod]
    for k in range(zones):
        cut = pl.ds(pl.multiple_of(lax.rem(plan[at.tok] + k, zones) * step, 16), step)
        for ref, x in ((mine_ref, side), (other_ref, 1 - side)):
            whole[cut, pl.ds(pl.multiple_of(x * half, half), half)] = ref[k].astype(F32)
    for i, ref in enumerate((key_ref, value_ref, query_ref)):
        ref[...] = whole[own * i : own * (i + 1)]
    for i in range(2):
        rows = whole[3 * own + 8 * i : 3 * own + 8 * (i + 1)]
        sums_ref[i : i + 1] = jnp.sum(rows, 0, keepdims=True)


def out_rows_kernel(plan, halves_ref, out_ref, *, at):
    clips, half = out_ref.shape[0], halves_ref.shape[1]
    for place in range(clips):
        zone = lax.rem(plan[at.tok] + place // 2, clips // 2)
        first = 4 * zone + 2 * lax.rem(plan[SIDE_Y] + place % 2, 2)
        for x in range(2):
            out_ref[plan[at.clip + place], half * x : half * (x + 1)] = halves_ref[first + x]


def in_clip_order_kernel(plan, r0, r1, r2, r3, out_ref, *sums_ref, at):
    half = out_ref.shape[1] // 2
    side = plan[at.side_x]
    for place in range(out_ref.shape[0]):
        same, crossed = (r0, r1) if place % 2 == 0 else (r2, r3)
        clip, zone = plan[at.clip + place], place // 2
        out_ref[clip, pl.ds(pl.multiple_of(side * half, half), half)] = same[zone, :half]
        out_ref[clip, pl.ds(pl.multiple_of((1 - side) * half, half), half)] = crossed[zone, :half]
    for ref in sums_ref:
        ref[...] = sum_of(
            [r[zone, half:].astype(F32)[:8] for zone in range(r0.shape[0]) for r in (r0, r2)]
        )


def in_clip_order(at, plan, lat, results, deps=()):
    height, width = results[0].shape[1:]
    outs = [((at.clips, lat, width), BF)] + [((8, width), F32)] * (height > lat // 2)
    return kernel_call(
        functools.partial(in_clip_order_kernel, at=at), outs, *results,
        name="in_clip_order", scalars=(plan,), deps=deps,
    )


def mlp_grads_kernel(inner, d_pre, hidden, low, low_y, moved, out_ref):
    lat, width = inner.shape
    near = [moved[lat * i : lat * (i + 1)] for i in range(3)]
    last = low_y.shape[0] - lat
    out_ref[:width] = (dot_tn(inner[...], d_pre[0]) + dot_tn(near[0], near[1])).astype(BF)
    out_ref[width:] = (dot_tn(hidden[0], low[:lat]) + dot_tn(near[2], low_y[last:])).astype(BF)


def self_grads_kernel(inner, branch, d_rows, low_t, moved, outs):
    lat = inner.shape[0]
    own = low_t.shape[1]
    heads_in = [moved[2 * lat :, own * i : own * (i + 1)] for i in range(4)]
    for i in range(3):
        part = dot_tn(d_rows[0, i], inner[...]) + dot_tn(heads_in[i], moved[:lat])
        outs[own * i : own * (i + 1)] = part.astype(BF)
    part = dot(low_t[0], branch[...]) + dot_tn(heads_in[3], moved[lat : 2 * lat])
    outs[3 * own :] = part.astype(BF)


def output_grad_kernel(low, branch, branch_y, out_ref):
    part = dot(low[0], branch[...]) + dot(low[1], branch_y[...])
    out_ref[...] = part.astype(BF)


def head_move(x, k):
    n = lax.axis_size("head")
    return lax.ppermute(x, "head", [(i, i ^ k) for i in range(n)])


def mod_move(x):
    return lax.ppermute(x, "mod", [(0, 1), (1, 0)])


def tok_move(x, shift):
    n = lax.axis_size("tok")
    return lax.ppermute(x, "tok", [(i, (i + shift) % n) for i in range(n)])


def after(x, *earlier):
    return lax.optimization_barrier((x, *earlier))[0]


def on_device(
    latents,
    video_tokens,
    text_tokens,
    frame_counts,
    text_lengths,
    drop_mask,
    cotangent,
    norm_latent_gain,
    norm_latent_bias,
    norm_input_gain,
    norm_input_bias,
    cross_query,
    cross_key,
    cross_value,
    cross_output,
    norm_cross_gain,
    norm_cross_bias,
    cross_up,
    cross_down,
    norm_self_gain,
    norm_self_bias,
    self_query,
    self_key,
    self_value,
    self_output,
    norm_ffn_gain,
    norm_ffn_bias,
    self_up,
    self_down,
):
    clips, lat, width = latents.shape
    span = video_tokens.shape[1]
    own = cross_key.shape[1]
    heads = own // HEAD
    shards = lax.axis_size("tok")
    zones = clips // 2
    tok, mod, head = lax.axis_index("tok"), lax.axis_index("mod"), lax.axis_index("head")
    side_x, side_y = lax.rem(head, 2), head // 2
    rows = 784 if span % 784 == 0 else span
    norms = jnp.stack(
        [norm_latent_gain, norm_latent_bias, norm_input_gain, norm_input_bias,
         norm_cross_gain, norm_cross_bias, norm_self_gain, norm_self_bias,
         norm_ffn_gain, norm_ffn_bias]
    )
    cross_kvq = [cross_key.T, cross_value.T, cross_query.T]
    self_weights = [self_query.T, self_key.T, self_value.T, self_output]

    at = Plan(clips, span // rows)
    last = (tok == shards - 1).astype(jnp.int32)
    places = jnp.stack([tok, side_x, side_y, mod, last]).astype(jnp.int32)
    plan = make_plan(at, places, frame_counts, text_lengths, drop_mask, rows, span)

    (pack,) = pack_halves(at, plan, [[cross_up, cross_down] + self_weights + [cross_output]])
    near = head_move(pack, 2)
    tables = jnp.concatenate(cross_kvq, 0)
    if shards == zones:
        part = tables.shape[0] // shards
        tables = lax.dynamic_slice_in_dim(tables, tok * part, part, 0)
        tables = lax.all_gather(tables, ("tok", "head")).reshape(shards, 4, part, width)
    else:
        tables = lax.all_gather(tables, "head")[None]

    d_video, *partial = tokens_forward(
        at, plan, video_tokens, text_tokens, latents, (norms, *cross_kvq), rows
    )
    received = [tok_move(partial[k % zones], k) for k in range(1, shards)]
    (pack3,) = pack_halves(at, tie(plan, partial[0]), [[self_up, self_down]])
    my_latents, my_cotangent, other_cotangent, keep = own_rows(
        at, tie(plan, partial[0]), latents, cotangent
    )
    lw = (lat, width)
    square = ((width, width), BF)
    mine, other, low, branch, branch_other = kernel_call(
        combine_kernel, [(partial[0].shape[1:], BF)] * 2 + [((2, own, lat), BF)] + [(lw, BF)] * 2,
        cross_output, partial[0], *received, name="combine", scalars=(plan,),
    )
    near = tie(near, mine)
    far = mod_move(near)
    branch_parts = [branch, head_move(branch, 1), head_move(branch_other, 2), head_move(branch_other, 3)]

    near3 = head_move(tie(pack3, *branch_parts[1:]), 2)

    first, inner1, pre1, hidden1, part = kernel_call(
        cross_forward_kernel,
        [(lw, F32), (lw, BF), ((2,) + lw, F32), ((2,) + lw, BF), (lw, BF)],
        *branch_parts, my_latents, keep, norms, cross_up, cross_down, near, far,
        name="cross_forward", scalars=(plan,), scratch=[square] * 2,
    )
    mine_y = head_move(tie(other, first), 2)
    second, self_in, self_rows, self_query_t, self_attended, self_lse, part = kernel_call(
        self_forward_kernel,
        [(lw, F32), (lw, BF), ((2, 3, lat, own), BF), ((2, own, lat), BF), ((2, own, lat), F32),
         ((2, 1, heads * lat), F32), (lw, BF)],
        first, part, head_move(part, 1), norms, *self_weights, near, far,
        name="self_forward", scalars=(plan,), scratch=[((4, own, width), BF)],
    )
    near3 = tie(near3, second)
    far3 = mod_move(near3)
    third, inner2, hidden2, d_pre2, part, moving = kernel_call(
        last_back_kernel,
        [(lw, F32), (lw, BF), ((2,) + lw, BF), ((2,) + lw, BF), (lw, BF), ((3 * lat, width), BF)],
        second, part, head_move(part, 1), my_cotangent, norms, self_up, self_down, near3, far3,
        name="last_back", scalars=(plan,), scratch=[square] * 2,
    )
    received = head_move(part, 1)
    halves = head_move(moving, 2)
    (out_part,) = kernel_call(
        down_kernel, [(lw, BF)], hidden2, self_down, near3, far3,
        name="down", beside=3.4, scalars=(plan,), scratch=[square], deps=(part,),
    )
    grad_third, ffn_sums, self_branch, self_d_rows, self_low, part, moving = kernel_call(
        self_back_kernel,
        [(lw, F32), ((2, width), F32), (lw, BF), ((2, 3, lat, own), BF), ((2, own, lat), BF), (lw, BF),
         ((3 * lat, width), BF)],
        my_cotangent, third, part, received, norms,
        self_rows, self_query_t, self_attended, self_lse, *self_weights, near, far, self_in,
        name="self_back", scalars=(plan,), deps=(out_part,), scratch=[((4, own, width), BF)],
    )
    out_moved = head_move(tie(out_part, grad_third), 1)
    moved_self = head_move(moving, 2)
    (out_half,) = kernel_call(
        half_rows_kernel, [((lat // 2, width), BF)], third, out_part, out_moved,
        name="half_rows", beside=1.5, scalars=(plan,), scratch=[(lw, F32)],
    )
    out_halves = lax.all_gather(out_half, ("tok", "head"))
    grad_second, self_sums, low1, d_pre1, part, moving = kernel_call(
        cross_back_kernel,
        [(lw, F32), ((2, width), F32), (lw, BF), ((2,) + lw, BF), (lw, BF), ((4 * lat, width), BF)],
        grad_third, second, part, head_move(part, 1), norms, pre1,
        cross_up, cross_down, near, far, inner1, hidden1,
        name="cross_back", scalars=(plan,), deps=(out_half,), scratch=[square] * 2,
    )

    pair, pair_t, query_t = kernel_call(
        tables_kernel,
        [((width, 2 * width), BF), ((2 * width, width), BF), ((width, width), BF)],
        tables, name="tables", beside=4.7, scalars=(plan,),
    )
    moved = head_move(moving, 2)
    cross_branch, packed, grad_first, cross_sums = kernel_call(
        attended_back_kernel,
        [(lw, BF), ((2 * own + 2 * STAT, lat), BF), (lw, F32), ((2, width), F32)],
        grad_second, first, part, head_move(part, 1), norms, keep,
        mine, mine_y, cross_output, near, far,
        name="attended_back", scalars=(plan,), scratch=[((own, width), BF)], deps=(pair,),
    )

    (stages,) = kernel_call(
        stack_kernel, [((zones,) + packed.shape, BF)],
        packed, *[tok_move(packed, shards - k) for k in range(1, zones)], name="stack",
    )
    arrived = [stages] + [head_move(stages, k) for k in (1, 2, 3)]
    (mlp2,) = kernel_call(
        mlp_grads_kernel, [((2 * width, width), BF)], inner2, d_pre2, hidden2, my_cotangent, other_cotangent, halves,
        name="last_weights", beside=4.0, deps=(packed,),
    )
    branch_y = head_move(cross_branch, 2)
    (self_grads,) = kernel_call(
        self_grads_kernel, [((4 * own, width), BF)],
        self_in, self_branch, self_d_rows, self_low, moved_self, name="self_weights", beside=3.3,
        deps=(stages,),
    )
    (mlp1,) = kernel_call(
        mlp_grads_kernel, [((2 * width, width), BF)], inner1, d_pre1, hidden1,
        low1, moved, moved, name="cross_weights", beside=4.4,
        deps=(stages,),
    )
    (output_grad,) = kernel_call(
        output_grad_kernel, [((own, width), BF)], low, cross_branch, branch_y,
        name="output_weights", beside=2.1,
    )
    counted = lambda grads: [jnp.where(tok < zones, a, 0) if shards > zones else a for a in grads]
    params = (norms, pair, pair_t, query_t)
    tokens = (video_tokens, text_tokens, latents)
    d_text = jnp.zeros_like(text_tokens)
    d_video, d_text, token_weights, first_query = tokens_back(
        at, plan, 0, *tokens, params, arrived, [d_video, d_text], None, rows,
        deps=(mlp2, self_grads, mlp1, output_grad),
    )
    d_video, d_text, token_weights, d_query, keep_half, send_half = tokens_back(
        at, plan, 1, *tokens, params, arrived, [d_video, d_text], token_weights, rows,
        deps=(out_halves,),
    )
    sums = lax.psum(counted([mlp2, self_grads, mlp1, output_grad]), ("tok", "mod"))
    mlp2, self_grads, mlp1, output_grad = (a.astype(F32) for a in sums)
    up1, down1 = mlp1[:width], mlp1[width:]
    up2, down2 = mlp2[:width], mlp2[width:]

    (latents_out,) = kernel_call(
        functools.partial(out_rows_kernel, at=at), [(latents.shape, BF)], out_halves[: 4 * zones],
        name="out_rows", scalars=(plan,),
    )

    whole_rows = token_weights.shape[0]
    step = whole_rows // zones
    if shards == zones:
        token_own, *pieces = kernel_call(
            functools.partial(tail_pack_kernel, at=at),
            [((step, width // 2), F32)] + [((2 * own + step * width // 2 // lat, lat), BF)] * (zones - 1),
            keep_half, mod_move(send_half), d_query,
            name="tail_pack", scalars=(plan,), deps=(latents_out,),
        )
        received = [tok_move(p, k + 1) for k, p in enumerate(pieces)]
        my_query, other_query, share = kernel_call(
            tail_sum_kernel, [((own, lat), BF)] * 2 + [((step, width // 2), BF)],
            first_query, d_query, token_own, *received, name="tail_sum",
        )
        shares = [share] + [tok_move(share, shards - k) for k in range(1, zones)]
        (shares,) = kernel_call(
            stack_kernel, [((zones,) + share.shape, BF)], *shares, name="stack"
        )
        d_key_t, d_value_t, d_query_t, input_sums = kernel_call(
            functools.partial(token_weights_kernel, at=at),
            [((own, width), F32)] * 3 + [((2, width), F32)],
            shares, mod_move(shares), name="token_weights", scalars=(plan,),
            scratch=[((whole_rows, width), F32)],
        )
    else:
        pieces = jnp.concatenate([first_query, d_query], 0).reshape(zones, 2, own, lat)
        received = [tok_move(pieces[k % zones], k) for k in range(1, shards)]
        d_query = sum_of([a.astype(F32) for a in [pieces[0]] + received]).astype(BF)
        my_query, other_query = d_query[0], d_query[1]
        total = lax.psum(token_weights, ("tok", "mod"))
        d_key_t, d_value_t, d_query_t = (total[own * i : own * (i + 1)] for i in range(3))
        input_sums = jnp.sum(total[3 * own : 3 * own + 16].reshape(2, 8, width), 1)
    d_queries = [my_query] + [head_move(a, k) for k, a in ((1, my_query), (2, other_query), (3, other_query))]
    (my_grad,) = kernel_call(
        latent_back_kernel, [((lat // 2 + STAT, width), BF)],
        grad_first, my_latents, norms, *d_queries, query_t, cross_sums, self_sums, ffn_sums,
        name="latent_back", scalars=(plan,), scratch=[(lw, F32)],
    )
    zones_grad = jnp.stack([my_grad] + [tok_move(my_grad, shards - k) for k in range(1, zones)])
    zones_grad = [zones_grad] + [head_move(zones_grad, k) for k in (1, 2, 3)]
    grad_latents, norm_sums = in_clip_order(at, plan, lat, zones_grad)
    norm_sums = norm_sums + mod_move(norm_sums)
    return (
        latents_out,
        grad_latents,
        d_video,
        d_text,
        norm_sums[0],
        norm_sums[1],
        input_sums[0],
        input_sums[1],
        d_query_t.T,
        d_key_t.T,
        d_value_t.T,
        output_grad,
        norm_sums[2],
        norm_sums[3],
        up1,
        down1,
        norm_sums[4],
        norm_sums[5],
        self_grads[:own].T,
        self_grads[own : 2 * own].T,
        self_grads[2 * own : 3 * own].T,
        self_grads[3 * own :],
        norm_sums[6],
        norm_sums[7],
        up2,
        down2,
    )


def solution(mesh):
    in_specs = (
        P("mod", None, None),
        P("mod", "tok", None),
        P("mod", None, None),
        P("mod"),
        P("mod"),
        P("mod"),
        P("mod", None, None),
        P(),
        P(),
        P(),
        P(),
        P(None, "head"),
        P(None, "head"),
        P(None, "head"),
        P("head", None),
        P(),
        P(),
        P(None, "head"),
        P("head", None),
        P(),
        P(),
        P(None, "head"),
        P(None, "head"),
        P(None, "head"),
        P("head", None),
        P(),
        P(),
        P(None, "head"),
        P("head", None),
    )
    out_specs = (
        P("mod", None, None),
        P("mod", None, None),
        P("mod", "tok", None),
        P("mod", None, None),
        P(),
        P(),
        P(),
        P(),
        P(None, "head"),
        P(None, "head"),
        P(None, "head"),
        P("head", None),
        P(),
        P(),
        P(None, "head"),
        P("head", None),
        P(),
        P(),
        P(None, "head"),
        P(None, "head"),
        P(None, "head"),
        P("head", None),
        P(),
        P(),
        P(None, "head"),
        P("head", None),
    )
    return jax.shard_map(
        on_device, mesh=mesh, in_specs=in_specs, out_specs=out_specs, check_vma=False
    )
```

time: 558 us -> 477 us (0.85); the launches traced: 562 us -> 469 us
  Pallas kernels: 157 us -> 246 us
  starting transfers between devices: 127 us -> 58.1 us
  other arithmetic: 56.5 us -> 5.13 us
  local copies, waits for them, and re-layouts: 73.3 us -> 31.2 us
  waiting for transfers between devices: 129 us -> 114 us
    pallas_call x14 -> x35, Pallas kernels: 157 us -> 246 us  [the longest x2 121 us: tokens_back(): pl.pallas_call(functools.partial(tokens_back_kernel, at=at, call=call, ca...]
    ppermute x12 -> x5, starting transfers between devices: 34.1 us -> 0.08 us  [mod_move(): return lax.ppermute(x, 'mod', [(0, 1), (1, 0)])]
    psum x3 -> x1, waiting for transfers between devices: 30.5 us -> 0.01 us  [on_device(): lax.psum(counted([mlp2, self_grads, mlp1, output_grad]), ('tok', 'mod'))]
    ppermute x48 -> x25, starting transfers between devices: 58.1 us -> 33.9 us  [head_move(): return lax.ppermute(x, 'head', [(i, i ^ k) for i in range(n)])]
    ppermute x21 -> x15, waiting for transfers between devices: 25.4 us -> 47.1 us  [tok_move(): return lax.ppermute(x, 'tok', [(i, (i + shift) % n) for i in range(n)])]
    select_n x12 -> x0, other arithmetic: 16.3 us -> none  [the longest x9 11.5 us: shared_head_move(): low = jnp.where(mod == 0, part, other)]
    squeeze x11 -> x0, local copies, waits for them, and re-layouts: 12.3 us -> none  [the longest x2 2.32 us: on_device(): d_rows_y, low_y = (move_y(self_d_rows[1]), move_y(self_low[1]))]
    convert_element_type x9 -> x2, other arithmetic: 14.6 us -> 2.4 us  [on_device(): mlp2, self_grads, mlp1, output_grad = (a.astype(F32) for a in sums)]
  transfers between devices with their start and end apart: 84 -> 48, of which waited for: 24 -> 25; matrix products, arithmetic and copies ran while one was open for 20% -> 2% of each run, Pallas kernels for 28% -> 51%
where the time goes in v2:
time: 477 us; the launch traced here: 469 us
  Pallas kernels  246 us (52%)
  waiting for transfers between devices  114 us (24%)
  starting transfers between devices  58.1 us (12%)
  local copies, waits for them, and re-layouts  31.2 us (7%)
  between operations  14.5 us (3%)
  other arithmetic  5.13 us (1%)
    pallas_call x2, Pallas kernels, tokens_back(): pl.pallas_call(functools.partial(tokens_back_kernel, at=at, call=call, ca...  121 us
    pallas_call x22, Pallas kernels, kernel_call(): pl.pallas_call(lambda *refs: body(*refs[:first], *refs[first + count:]),...  81.3 us
    ppermute x25, waiting for transfers between devices, head_move(): return lax.ppermute(x, 'head', [(i, i ^ k) for i in range(n)])  65.8 us
    ppermute x15, waiting for transfers between devices, tok_move(): return lax.ppermute(x, 'tok', [(i, (i + shift) % n) for i in range(n)])  47.1 us
    ppermute x25, starting transfers between devices, head_move(): return lax.ppermute(x, 'head', [(i, i ^ k) for i in range(n)])  33.9 us
    pallas_call x1, Pallas kernels, tokens_forward(): pl.pallas_call(functools.partial(tokens_forward_kernel, at=at), grid_spec...  33.2 us
    ppermute x15, starting transfers between devices, tok_move(): return lax.ppermute(x, 'tok', [(i, (i + shift) % n) for i in range(n)])  24 us
    unnamed x132, local copies, waits for them, and re-layouts  20.4 us
  transfers between devices with their start and end apart: 48, of which 25 were waited for; matrix products, arithmetic and copies ran while one was open for 2% of the time, Pallas kernels for 51%

profile of v2, /device:TPU:0, one launch (start us, length us, event | category | flops | bytes accessed | tf_op | source)
XLA Modules:
  0.0 469.1 jit_solution(11811688086197460558)
XLA Ops:
  9.6 3.6 pack_halves.2
  18.8 33.2 %tokens_forward.1 = (bf16[8,1568,768]{2,1,0:T(8,128)(2,1)}, bf16[2,208,128]{2,1,0:T(8,128)(2,1)}, bf16[2,208,128]{2,1,0:T(8,128)(2,1)}, bf16[2,208,128]{2,1,0:T(8,128)(2,1)}, bf16[2,208,128]{2,1,0:T(8,128)(2,1)}) custom-call(s32[152]{0:T(256)} %plan.1.refs_0_, bf16[8,1568,768]{2,1,0:T(8,128)(2,1)} %refs_0_.7, bf16[8,40,768]{2,1,0:T(8,128)(2,1)} %refs_1_.9, ...), custom_call_target="tpu_custom_call" | custom-call | flops 30000001024 | tf_op jit(solution)/shard_map/tokens_forward/pallas_call | solution.py:431
  61.4 5.0 %collective-permute-done.1.refs_4_ = bf16[2,208,128]{2,1,0:T(8,128)(2,1)S(1)} collective-permute-done((bf16[2,208,128]{2,1,0:T(8,128)(2,1)}, bf16[2,208,128]{2,1,0:T(8,128)(2,1)S(1)}, u32[]{:S(2)}, u32[]{:S(2)}) %collective-permute-start.1) | collective-permute-done | bytes 106528 | tf_op jit(solution)/shard_map/ppermute | solution.py:1110
  77.8 4.5 collective-permute-done.3.refs_2_.refs_1_
  85.6 5.1 %collective-permute-done.5.refs_4_.refs_3_ = bf16[128,768]{1,0:T(8,128)(2,1)S(1)} collective-permute-done((bf16[128,768]{1,0:T(8,128)(2,1)S(1)}, bf16[128,768]{1,0:T(8,128)(2,1)S(1)}, u32[]{:S(2)}, u32[]{:S(2)}) %collective-permute-start.5) | collective-permute-done | bytes 196640 | tf_op jit(solution)/shard_map/ppermute | solution.py:1101
  96.6 5.8 %cross_forward.1 = (f32[128,768]{1,0:T(8,128)}, bf16[128,768]{1,0:T(8,128)(2,1)}, f32[2,128,768]{2,1,0:T(8,128)}, bf16[2,128,768]{2,1,0:T(8,128)(2,1)}, bf16[128,768]{1,0:T(8,128)(2,1)}) custom-call(s32[152]{0:T(256)} %plan.1.refs_0_, bf16[128,768]{1,0:T(8,128)(2,1)} %get-tuple-element.104.refs_1_, bf16[128,768]{1,0:T(8,128)(2,1)} %copy-done.8, ...), custom_call_target="tpu_custom_call" | custom-call | tf_op jit(solution)/shard_map/cross_forward/pallas_call | solution.py:144
  104.3 4.7 collective-permute-done.8.refs_3_
  109.6 5.5 %self_forward.1 = (f32[128,768]{1,0:T(8,128)}, bf16[128,768]{1,0:T(8,128)(2,1)}, bf16[2,3,128,192]{3,2,1,0:T(8,128)(2,1)}, bf16[2,192,128]{2,1,0:T(8,128)(2,1)},...) custom-call(s32[152]{0:T(256)} %plan.1.refs_0_, ...), custom_call_target="tpu_custom_call" | custom-call | tf_op jit(solution)/shard_map/self_forward/pallas_call | solution.py:144
  115.1 4.4 collective-permute-done.10.refs_0_
  121.9 5.8 %collective-permute-done.9.refs_3_ = bf16[128,768]{1,0:T(8,128)(2,1)S(1)} collective-permute-done((bf16[128,768]{1,0:T(8,128)(2,1)S(1)}, bf16[128,768]{1,0:T(8,128)(2,1)S(1)}, u32[]{:S(2)}, u32[]{:S(2)}) %collective-permute-start.9) | collective-permute-done | bytes 196640 | tf_op jit(solution)/shard_map/ppermute | solution.py:1101
  128.9 5.9 %last_back.1 = (f32[128,768]{1,0:T(8,128)}, bf16[128,768]{1,0:T(8,128)(2,1)}, bf16[2,128,768]{2,1,0:T(8,128)(2,1)}, bf16[2,128,768]{2,1,0:T(8,128)(2,1)}, bf16[1...) custom-call(s32[152]{0:T(256)} %plan.1.refs_0_, f32[128,768]{1,0:T(8,128)} %get-tuple-element.111.refs_1_.refs_2_, ...), custom_call_target="tpu_custom_call" | custom-call | tf_op jit(solution)/shard_map/last_back/pallas_call | solution.py:144
  136.3 3.3 down.1.refs_17_.refs_2_
  142.2 6.4 %self_back.1 = (f32[128,768]{1,0:T(8,128)}, f32[2,768]{1,0:T(2,128)}, bf16[128,768]{1,0:T(8,128)(2,1)}, bf16[2,3,128,192]{3,2,1,0:T(8,128)(2,1)}, bf16[2,192,128...) custom-call(s32[152]{0:T(256)} %plan.1.refs_0_, ...), custom_call_target="tpu_custom_call" | custom-call | tf_op jit(solution)/shard_map/self_back/pallas_call | solution.py:144
  160.1 7.0 %cross_back.1 = (f32[128,768]{1,0:T(8,128)}, f32[2,768]{1,0:T(2,128)}, bf16[128,768]{1,0:T(8,128)(2,1)}, bf16[2,128,768]{2,1,0:T(8,128)(2,1)}, bf16[128,768]{1,0:T(8,128)(2,1)}, /*index=5*/bf16[512,768]{1,0:T(8,128)(2,1)}) custom-call(s32[152]{0:T(256)} %plan.1.refs_0_, f32[128,768]{1,0:T(8,128)} %get-tuple-element.122.refs_1_, ...), custom_call_target="tpu_custom_call" | custom-call | tf_op jit(solution)/shard_map/cross_back/pallas_call | solution.py:144
  169.8 5.6 %tables.1 = (bf16[768,1536]{1,0:T(8,128)(2,1)}, bf16[1536,768]{1,0:T(8,128)(2,1)}, bf16[768,768]{1,0:T(8,128)(2,1)}) custom-call(s32[152]{0:T(256)} %plan.1.refs_0_, bf16[4,4,144,768]{3,2,1,0:T(8,128)(2,1)} %bitcast.47), custom_call_target="tpu_custom_call" | custom-call | flops 4700000256 | tf_op jit(solution)/shard_map/tables/pallas_call | solution.py:144
  176.1 4.2 attended_back.1
  184.5 4.4 last_weights.1.refs_13_
  197.4 4.1 collective-permute-done.25.refs_4_.refs_5_
  204.7 4.6 cross_weights.1.refs_15_
  216.1 9.2 %collective-permute-done.21.refs_9_ = bf16[4,416,128]{2,1,0:T(8,128)(2,1)S(1)} collective-permute-done((bf16[4,416,128]{2,1,0:T(8,128)(2,1)}, bf16[4,416,128]{2,1,0:T(8,128)(2,1)S(1)}, u32[]{:S(2)}, u32[]{:S(2)}) %collective-permute-start.21) | collective-permute-done | bytes 426016 | tf_op jit(solution)/shard_map/ppermute | solution.py:1101
  226.4 26.6 %tokens_back.2 = (bf16[8,1568,768]{2,1,0:T(8,128)(2,1)}, bf16[8,40,768]{2,1,0:T(8,128)(2,1)}, f32[640,768]{1,0:T(8,128)}, bf16[1,192,128]{2,1,0:T(8,128)(2,1)}) custom-call(s32[152]{0:T(256)} %plan.1.refs_0_, bf16[8,1568,768]{2,1,0:T(8,128)(2,1)} %refs_0_.7, bf16[8,40,768]{2,1,0:T(8,128)(2,1)} %refs_1_.9, ...), custom_call_target="tpu_custom_call", output_to_operand_aliasing={{0}: (12, {}), {1}: (13, {})} | custom-call | flops 24999999488 | tf_op jit(solution)/shard_map/tokens_back/pallas_call | solution.py:660
  253.8 94.4 %tokens_back.3 = (bf16[8,1568,768]{2,1,0:T(8,128)(2,1)}, bf16[8,40,768]{2,1,0:T(8,128)(2,1)}, f32[640,768]{1,0:T(8,128)}, bf16[7,192,128]{2,1,0:T(8,128)(2,1)}, ...) custom-call(s32[152]{0:T(256)} %plan.1.refs_0_, ...), custom_call_target="tpu_custom_call", output_to_operand_aliasing={{0}: (12, {}), {1}: (13, {})} | custom-call | flops 10000000000 | tf_op jit(solution)/shard_map/tokens_back/pallas_call | solution.py:660
  354.2 3.7 collective-permute-start.28
  360.5 8.8 %collective-permute-done.28.refs_3_ = bf16[864,128]{1,0:T(8,128)(2,1)S(1)} collective-permute-done((bf16[864,128]{1,0:T(8,128)(2,1)}, bf16[864,128]{1,0:T(8,128)(2,1)S(1)}, u32[]{:S(2)}, u32[]{:S(2)}) %collective-permute-start.28) | collective-permute-done | bytes 221216 | tf_op jit(solution)/shard_map/ppermute | solution.py:1110
  369.2 10.7 %collective-permute-done.29.refs_4_ = bf16[864,128]{1,0:T(8,128)(2,1)S(1)} collective-permute-done((bf16[864,128]{1,0:T(8,128)(2,1)}, bf16[864,128]{1,0:T(8,128)(2,1)S(1)}, u32[]{:S(2)}, u32[]{:S(2)}) %collective-permute-start.29) | collective-permute-done | bytes 221216 | tf_op jit(solution)/shard_map/ppermute | solution.py:1110
  379.9 7.6 %collective-permute-done.30.refs_5_ = bf16[864,128]{1,0:T(8,128)(2,1)S(1)} collective-permute-done((bf16[864,128]{1,0:T(8,128)(2,1)}, bf16[864,128]{1,0:T(8,128)(2,1)S(1)}, u32[]{:S(2)}, u32[]{:S(2)}) %collective-permute-start.30) | collective-permute-done | bytes 221216 | tf_op jit(solution)/shard_map/ppermute | solution.py:1110
  390.3 4.2 collective-permute-start.41
  407.0 3.3 collective-permute-start.34
  417.2 5.6 %collective-permute-done.35 = bf16[80,768]{1,0:T(8,128)(2,1)S(1)} collective-permute-done((bf16[80,768]{1,0:T(8,128)(2,1)}, bf16[80,768]{1,0:T(8,128)(2,1)S(1)}, u32[]{:S(2)}, u32[]{:S(2)}) %collective-permute-start.35) | collective-permute-done | bytes 122912 | tf_op jit(solution)/shard_map/ppermute | solution.py:1110
  430.8 7.2 %collective-permute-done.37.refs_2_ = bf16[4,80,768]{2,1,0:T(8,128)(2,1)S(1)} collective-permute-done((bf16[4,80,768]{2,1,0:T(8,128)(2,1)S(1)}, bf16[4,80,768]{2,1,0:T(8,128)(2,1)S(1)}, u32[]{:S(2)}, u32[]{:S(2)}) %collective-permute-start.37) | collective-permute-done | bytes 491552 | tf_op jit(solution)/shard_map/ppermute | solution.py:1101
  438.0 8.3 %collective-permute-done.38.refs_3_ = bf16[4,80,768]{2,1,0:T(8,128)(2,1)S(1)} collective-permute-done((bf16[4,80,768]{2,1,0:T(8,128)(2,1)S(1)}, bf16[4,80,768]{2,1,0:T(8,128)(2,1)S(1)}, u32[]{:S(2)}, u32[]{:S(2)}) %collective-permute-start.38) | collective-permute-done | bytes 491552 | tf_op jit(solution)/shard_map/ppermute | solution.py:1101
  458.5 3.8 fusion.2
  (257 shorter events, 137.8 us)
Async XLA Ops:
  7.2 162.6 %all-gather.7.cloned.1.call-start = ((), (), s32[]{:S(2)}) async-start(), calls=%async_computation.1 | async-start | bytes 3760128 | tf_op jit(solution)/shard_map/all_gather | solution.py:1176
  13.3 56.2 %collective-permute-start.6 = (bf16[1248,768]{1,0:T(8,128)(2,1)}, bf16[1248,768]{1,0:T(8,128)(2,1)S(1)}, u32[]{:S(2)}, u32[]{:S(2)}) collective-permute-start(bf16[1248,768]{1,0:T(8,128)(2,1)} %pack_halves.2), channel_id=1, source_target_pairs={{0,2},{1,3},{2,0},{3,1},{4,6},{5,7},{6,4},{7,5},{8,10},{9,11},{10,... | collective-permute-start | bytes 5750792 | tf_op jit(solution)/shard_map/ppermute | solution.py:1101
  17.3 236.5 %all-gather.5.cloned.1.call-start = ((), (), s32[]{:S(2)}) async-start(), calls=%async_computation | async-start | bytes 1671168 | tf_op jit(solution)/shard_map/all_gather | solution.py:1242
  54.9 11.6 %collective-permute-start.1 = (bf16[2,208,128]{2,1,0:T(8,128)(2,1)}, bf16[2,208,128]{2,1,0:T(8,128)(2,1)S(1)}, u32[]{:S(2)}, u32[]{:S(2)}) collective-permute-start(bf16[2,208,128]{2,1,0:T(8,128)(2,1)} %get-tuple-element.102), channel_id=1, source_target_pairs={{0,16},{8,24},{16,0},{24,8},{1,17},{9,25},{17,1},{25,9},{2,18},{10... | collective-permute-start | bytes 319496 | tf_op jit(solution)/shard_map/ppermute | solution.py:1110
  55.2 11.3 %collective-permute-start.2 = (bf16[2,208,128]{2,1,0:T(8,128)(2,1)}, bf16[2,208,128]{2,1,0:T(8,128)(2,1)S(1)}, u32[]{:S(2)}, u32[]{:S(2)}) collective-permute-start(bf16[2,208,128]{2,1,0:T(8,128)(2,1)} %get-tuple-element.103), channel_id=1, source_target_pairs={{0,24},{8,0},{16,8},{24,16},{1,25},{9,1},{17,9},{25,17},{2,26},{10... | collective-permute-start | bytes 319496 | tf_op jit(solution)/shard_map/ppermute | solution.py:1110
  70.7 24.6 %collective-permute-start.7 = (bf16[1248,768]{1,0:T(8,128)(2,1)}, bf16[1248,768]{1,0:T(8,128)(2,1)S(1)}, u32[]{:S(2)}, u32[]{:S(2)}) collective-permute-start(bf16[1248,768]{1,0:T(8,128)(2,1)} %tie.7.refs_10_.refs_9_.refs_14_), channel_id=1, source_target_pairs={{0,4},{4,0},{1,5},{5,1},{2,6},{6,2},{3,7},{7,3},{8,12},{12,8},{9,1... | collective-permute-start | bytes 5750792 | tf_op jit(solution)/shard_map/ppermute | solution.py:1105
  70.7 11.6 %collective-permute-start.3 = (bf16[128,768]{1,0:T(8,128)(2,1)S(1)}, bf16[128,768]{1,0:T(8,128)(2,1)S(1)}, u32[]{:S(2)}, u32[]{:S(2)}) collective-permute-start(bf16[128,768]{1,0:T(8,128)(2,1)S(1)} %copy-done.31), channel_id=1, source_target_pairs={{0,1},{1,0},{2,3},{3,2},{4,5},{5,4},{6,7},{7,6},{8,9},{9,8},{10,11... | collective-permute-start | bytes 589832 | tf_op jit(solution)/shard_map/ppermute | solution.py:1101
  72.2 13.4 %collective-permute-start.4 = (bf16[128,768]{1,0:T(8,128)(2,1)S(1)}, bf16[128,768]{1,0:T(8,128)(2,1)S(1)}, u32[]{:S(2)}, u32[]{:S(2)}) collective-permute-start(bf16[128,768]{1,0:T(8,128)(2,1)S(1)} %copy-done.63), channel_id=1, source_target_pairs={{0,2},{1,3},{2,0},{3,1},{4,6},{5,7},{6,4},{7,5},{8,10},{9,11},{10,... | collective-permute-start | bytes 589832 | tf_op jit(solution)/shard_map/ppermute | solution.py:1101
  72.9 17.8 %collective-permute-start.5 = (bf16[128,768]{1,0:T(8,128)(2,1)S(1)}, bf16[128,768]{1,0:T(8,128)(2,1)S(1)}, u32[]{:S(2)}, u32[]{:S(2)}) collective-permute-start(bf16[128,768]{1,0:T(8,128)(2,1)S(1)} %copy-done.63), channel_id=1, source_target_pairs={{0,3},{1,2},{2,1},{3,0},{4,7},{5,6},{6,5},{7,4},{8,11},{9,10},{10,... | collective-permute-start | bytes 589832 | tf_op jit(solution)/shard_map/ppermute | solution.py:1101
  91.4 28.0 %collective-permute-start.10 = (bf16[768,768]{1,0:T(8,128)(2,1)}, bf16[768,768]{1,0:T(8,128)(2,1)S(1)}, u32[]{:S(2)}, u32[]{:S(2)}) collective-permute-start(bf16[768,768]{1,0:T(8,128)(2,1)} %tie.8), channel_id=1, source_target_pairs={{0,2},{1,3},{2,0},{3,1},{4,6},{5,7},{6,4},{7,5},{8,10},{9,11},{10,... | collective-permute-start | bytes 3538952 | tf_op jit(solution)/shard_map/ppermute | solution.py:1101
  150.7 33.0 %collective-permute-start.23 = (bf16[384,768]{1,0:T(8,128)(2,1)S(1)}, bf16[384,768]{1,0:T(8,128)(2,1)S(1)}, u32[]{:S(2)}, u32[]{:S(2)}) collective-permute-start(bf16[384,768]{1,0:T(8,128)(2,1)S(1)} %copy-done.59), channel_id=1, source_target_pairs={{0,2},{1,3},{2,0},{3,1},{4,6},{5,7},{6,4},{7,5},{8,10},{9,11},{10,... | collective-permute-start | bytes 1769480 | tf_op jit(solution)/shard_map/ppermute | solution.py:1101
  151.9 23.5 %collective-permute-start.16 = (bf16[208,128]{1,0:T(8,128)(2,1)}, bf16[208,128]{1,0:T(8,128)(2,1)S(1)}, u32[]{:S(2)}, u32[]{:S(2)}) collective-permute-start(bf16[208,128]{1,0:T(8,128)(2,1)} %tie.11), channel_id=1, source_target_pairs={{0,2},{1,3},{2,0},{3,1},{4,6},{5,7},{6,4},{7,5},{8,10},{9,11},{10,... | collective-permute-start | bytes 159752 | tf_op jit(solution)/shard_map/ppermute | solution.py:1101
  152.8 56.5 %collective-permute-start.24 = (bf16[384,768]{1,0:T(8,128)(2,1)}, bf16[384,768]{1,0:T(8,128)(2,1)S(1)}, u32[]{:S(2)}, u32[]{:S(2)}) collective-permute-start(bf16[384,768]{1,0:T(8,128)(2,1)} %get-tuple-element.143), channel_id=1, source_target_pairs={{0,2},{1,3},{2,0},{3,1},{4,6},{5,7},{6,4},{7,5},{8,10},{9,11},{10,... | collective-permute-start | bytes 1769480 | tf_op jit(solution)/shard_map/ppermute | solution.py:1101
  168.4 33.1 %collective-permute-start.25 = (bf16[512,768]{1,0:T(8,128)(2,1)}, bf16[512,768]{1,0:T(8,128)(2,1)S(1)}, u32[]{:S(2)}, u32[]{:S(2)}) collective-permute-start(bf16[512,768]{1,0:T(8,128)(2,1)} %get-tuple-element.146), channel_id=1, source_target_pairs={{0,2},{1,3},{2,0},{3,1},{4,6},{5,7},{6,4},{7,5},{8,10},{9,11},{10,... | collective-permute-start | bytes 2359304 | tf_op jit(solution)/shard_map/ppermute | solution.py:1101
  188.9 24.4 %collective-permute-start.26 = (bf16[128,768]{1,0:T(8,128)(2,1)S(1)}, bf16[128,768]{1,0:T(8,128)(2,1)S(1)}, u32[]{:S(2)}, u32[]{:S(2)}) collective-permute-start(bf16[128,768]{1,0:T(8,128)(2,1)S(1)} %copy-done.61), channel_id=1, source_target_pairs={{0,2},{1,3},{2,0},{3,1},{4,6},{5,7},{6,4},{7,5},{8,10},{9,11},{10,... | collective-permute-start | bytes 589832 | tf_op jit(solution)/shard_map/ppermute | solution.py:1101
  195.3 20.8 %collective-permute-start.20 = (bf16[4,416,128]{2,1,0:T(8,128)(2,1)}, bf16[4,416,128]{2,1,0:T(8,128)(2,1)S(1)}, u32[]{:S(2)}, u32[]{:S(2)}) collective-permute-start(bf16[4,416,128]{2,1,0:T(8,128)(2,1)} %stack.95.refs_5_.refs_6_.refs_7_), channel_id=1, source_target_pairs={{0,1},{1,0},{2,3},{3,2},{4,5},{5,4},{6,7},{7,6},{8,9},{9,8},{10,11... | collective-permute-start | bytes 1277960 | tf_op jit(solution)/shard_map/ppermute | solution.py:1101
  196.6 28.8 %collective-permute-start.21 = (bf16[4,416,128]{2,1,0:T(8,128)(2,1)}, bf16[4,416,128]{2,1,0:T(8,128)(2,1)S(1)}, u32[]{:S(2)}, u32[]{:S(2)}) collective-permute-start(bf16[4,416,128]{2,1,0:T(8,128)(2,1)} %stack.95.refs_5_.refs_6_.refs_7_), channel_id=1, source_target_pairs={{0,2},{1,3},{2,0},{3,1},{4,6},{5,7},{6,4},{7,5},{8,10},{9,11},{10,... | collective-permute-start | bytes 1277960 | tf_op jit(solution)/shard_map/ppermute | solution.py:1101
  201.5 23.9 %collective-permute-start.22 = (bf16[4,416,128]{2,1,0:T(8,128)(2,1)}, bf16[4,416,128]{2,1,0:T(8,128)(2,1)S(1)}, u32[]{:S(2)}, u32[]{:S(2)}) collective-permute-start(bf16[4,416,128]{2,1,0:T(8,128)(2,1)} %stack.95.refs_5_.refs_6_.refs_7_), channel_id=1, source_target_pairs={{0,3},{1,2},{2,1},{3,0},{4,7},{5,6},{6,5},{7,4},{8,11},{9,10},{10,... | collective-permute-start | bytes 1277960 | tf_op jit(solution)/shard_map/ppermute | solution.py:1101
  253.1 200.7 %all-reduce.3.cloned.1.call-start = ((), (), s32[]{:S(2)}) async-start(), calls=%async_computation.2 | async-start | bytes 12386304 | tf_op jit(solution)/shard_map/psum | solution.py:1301
  354.2 15.0 %collective-permute-start.28 = (bf16[864,128]{1,0:T(8,128)(2,1)}, bf16[864,128]{1,0:T(8,128)(2,1)S(1)}, u32[]{:S(2)}, u32[]{:S(2)}) collective-permute-start(bf16[864,128]{1,0:T(8,128)(2,1)} %get-tuple-element.157), channel_id=1, source_target_pairs={{0,8},{8,16},{16,24},{24,0},{1,9},{9,17},{17,25},{25,1},{2,10},{10... | collective-permute-start | bytes 663560 | tf_op jit(solution)/shard_map/ppermute | solution.py:1110
  357.9 22.0 %collective-permute-start.29 = (bf16[864,128]{1,0:T(8,128)(2,1)}, bf16[864,128]{1,0:T(8,128)(2,1)S(1)}, u32[]{:S(2)}, u32[]{:S(2)}) collective-permute-start(bf16[864,128]{1,0:T(8,128)(2,1)} %get-tuple-element.158), channel_id=1, source_target_pairs={{0,16},{8,24},{16,0},{24,8},{1,17},{9,25},{17,1},{25,9},{2,18},{10... | collective-permute-start | bytes 663560 | tf_op jit(solution)/shard_map/ppermute | solution.py:1110
  357.9 29.6 %collective-permute-start.30 = (bf16[864,128]{1,0:T(8,128)(2,1)}, bf16[864,128]{1,0:T(8,128)(2,1)S(1)}, u32[]{:S(2)}, u32[]{:S(2)}) collective-permute-start(bf16[864,128]{1,0:T(8,128)(2,1)} %get-tuple-element.159), channel_id=1, source_target_pairs={{0,24},{8,0},{16,8},{24,16},{1,25},{9,1},{17,9},{25,17},{2,26},{10... | collective-permute-start | bytes 663560 | tf_op jit(solution)/shard_map/ppermute | solution.py:1110
  390.3 16.7 %collective-permute-start.41 = (bf16[160,384]{1,0:T(8,128)(2,1)}, bf16[160,384]{1,0:T(8,128)(2,1)S(1)}, u32[]{:S(2)}, u32[]{:S(2)}) collective-permute-start(bf16[160,384]{1,0:T(8,128)(2,1)} %get-tuple-element.169.refs_0_), channel_id=1, source_target_pairs={{0,24},{8,0},{16,8},{24,16},{1,25},{9,1},{17,9},{25,17},{2,26},{10... | collective-permute-start | bytes 368648 | tf_op jit(solution)/shard_map/ppermute | solution.py:1110
  398.1 15.1 %collective-permute-start.42 = (bf16[160,384]{1,0:T(8,128)(2,1)}, bf16[160,384]{1,0:T(8,128)(2,1)S(1)}, u32[]{:S(2)}, u32[]{:S(2)}) collective-permute-start(bf16[160,384]{1,0:T(8,128)(2,1)} %get-tuple-element.169.refs_0_), channel_id=1, source_target_pairs={{0,16},{8,24},{16,0},{24,8},{1,17},{9,25},{17,1},{25,9},{2,18},{10... | collective-permute-start | bytes 368648 | tf_op jit(solution)/shard_map/ppermute | solution.py:1110
  398.8 14.5 %collective-permute-start.43 = (bf16[160,384]{1,0:T(8,128)(2,1)}, bf16[160,384]{1,0:T(8,128)(2,1)S(1)}, u32[]{:S(2)}, u32[]{:S(2)}) collective-permute-start(bf16[160,384]{1,0:T(8,128)(2,1)} %get-tuple-element.169.refs_0_), channel_id=1, source_target_pairs={{0,8},{8,16},{16,24},{24,0},{1,9},{9,17},{17,25},{25,1},{2,10},{10... | collective-permute-start | bytes 368648 | tf_op jit(solution)/shard_map/ppermute | solution.py:1110
  406.4 10.8 %collective-permute-start.36 = (bf16[80,768]{1,0:T(8,128)(2,1)}, bf16[80,768]{1,0:T(8,128)(2,1)S(1)}, u32[]{:S(2)}, u32[]{:S(2)}) collective-permute-start(bf16[80,768]{1,0:T(8,128)(2,1)} %latent_back.1), channel_id=1, source_target_pairs={{0,8},{8,16},{16,24},{24,0},{1,9},{9,17},{17,25},{25,1},{2,10},{10... | collective-permute-start | bytes 368648 | tf_op jit(solution)/shard_map/ppermute | solution.py:1110
  406.4 16.4 %collective-permute-start.35 = (bf16[80,768]{1,0:T(8,128)(2,1)}, bf16[80,768]{1,0:T(8,128)(2,1)S(1)}, u32[]{:S(2)}, u32[]{:S(2)}) collective-permute-start(bf16[80,768]{1,0:T(8,128)(2,1)} %latent_back.1), channel_id=1, source_target_pairs={{0,16},{8,24},{16,0},{24,8},{1,17},{9,25},{17,1},{25,9},{2,18},{10... | collective-permute-start | bytes 368648 | tf_op jit(solution)/shard_map/ppermute | solution.py:1110
  407.0 15.8 %collective-permute-start.34 = (bf16[80,768]{1,0:T(8,128)(2,1)}, bf16[80,768]{1,0:T(8,128)(2,1)S(1)}, u32[]{:S(2)}, u32[]{:S(2)}) collective-permute-start(bf16[80,768]{1,0:T(8,128)(2,1)} %latent_back.1), channel_id=1, source_target_pairs={{0,24},{8,0},{16,8},{24,16},{1,25},{9,1},{17,9},{25,17},{2,26},{10... | collective-permute-start | bytes 368648 | tf_op jit(solution)/shard_map/ppermute | solution.py:1110
  416.5 11.0 %collective-permute-start.44 = (bf16[4,160,384]{2,1,0:T(8,128)(2,1)}, bf16[4,160,384]{2,1,0:T(8,128)(2,1)S(1)}, u32[]{:S(2)}, u32[]{:S(2)}) collective-permute-start(bf16[4,160,384]{2,1,0:T(8,128)(2,1)} %stack.96.refs_1_), channel_id=1, source_target_pairs={{0,4},{4,0},{1,5},{5,1},{2,6},{6,2},{3,7},{7,3},{8,12},{12,8},{9,1... | collective-permute-start | bytes 1474568 | tf_op jit(solution)/shard_map/ppermute | solution.py:1105
  423.8 14.2 %collective-permute-start.37 = (bf16[4,80,768]{2,1,0:T(8,128)(2,1)S(1)}, bf16[4,80,768]{2,1,0:T(8,128)(2,1)S(1)}, u32[]{:S(2)}, u32[]{:S(2)}) collective-permute-start(bf16[4,80,768]{2,1,0:T(8,128)(2,1)S(1)} %pad_maximum_fusion.refs_1_), channel_id=1, source_target_pairs={{0,1},{1,0},{2,3},{3,2},{4,5},{5,4},{6,7},{7,6},{8,9},{9,8},{10,11... | collective-permute-start | bytes 1474568 | tf_op jit(solution)/shard_map/ppermute | solution.py:1101
  425.0 21.3 %collective-permute-start.38 = (bf16[4,80,768]{2,1,0:T(8,128)(2,1)S(1)}, bf16[4,80,768]{2,1,0:T(8,128)(2,1)S(1)}, u32[]{:S(2)}, u32[]{:S(2)}) collective-permute-start(bf16[4,80,768]{2,1,0:T(8,128)(2,1)S(1)} %pad_maximum_fusion.refs_1_), channel_id=1, source_target_pairs={{0,2},{1,3},{2,0},{3,1},{4,6},{5,7},{6,4},{7,5},{8,10},{9,11},{10,... | collective-permute-start | bytes 1474568 | tf_op jit(solution)/shard_map/ppermute | solution.py:1101
  427.1 20.3 %collective-permute-start.39 = (bf16[4,80,768]{2,1,0:T(8,128)(2,1)S(1)}, bf16[4,80,768]{2,1,0:T(8,128)(2,1)S(1)}, u32[]{:S(2)}, u32[]{:S(2)}) collective-permute-start(bf16[4,80,768]{2,1,0:T(8,128)(2,1)S(1)} %pad_maximum_fusion.refs_1_), channel_id=1, source_target_pairs={{0,3},{1,2},{2,1},{3,0},{4,7},{5,6},{6,5},{7,4},{8,11},{9,10},{10,... | collective-permute-start | bytes 1474568 | tf_op jit(solution)/shard_map/ppermute | solution.py:1101
  (81 other events, 390.8 us)
Sparse Core Ops, SparseCore 0:
  17.4 88.6 all-gather.6
  159.5 69.5 all-gather.4
  257.1 167.6 all-reduce.2

commit v3 on v2

--- a/solution.py
+++ b/solution.py
@@ -155,7 +155,7 @@
     )(*scalars, *args, *deps)
 
 
-def tie(x, *deps):
+def tie(x, *deps, beside=0.0):
     anywhere = pl.BlockSpec(memory_space=pl.ANY)
     return pl.pallas_call(
         lambda *refs: None,
@@ -163,7 +163,7 @@
         in_specs=[anywhere] * (1 + len(deps)),
         out_specs=anywhere,
         input_output_aliases={0: 0},
-        cost_estimate=NO_COST,
+        cost_estimate=cost_of(beside),
         name="tie",
     )(x, *deps)
 
@@ -238,7 +238,7 @@
         steps = clips * blocks
         self.clips, self.blocks, self.size = clips, blocks, 0
         for name, length in (
-            ("side_x", 1), ("side_y", 1), ("mod", 1), ("share", 1), ("some", 2), ("keep", 1), ("tok", 1),
+            ("side_x", 1), ("side_y", 1), ("mod", 1), ("share", 1), ("some", 1), ("keep", 1), ("tok", 1),
             ("clip_plain", clips), ("count_plain", clips), ("text_plain", clips),
             ("read_clip", steps), ("read_block", steps), ("zero_clip", steps), ("zero_block", steps),
             ("clip", clips), ("count", clips), ("text", clips),
@@ -248,7 +248,7 @@
             self.size += length
 
     def calls(self):
-        return ((0, 1), (1, self.clips - 1))
+        return ((0, self.clips),)
 
 
 def plan_kernel(place_ref, frames_ref, lengths_ref, drop_ref, plan, order, *, at, rows, span):
@@ -477,12 +477,9 @@
     if carried:
         before_ref, refs = refs[0], refs[1:]
     refs = refs[extra:]
-    d_video_ref, d_text_ref, weights_ref, d_query_ref = refs[:4]
-    final = call == len(at.calls()) - 1
-    if final:
-        keep_ref, send_ref = refs[4:6]
-        refs = refs[2:]
-    q_down, q_across, d_down, d_across, lse, delta, d_query, queries = refs[4:]
+    d_video_ref, d_text_ref, weights_ref, keep_ref, send_ref = refs[:5]
+    d_query_refs = refs[5:-8]
+    q_down, q_across, d_down, d_across, lse, delta, d_query, queries = refs[-8:]
     step, j = pl.program_id(0), pl.program_id(1)
     place = step + at.calls()[call][0]
     rows, width = video_ref.shape[1:]
@@ -544,13 +541,21 @@
                     head = shard * own_heads + h
                     kind[:, lat * head : lat * (head + 1)] = row
 
-    def block(x, limit, out_ref, share):
-        counted = (lambda a: a) if share is None else (lambda a: a * share)
+    share = plan[at.share].astype(F32)
+
+    def block(x, video_rows):
+        n = x.shape[0]
+        spans = [(0, video_rows, lambda a: a), (video_rows, n, lambda a: a * share)]
+        spans = [span for span in spans if span[0] < span[1]]
         normed, rstd = normalize(x.astype(F32))
         inputs_in = (normed * gain + bias).astype(BF)
         key = dot(inputs_in, pair_ref[:, :width]).astype(BF)
         value = dot(inputs_in, pair_ref[:, width:]).astype(BF)
-        mask = lax.broadcasted_iota(jnp.int32, (x.shape[0], 1), 0) < limit
+        index = lax.broadcasted_iota(jnp.int32, (n, 1), 0)
+        mask = index < count if video_rows else index < text_count
+        if 0 < video_rows < n:
+            mask = jnp.where(index < video_rows, index, n * n) < count
+            mask = mask | ((index >= video_rows) & (index < video_rows + text_count))
         d_keys, d_values = [], []
         for g in range(groups):
             cut = slice(GROUP * HEAD * g, GROUP * HEAD * (g + 1))
@@ -562,34 +567,48 @@
             d_values.append(dot(probs.astype(BF), d_down[g]).astype(BF))
             d_keys.append(dot(d_scores, q_down[g]).astype(BF))
             if g == 0:
-                table = dot_tn(key[:, cut], d_scores)
-                for h, part in enumerate(diagonal_parts(table, lat, own_heads)):
-                    d_query[HEAD * h : HEAD * (h + 1)] += counted(part)
+                for a, b, counted in spans:
+                    table = dot_tn(key[a:b, cut], d_scores[a:b])
+                    for h, part in enumerate(diagonal_parts(table, lat, own_heads)):
+                        d_query[HEAD * h : HEAD * (h + 1)] += counted(part)
         d_key, d_value = jnp.concatenate(d_keys, 1), jnp.concatenate(d_values, 1)
         d_in = dot(d_key, pair_t_ref[:width]) + dot(d_value, pair_t_ref[width:])
-        weights_ref[:own] += counted(dot_tn(d_keys[0], inputs_in)[:own])
-        weights_ref[own : 2 * own] += counted(dot_tn(d_values[0], inputs_in)[:own])
-        weights_ref[3 * own : 3 * own + 8] += counted(row_sums(d_in * normed))
-        weights_ref[3 * own + 8 : 3 * own + 16] += counted(row_sums(d_in))
+        for a, b, counted in spans:
+            rows_in, part = inputs_in[a:b], d_in[a:b]
+            weights_ref[:own] += counted(dot_tn(d_keys[0][a:b], rows_in)[:own])
+            weights_ref[own : 2 * own] += counted(dot_tn(d_values[0][a:b], rows_in)[:own])
+            weights_ref[3 * own : 3 * own + 8] += counted(row_sums(part * normed[a:b]))
+            weights_ref[3 * own + 8 : 3 * own + 16] += counted(row_sums(part))
         scaled = d_in * gain
         d_x = rstd * (
             scaled
             - jnp.mean(scaled, -1, keepdims=True)
             - normed * jnp.mean(scaled * normed, -1, keepdims=True)
         )
-        out_ref[0] = d_x.astype(BF)
-
-    @pl.when(count > 0)
+        if video_rows:
+            d_video_ref[0] = d_x[:video_rows].astype(BF)
+        if video_rows < n:
+            d_text_ref[0] = d_x[video_rows:].astype(BF)
+
+    joined = rows % 16 == 0
+
+    @pl.when((count > 0) & (j > 0 if joined else True))
     def _():
-        block(video_ref[0], count, d_video_ref, None)
+        block(video_ref[0], rows)
+
+    if joined:
+
+        @pl.when((j == 0) & alive & (count > 0))
+        def _():
+            block(jnp.concatenate([video_ref[0], text_ref[0]], 0), rows)
 
     @pl.when((plan[at.some + call] == 0) & (step == 0) & (j == 0))
     def _():
         d_video_ref[...] = jnp.zeros_like(d_video_ref)
 
-    @pl.when((j == 0) & alive)
+    @pl.when((j == 0) & alive & ((count <= 0) if joined else True))
     def _():
-        block(text_ref[0], text_count, d_text_ref, plan[at.share].astype(F32))
+        block(text_ref[0], 0)
 
     @pl.when((j == 0) & jnp.logical_not(alive))
     def _():
@@ -598,22 +617,24 @@
     @pl.when(j == pl.num_programs(1) - 1)
     def _():
         d_rows = (d_query[...] * HEAD**-0.5).astype(BF)
-        d_query_ref[0] = d_rows
+        for zone, d_query_ref in enumerate(d_query_refs):
+
+            @pl.when(place // 2 == zone)
+            def _(d_query_ref=d_query_ref):
+                d_query_ref[0] = d_rows
 
         @pl.when(alive)
         def _():
             weights_ref[2 * own : 3 * own] += dot(d_rows, queries[...])
 
-        if final:
-
-            @pl.when(step == pl.num_programs(0) - 1)
-            def _():
-                half = width // 2
-                side = plan[at.mod]
-                keep_ref[...] = weights_ref[:, pl.ds(pl.multiple_of(side * half, half), half)]
-                send_ref[...] = weights_ref[
-                    :, pl.ds(pl.multiple_of((1 - side) * half, half), half)
-                ].astype(BF)
+        @pl.when(step == pl.num_programs(0) - 1)
+        def _():
+            half = width // 2
+            side = plan[at.mod]
+            keep_ref[...] = weights_ref[:, pl.ds(pl.multiple_of(side * half, half), half)]
+            send_ref[...] = weights_ref[
+                :, pl.ds(pl.multiple_of((1 - side) * half, half), half)
+            ].astype(BF)
 
 
 WEIGHT_ROWS = 64
@@ -639,7 +660,6 @@
     )
     weight_shape = (3 * own + WEIGHT_ROWS, width)
     half_shape = (weight_shape[0], width // 2)
-    final = call == len(at.calls()) - 1
     operands = [video, text, latents, *params, *arrived]
     in_specs = [video_spec, clip_spec(text), clip_spec(latents)]
     in_specs += [full(a) for a in params]
@@ -669,9 +689,12 @@
                 video_spec,
                 clip_spec(text),
                 pl.BlockSpec(weight_shape, lambda s, j, *_: (0, 0)),
-                pl.BlockSpec((1, own, lat), lambda s, j, *_: (s, 0, 0)),
             ]
-            + [pl.BlockSpec(half_shape, lambda s, j, *_: (0, 0))] * (2 * final),
+            + [pl.BlockSpec(half_shape, lambda s, j, *_: (0, 0))] * 2
+            + [
+                pl.BlockSpec((1, own, lat), lambda s, j, p, z=z: (jnp.clip(s - 2 * z, 0, 1), 0, 0))
+                for z in range(at.clips // 2)
+            ],
             scratch_shapes=[
                 pltpu.VMEM((groups, GROUP * lat, GROUP * HEAD), BF),
                 pltpu.VMEM((groups, GROUP * HEAD, GROUP * lat), BF),
@@ -687,14 +710,15 @@
             jax.ShapeDtypeStruct(video.shape, BF),
             jax.ShapeDtypeStruct(text.shape, BF),
             jax.ShapeDtypeStruct(weight_shape, F32),
-            jax.ShapeDtypeStruct((steps, own, lat), BF),
+            jax.ShapeDtypeStruct(half_shape, F32),
+            jax.ShapeDtypeStruct(half_shape, BF),
         ]
-        + [jax.ShapeDtypeStruct(half_shape, F32), jax.ShapeDtypeStruct(half_shape, BF)] * final,
+        + [jax.ShapeDtypeStruct((2, own, lat), BF)] * (at.clips // 2),
         input_output_aliases={start: 0, start + 1: 1},
         compiler_params=pltpu.CompilerParams(
             vmem_limit_bytes=VMEM_LIMIT, dimension_semantics=("arbitrary", "arbitrary")
         ),
-        cost_estimate=cost_of((25.0, 10.0)[call]),
+        cost_estimate=cost_of(10.0),
         name="tokens_back",
     )(plan, *operands)
 
@@ -783,8 +807,8 @@
 
 
 def self_forward_kernel(
-    plan, first_ref, part0, part1, norms_ref, wq, wk, wv, wo, near, far,
-    second_ref, inner_ref, rows_ref, query_t_ref, attended_ref, lse_ref, part_ref, joined,
+    plan, first_ref, part0, part1, norms_ref, wq, wk, wv, wo, near, far, inner1_ref, hidden1_ref,
+    second_ref, inner_ref, rows_ref, query_t_ref, attended_ref, lse_ref, part_ref, moving_ref, joined,
 ):
     join_self(near, far, plan[MOD], joined)
     second = first_ref[...] + received_sum(part0, part1)
@@ -819,6 +843,8 @@
         lse_ref[k] = top + jnp.log2(total)
         terms.append(dot_tn(attended.astype(BF), o[...]))
     part_ref[...] = sum_of(terms).astype(BF)
+    for i, a in enumerate((inner1_ref[...], hidden1_ref[1], inner)):
+        moving_ref[lat * i : lat * (i + 1)] = a
 
 
 def hidden_back(grad_low, pre, up, down):
@@ -856,7 +882,7 @@
 
 def self_back_kernel(
     plan, cotangent_ref, third_ref, part0, part1, norms_ref,
-    rows_ref, query_t_ref, attended_ref, lse_ref, wq, wk, wv, wo, near, far, self_in_ref,
+    rows_ref, query_t_ref, attended_ref, lse_ref, wq, wk, wv, wo, near, far,
     grad_ref, sums_ref, branch_ref, d_rows_ref, low_ref, part_ref, moving_ref, joined,
 ):
     join_self(near, far, plan[MOD], joined)
@@ -903,16 +929,14 @@
             d_rows_ref[k, i] = a
             terms.append(dot(a, weights[i][...]))
             if k == 1:
-                moving_ref[2 * lat :, own * i : own * (i + 1)] = a
+                moving_ref[lat:, own * i : own * (i + 1)] = a
     part_ref[...] = sum_of(terms).astype(BF)
-    moving_ref[:lat] = self_in_ref[...]
-    moving_ref[lat : 2 * lat] = branch
-    moving_ref[2 * lat :, 3 * own :] = attended_ref[1].T.astype(BF)
+    moving_ref[:lat] = branch
+    moving_ref[lat:, 3 * own :] = attended_ref[1].T.astype(BF)
 
 
 def cross_back_kernel(
     plan, grad_ref, second_ref, part0, part1, norms_ref, pre_ref, up0, down0, near, far,
-    inner_ref, hidden_ref,
     out_ref, sums_ref, low_ref, d_pre_ref, part_ref, moving_ref, up1, down1,
 ):
     join_mlp(near, far, plan[MOD], up1, down1)
@@ -930,8 +954,8 @@
         terms.append(term)
     part_ref[...] = sum_of(terms).astype(BF)
     lat = grad.shape[0]
-    for i, a in enumerate((inner_ref[...], d_pre_ref[1], hidden_ref[1], grad_low)):
-        moving_ref[lat * i : lat * (i + 1)] = a
+    moving_ref[:lat] = d_pre_ref[1]
+    moving_ref[lat:] = grad_low
 
 
 def attended_back_kernel(
@@ -992,37 +1016,22 @@
     out_ref[half:] = stat_tile(sums, STAT)
 
 
-def tail_pack_kernel(plan, keep_ref, arrived_ref, query_ref, own_ref, *outs, at):
+def tail_pack_kernel(plan, keep_ref, arrived_ref, own_ref, *outs, at):
     zones = len(outs) + 1
-    own, lat = query_ref.shape[1:]
     step = own_ref.shape[0]
-    for k in range(zones):
+    for k, out in enumerate((own_ref, *outs)):
         cut = pl.ds(pl.multiple_of(lax.rem(plan[at.tok] + k, zones) * step, 16), step)
-        total = keep_ref[cut] + arrived_ref[cut].astype(F32)
-        if k == 0:
-            own_ref[...] = total
-            continue
-        out = outs[k - 1]
-        out[:own] = query_ref[2 * k - 1]
-        out[own : 2 * own] = query_ref[2 * k]
-        for c in range(total.shape[1] // lat):
-            out[2 * own + step * c : 2 * own + step * (c + 1)] = total[
-                :, lat * c : lat * (c + 1)
-            ].astype(BF)
-
-
-def tail_sum_kernel(first_ref, query_ref, own_ref, *refs):
-    parts, (mine_ref, other_ref, share_ref) = refs[:-3], refs[-3:]
-    own, lat = mine_ref.shape
-    step = own_ref.shape[0]
-    for i, (ref, near) in enumerate(((mine_ref, first_ref), (other_ref, query_ref))):
-        cut = slice(own * i, own * (i + 1))
-        ref[...] = (near[0].astype(F32) + sum_of([p[cut].astype(F32) for p in parts])).astype(BF)
-    for c in range(own_ref.shape[1] // lat):
-        lanes = slice(lat * c, lat * (c + 1))
-        cut = slice(2 * own + step * c, 2 * own + step * (c + 1))
-        total = own_ref[:, lanes] + sum_of([p[cut].astype(F32) for p in parts])
-        share_ref[:, lanes] = total.astype(BF)
+        out[...] = (keep_ref[cut] + arrived_ref[cut].astype(F32)).astype(out.dtype)
+
+
+def query_sum_kernel(*refs):
+    parts, outs = refs[:-2], refs[-2:]
+    for i, out in enumerate(outs):
+        out[...] = sum_of([p[i].astype(F32) for p in parts]).astype(BF)
+
+
+def share_sum_kernel(*refs):
+    refs[-1][...] = sum_of([p[...].astype(F32) for p in refs[:-1]]).astype(BF)
 
 
 def token_weights_kernel(plan, mine_ref, other_ref, key_ref, value_ref, query_ref, sums_ref, whole, *, at):
@@ -1072,22 +1081,22 @@
     )
 
 
-def mlp_grads_kernel(inner, d_pre, hidden, low, low_y, moved, out_ref):
+def mlp_grads_kernel(inner, d_pre, hidden, low, *refs, cuts):
     lat, width = inner.shape
-    near = [moved[lat * i : lat * (i + 1)] for i in range(3)]
-    last = low_y.shape[0] - lat
+    out_ref = refs[-1]
+    near = [refs[k][lat * i : lat * (i + 1)] for k, i in cuts]
     out_ref[:width] = (dot_tn(inner[...], d_pre[0]) + dot_tn(near[0], near[1])).astype(BF)
-    out_ref[width:] = (dot_tn(hidden[0], low[:lat]) + dot_tn(near[2], low_y[last:])).astype(BF)
-
-
-def self_grads_kernel(inner, branch, d_rows, low_t, moved, outs):
+    out_ref[width:] = (dot_tn(hidden[0], low[...]) + dot_tn(near[2], near[3])).astype(BF)
+
+
+def self_grads_kernel(inner, branch, d_rows, low_t, early, moved, outs):
     lat = inner.shape[0]
     own = low_t.shape[1]
-    heads_in = [moved[2 * lat :, own * i : own * (i + 1)] for i in range(4)]
+    heads_in = [moved[lat:, own * i : own * (i + 1)] for i in range(4)]
     for i in range(3):
-        part = dot_tn(d_rows[0, i], inner[...]) + dot_tn(heads_in[i], moved[:lat])
+        part = dot_tn(d_rows[0, i], inner[...]) + dot_tn(heads_in[i], early[2 * lat :])
         outs[own * i : own * (i + 1)] = part.astype(BF)
-    part = dot(low_t[0], branch[...]) + dot_tn(heads_in[3], moved[lat : 2 * lat])
+    part = dot(low_t[0], branch[...]) + dot_tn(heads_in[3], moved[:lat])
     outs[3 * own :] = part.astype(BF)
 
 
@@ -1204,13 +1213,14 @@
         name="cross_forward", scalars=(plan,), scratch=[square] * 2,
     )
     mine_y = head_move(tie(other, first), 2)
-    second, self_in, self_rows, self_query_t, self_attended, self_lse, part = kernel_call(
+    second, self_in, self_rows, self_query_t, self_attended, self_lse, part, moving = kernel_call(
         self_forward_kernel,
         [(lw, F32), (lw, BF), ((2, 3, lat, own), BF), ((2, own, lat), BF), ((2, own, lat), F32),
-         ((2, 1, heads * lat), F32), (lw, BF)],
-        first, part, head_move(part, 1), norms, *self_weights, near, far,
+         ((2, 1, heads * lat), F32), (lw, BF), ((3 * lat, width), BF)],
+        first, part, head_move(part, 1), norms, *self_weights, near, far, inner1, hidden1,
         name="self_forward", scalars=(plan,), scratch=[((4, own, width), BF)],
     )
+    early = head_move(moving, 2)
     near3 = tie(near3, second)
     far3 = mod_move(near3)
     third, inner2, hidden2, d_pre2, part, moving = kernel_call(
@@ -1228,10 +1238,10 @@
     grad_third, ffn_sums, self_branch, self_d_rows, self_low, part, moving = kernel_call(
         self_back_kernel,
         [(lw, F32), ((2, width), F32), (lw, BF), ((2, 3, lat, own), BF), ((2, own, lat), BF), (lw, BF),
-         ((3 * lat, width), BF)],
+         ((2 * lat, width), BF)],
         my_cotangent, third, part, received, norms,
-        self_rows, self_query_t, self_attended, self_lse, *self_weights, near, far, self_in,
-        name="self_back", scalars=(plan,), deps=(out_part,), scratch=[((4, own, width), BF)],
+        self_rows, self_query_t, self_attended, self_lse, *self_weights, near, far,
+        name="self_back", scalars=(plan,), deps=(out_part, early), scratch=[((4, own, width), BF)],
     )
     out_moved = head_move(tie(out_part, grad_third), 1)
     moved_self = head_move(moving, 2)
@@ -1242,10 +1252,10 @@
     out_halves = lax.all_gather(out_half, ("tok", "head"))
     grad_second, self_sums, low1, d_pre1, part, moving = kernel_call(
         cross_back_kernel,
-        [(lw, F32), ((2, width), F32), (lw, BF), ((2,) + lw, BF), (lw, BF), ((4 * lat, width), BF)],
+        [(lw, F32), ((2, width), F32), (lw, BF), ((2,) + lw, BF), (lw, BF), ((2 * lat, width), BF)],
         grad_third, second, part, head_move(part, 1), norms, pre1,
-        cross_up, cross_down, near, far, inner1, hidden1,
-        name="cross_back", scalars=(plan,), deps=(out_half,), scratch=[square] * 2,
+        cross_up, cross_down, near, far,
+        name="cross_back", scalars=(plan,), deps=(out_half, halves), scratch=[square] * 2,
     )
 
     pair, pair_t, query_t = kernel_call(
@@ -1259,27 +1269,30 @@
         [(lw, BF), ((2 * own + 2 * STAT, lat), BF), (lw, F32), ((2, width), F32)],
         grad_second, first, part, head_move(part, 1), norms, keep,
         mine, mine_y, cross_output, near, far,
-        name="attended_back", scalars=(plan,), scratch=[((own, width), BF)], deps=(pair,),
+        name="attended_back", scalars=(plan,), scratch=[((own, width), BF)],
+        deps=(pair, moved_self),
     )
 
     (stages,) = kernel_call(
         stack_kernel, [((zones,) + packed.shape, BF)],
         packed, *[tok_move(packed, shards - k) for k in range(1, zones)], name="stack",
+        deps=(moved,),
     )
     arrived = [stages] + [head_move(stages, k) for k in (1, 2, 3)]
     (mlp2,) = kernel_call(
-        mlp_grads_kernel, [((2 * width, width), BF)], inner2, d_pre2, hidden2, my_cotangent, other_cotangent, halves,
+        functools.partial(mlp_grads_kernel, cuts=((0, 0), (0, 1), (0, 2), (1, 0))),
+        [((2 * width, width), BF)], inner2, d_pre2, hidden2, my_cotangent, halves, other_cotangent,
         name="last_weights", beside=4.0, deps=(packed,),
     )
     branch_y = head_move(cross_branch, 2)
     (self_grads,) = kernel_call(
         self_grads_kernel, [((4 * own, width), BF)],
-        self_in, self_branch, self_d_rows, self_low, moved_self, name="self_weights", beside=3.3,
+        self_in, self_branch, self_d_rows, self_low, early, moved_self, name="self_weights", beside=3.3,
         deps=(stages,),
     )
     (mlp1,) = kernel_call(
-        mlp_grads_kernel, [((2 * width, width), BF)], inner1, d_pre1, hidden1,
-        low1, moved, moved, name="cross_weights", beside=4.4,
+        functools.partial(mlp_grads_kernel, cuts=((0, 0), (1, 0), (0, 1), (1, 1))),
+        [((2 * width, width), BF)], inner1, d_pre1, hidden1, low1, early, moved, name="cross_weights", beside=4.4,
         deps=(stages,),
     )
     (output_grad,) = kernel_call(
@@ -1290,13 +1303,9 @@
     params = (norms, pair, pair_t, query_t)
     tokens = (video_tokens, text_tokens, latents)
     d_text = jnp.zeros_like(text_tokens)
-    d_video, d_text, token_weights, first_query = tokens_back(
-        at, plan, 0, *tokens, params, arrived, [d_video, d_text], None, rows,
-        deps=(mlp2, self_grads, mlp1, output_grad),
-    )
-    d_video, d_text, token_weights, d_query, keep_half, send_half = tokens_back(
-        at, plan, 1, *tokens, params, arrived, [d_video, d_text], token_weights, rows,
-        deps=(out_halves,),
+    d_video = tie(d_video, mlp2, self_grads, mlp1, output_grad, *arrived[1:], beside=25.0)
+    d_video, d_text, token_weights, keep_half, send_half, *d_query = tokens_back(
+        at, plan, 0, *tokens, params, arrived, [d_video, d_text], None, rows, deps=(out_halves,)
     )
     sums = lax.psum(counted([mlp2, self_grads, mlp1, output_grad]), ("tok", "mod"))
     mlp2, self_grads, mlp1, output_grad = (a.astype(F32) for a in sums)
@@ -1310,17 +1319,20 @@
 
     whole_rows = token_weights.shape[0]
     step = whole_rows // zones
+    received = [tok_move(d_query[k % zones], k) for k in range(1, shards)]
+    my_query, other_query = kernel_call(
+        query_sum_kernel, [((own, lat), BF)] * 2, d_query[0], *received, name="query_sum"
+    )
     if shards == zones:
         token_own, *pieces = kernel_call(
             functools.partial(tail_pack_kernel, at=at),
-            [((step, width // 2), F32)] + [((2 * own + step * width // 2 // lat, lat), BF)] * (zones - 1),
-            keep_half, mod_move(send_half), d_query,
-            name="tail_pack", scalars=(plan,), deps=(latents_out,),
+            [((step, width // 2), F32)] + [((step, width // 2), BF)] * (zones - 1),
+            keep_half, mod_move(send_half), name="tail_pack", scalars=(plan,),
         )
         received = [tok_move(p, k + 1) for k, p in enumerate(pieces)]
-        my_query, other_query, share = kernel_call(
-            tail_sum_kernel, [((own, lat), BF)] * 2 + [((step, width // 2), BF)],
-            first_query, d_query, token_own, *received, name="tail_sum",
+        (share,) = kernel_call(
+            share_sum_kernel, [((step, width // 2), BF)], token_own, *received,
+            name="share_sum", deps=(my_query, latents_out),
         )
         shares = [share] + [tok_move(share, shards - k) for k in range(1, zones)]
         (shares,) = kernel_call(
@@ -1333,10 +1345,6 @@
             scratch=[((whole_rows, width), F32)],
         )
     else:
-        pieces = jnp.concatenate([first_query, d_query], 0).reshape(zones, 2, own, lat)
-        received = [tok_move(pieces[k % zones], k) for k in range(1, shards)]
-        d_query = sum_of([a.astype(F32) for a in [pieces[0]] + received]).astype(BF)
-        my_query, other_query = d_query[0], d_query[1]
         total = lax.psum(token_weights, ("tok", "mod"))
         d_key_t, d_value_t, d_query_t = (total[own * i : own * (i + 1)] for i in range(3))
         input_sums = jnp.sum(total[3 * own : 3 * own + 16].reshape(2, 8, width), 1)

time: 477 us -> 422 us (0.88)
  Pallas kernels: 246 us -> 169 us
  starting transfers between devices: 58.1 us -> 102 us
  waiting for transfers between devices: 114 us -> 89.9 us
    pallas_call x2 -> x1, Pallas kernels: 121 us -> 53.7 us  [tokens_back(): pl.pallas_call(functools.partial(tokens_back_kernel, at=at, call=call, ca...]
    ppermute x5, starting transfers between devices: 0.08 us -> 37.6 us  [mod_move(): return lax.ppermute(x, 'mod', [(0, 1), (1, 0)])]
    ppermute x25 -> x26, waiting for transfers between devices: 65.8 us -> 50.2 us  [head_move(): return lax.ppermute(x, 'head', [(i, i ^ k) for i in range(n)])]
    ppermute x15 -> x18, waiting for transfers between devices: 47.1 us -> 33.3 us  [tok_move(): return lax.ppermute(x, 'tok', [(i, (i + shift) % n) for i in range(n)])]
    pallas_call x1, Pallas kernels: 33.2 us -> 22.2 us  [tokens_forward(): pl.pallas_call(functools.partial(tokens_forward_kernel, at=at), grid_spec...]
    ppermute x15 -> x18, starting transfers between devices: 24 us -> 33.6 us  [tok_move(): return lax.ppermute(x, 'tok', [(i, (i + shift) % n) for i in range(n)])]
    ppermute x25 -> x26, starting transfers between devices: 33.9 us -> 30.9 us  [head_move(): return lax.ppermute(x, 'head', [(i, i ^ k) for i in range(n)])]
    unnamed x132 -> x130, local copies, waits for them, and re-layouts: 20.4 us -> 21.4 us
  transfers between devices with their start and end apart: 48 -> 52, of which waited for: 25 -> 23; matrix products, arithmetic and copies ran while one was open for 2% -> 2% of each run, Pallas kernels for 51% -> 41%
where the time goes in v3:
time: 422 us; the launch traced here: 414 us
  Pallas kernels  169 us (40%)
  starting transfers between devices  102 us (24%)
  waiting for transfers between devices  89.9 us (21%)
  local copies, waits for them, and re-layouts  33.1 us (8%)
  between operations  14.6 us (3%)
  other arithmetic  5.07 us (1%)
    pallas_call x23, Pallas kernels, kernel_call(): pl.pallas_call(lambda *refs: body(*refs[:first], *refs[first + count:]),...  82.2 us
    pallas_call x1, Pallas kernels, tokens_back(): pl.pallas_call(functools.partial(tokens_back_kernel, at=at, call=call, ca...  53.7 us
    ppermute x26, waiting for transfers between devices, head_move(): return lax.ppermute(x, 'head', [(i, i ^ k) for i in range(n)])  50.2 us
    ppermute x5, starting transfers between devices, mod_move(): return lax.ppermute(x, 'mod', [(0, 1), (1, 0)])  37.6 us
    ppermute x18, starting transfers between devices, tok_move(): return lax.ppermute(x, 'tok', [(i, (i + shift) % n) for i in range(n)])  33.6 us
    ppermute x18, waiting for transfers between devices, tok_move(): return lax.ppermute(x, 'tok', [(i, (i + shift) % n) for i in range(n)])  33.3 us
    ppermute x26, starting transfers between devices, head_move(): return lax.ppermute(x, 'head', [(i, i ^ k) for i in range(n)])  30.9 us
    pallas_call x1, Pallas kernels, tokens_forward(): pl.pallas_call(functools.partial(tokens_forward_kernel, at=at), grid_spec...  22.2 us
  transfers between devices with their start and end apart: 52, of which 23 were waited for; matrix products, arithmetic and copies ran while one was open for 2% of the time, Pallas kernels for 41%

profile of v3, /device:TPU:0, one launch (start us, length us, event | category | flops | bytes accessed | tf_op | source)
XLA Modules:
  0.0 413.8 jit_solution(18417056820267558163)
XLA Ops:
  11.5 3.6 pack_halves.2
  19.6 22.2 %tokens_forward.1 = (bf16[8,1568,768]{2,1,0:T(8,128)(2,1)}, bf16[2,208,128]{2,1,0:T(8,128)(2,1)}, bf16[2,208,128]{2,1,0:T(8,128)(2,1)}, bf16[2,208,128]{2,1,0:T(8,128)(2,1)}, bf16[2,208,128]{2,1,0:T(8,128)(2,1)}) custom-call(s32[151]{0:T(256)} %plan.1.refs_0_, bf16[8,1568,768]{2,1,0:T(8,128)(2,1)} %refs_0_.5, bf16[8,40,768]{2,1,0:T(8,128)(2,1)} %refs_1_.7, ...), custom_call_target="tpu_custom_call" | custom-call | flops 30000001024 | tf_op jit(solution)/shard_map/tokens_forward/pallas_call | solution.py:431
  46.0 3.8 collective-permute-done.refs_3_
  49.8 4.5 %collective-permute-done.1.refs_4_ = bf16[2,208,128]{2,1,0:T(8,128)(2,1)S(1)} collective-permute-done((bf16[2,208,128]{2,1,0:T(8,128)(2,1)}, bf16[2,208,128]{2,1,0:T(8,128)(2,1)S(1)}, u32[]{:S(2)}, u32[]{:S(2)}) %collective-permute-start.1) | collective-permute-done | bytes 106528 | tf_op jit(solution)/shard_map/ppermute | solution.py:1119
  57.2 7.6 %collective-permute-done.6.refs_0_ = bf16[1248,768]{1,0:T(8,128)(2,1)S(1)} collective-permute-done((bf16[1248,768]{1,0:T(8,128)(2,1)}, bf16[1248,768]{1,0:T(8,128)(2,1)S(1)}, u32[]{:S(2)}, u32[]{:S(2)}) %collective-permute-start.6) | collective-permute-done | bytes 1916960 | tf_op jit(solution)/shard_map/ppermute | solution.py:1110
  73.6 4.4 %collective-permute-done.3.refs_2_.refs_1_ = bf16[128,768]{1,0:T(8,128)(2,1)S(1)} collective-permute-done((bf16[128,768]{1,0:T(8,128)(2,1)S(1)}, bf16[128,768]{1,0:T(8,128)(2,1)S(1)}, u32[]{:S(2)}, u32[]{:S(2)}) %collective-permute-start.3) | collective-permute-done | bytes 196640 | tf_op jit(solution)/shard_map/ppermute | solution.py:1110
  78.0 9.1 %collective-permute-done.5.refs_4_.refs_3_ = bf16[128,768]{1,0:T(8,128)(2,1)S(1)} collective-permute-done((bf16[128,768]{1,0:T(8,128)(2,1)S(1)}, bf16[128,768]{1,0:T(8,128)(2,1)S(1)}, u32[]{:S(2)}, u32[]{:S(2)}) %collective-permute-start.5) | collective-permute-done | bytes 196640 | tf_op jit(solution)/shard_map/ppermute | solution.py:1110
  93.0 5.8 %cross_forward.1 = (f32[128,768]{1,0:T(8,128)}, bf16[128,768]{1,0:T(8,128)(2,1)}, f32[2,128,768]{2,1,0:T(8,128)}, bf16[2,128,768]{2,1,0:T(8,128)(2,1)}, bf16[128,768]{1,0:T(8,128)(2,1)}) custom-call(s32[151]{0:T(256)} %plan.1.refs_0_, bf16[128,768]{1,0:T(8,128)(2,1)} %get-tuple-element.103.refs_1_, bf16[128,768]{1,0:T(8,128)(2,1)} %copy-done.7, ...), custom_call_target="tpu_custom_call" | custom-call | tf_op jit(solution)/shard_map/cross_forward/pallas_call | solution.py:144
  100.6 4.6 %collective-permute-done.8.refs_3_ = bf16[128,768]{1,0:T(8,128)(2,1)S(1)} collective-permute-done((bf16[128,768]{1,0:T(8,128)(2,1)}, bf16[128,768]{1,0:T(8,128)(2,1)S(1)}, u32[]{:S(2)}, u32[]{:S(2)}) %collective-permute-start.8) | collective-permute-done | bytes 196640 | tf_op jit(solution)/shard_map/ppermute | solution.py:1110
  105.8 5.7 %self_forward.1 = (f32[128,768]{1,0:T(8,128)}, bf16[128,768]{1,0:T(8,128)(2,1)}, bf16[2,3,128,192]{3,2,1,0:T(8,128)(2,1)}, bf16[2,192,128]{2,1,0:T(8,128)(2,1)},...) custom-call(s32[151]{0:T(256)} %plan.1.refs_0_, ...), custom_call_target="tpu_custom_call" | custom-call | tf_op jit(solution)/shard_map/self_forward/pallas_call | solution.py:144
  111.6 5.0 %collective-permute-done.10.refs_0_ = bf16[768,768]{1,0:T(8,128)(2,1)S(1)} collective-permute-done((bf16[768,768]{1,0:T(8,128)(2,1)}, bf16[768,768]{1,0:T(8,128)(2,1)S(1)}, u32[]{:S(2)}, u32[]{:S(2)}) %collective-permute-start.10) | collective-permute-done | bytes 1179680 | tf_op jit(solution)/shard_map/ppermute | solution.py:1110
  119.4 5.5 %collective-permute-done.9.refs_3_ = bf16[128,768]{1,0:T(8,128)(2,1)S(1)} collective-permute-done((bf16[128,768]{1,0:T(8,128)(2,1)S(1)}, bf16[128,768]{1,0:T(8,128)(2,1)S(1)}, u32[]{:S(2)}, u32[]{:S(2)}) %collective-permute-start.9) | collective-permute-done | bytes 196640 | tf_op jit(solution)/shard_map/ppermute | solution.py:1110
  125.9 5.9 %last_back.1 = (f32[128,768]{1,0:T(8,128)}, bf16[128,768]{1,0:T(8,128)(2,1)}, bf16[2,128,768]{2,1,0:T(8,128)(2,1)}, bf16[2,128,768]{2,1,0:T(8,128)(2,1)}, bf16[1...) custom-call(s32[151]{0:T(256)} %plan.1.refs_0_, f32[128,768]{1,0:T(8,128)} %get-tuple-element.112.refs_1_.refs_2_, ...), custom_call_target="tpu_custom_call" | custom-call | tf_op jit(solution)/shard_map/last_back/pallas_call | solution.py:144
  134.9 3.4 down.1.refs_16_.refs_2_
  140.8 6.3 %self_back.1 = (f32[128,768]{1,0:T(8,128)}, f32[2,768]{1,0:T(2,128)}, bf16[128,768]{1,0:T(8,128)(2,1)}, bf16[2,3,128,192]{3,2,1,0:T(8,128)(2,1)}, bf16[2,192,128...) custom-call(s32[151]{0:T(256)} %plan.1.refs_0_, ...), custom_call_target="tpu_custom_call" | custom-call | tf_op jit(solution)/shard_map/self_back/pallas_call | solution.py:144
  151.2 3.9 collective-permute-done.14.refs_3_
  158.6 6.7 %cross_back.1 = (f32[128,768]{1,0:T(8,128)}, f32[2,768]{1,0:T(2,128)}, bf16[128,768]{1,0:T(8,128)(2,1)}, bf16[2,128,768]{2,1,0:T(8,128)(2,1)}, bf16[128,768]{1,0:T(8,128)(2,1)}, /*index=5*/bf16[256,768]{1,0:T(8,128)(2,1)}) custom-call(s32[151]{0:T(256)} %plan.1.refs_0_, f32[128,768]{1,0:T(8,128)} %get-tuple-element.123.refs_1_, ...), custom_call_target="tpu_custom_call" | custom-call | tf_op jit(solution)/shard_map/cross_back/pallas_call | solution.py:144
  166.3 5.6 %tables.1 = (bf16[768,1536]{1,0:T(8,128)(2,1)}, bf16[1536,768]{1,0:T(8,128)(2,1)}, bf16[768,768]{1,0:T(8,128)(2,1)}) custom-call(s32[151]{0:T(256)} %plan.1.refs_0_, bf16[4,4,144,768]{3,2,1,0:T(8,128)(2,1)} %bitcast.47), custom_call_target="tpu_custom_call" | custom-call | flops 4700000256 | tf_op jit(solution)/shard_map/tables/pallas_call | solution.py:144
  172.7 4.2 %attended_back.1 = (bf16[128,768]{1,0:T(8,128)(2,1)}, bf16[416,128]{1,0:T(8,128)(2,1)}, f32[128,768]{1,0:T(8,128)}, f32[2,768]{1,0:T(2,128)}) custom-call(s32[151]{0:T(256)} %plan.1.refs_0_, f32[128,768]{1,0:T(8,128)} %get-tuple-element.127.refs_1_, f32[128,768]{1,0:T(8,128)} %get-tuple-element.108.refs_1_.refs_2_, ...), custom_call_target="tpu_custom_call" | custom-call | tf_op jit(solution)/shard_map/attended_back/pallas_call | solution.py:144
  183.9 4.3 %last_weights.1.refs_1_ = bf16[1536,768]{1,0:T(8,128)(2,1)} custom-call(bf16[128,768]{1,0:T(8,128)(2,1)} %get-tuple-element.138.refs_0_, bf16[2,128,768]{2,1,0:T(8,128)(2,1)} %get-tuple-element.139.refs_1_, bf16[2,128,768]{2,1,0:T(8,128)(2,1)} %get-tuple-element.116.refs_1_.refs_2_, bf16[128,768]{1,0:T(8,128)(2,1)} %get-tuple-element.114.refs_4_.refs_1_.refs_3_, ...), custom_call_target="tpu_custom_call" | custom-call | flops 4000000000 | tf_op jit(solution)/shard_map/last_weights/pallas_call | solution.py:144
  195.0 4.4 %cross_weights.1.refs_3_ = bf16[1536,768]{1,0:T(8,128)(2,1)} custom-call(bf16[128,768]{1,0:T(8,128)(2,1)} %get-tuple-element.110.refs_11_.refs_0_, bf16[2,128,768]{2,1,0:T(8,128)(2,1)} %get-tuple-element.145.refs_1_, bf16[2,128,768]{2,1,0:T(8,128)(2,1)} %get-tuple-element.111.refs_12_.refs_2_, bf16[128,768]{1,0:T(8,128)(2,1)} %get-tuple-element.146.refs_3_, ...), custom_call_target="tpu_custom_call" | custom-call | flops 4400000000 | tf_op jit(solution)/shard_map/cross_weights/pallas_call | solution.py:144
  199.4 3.4 self_weights.1.refs_2_
  205.7 9.1 %collective-permute-done.25.refs_6_.refs_9_ = bf16[4,416,128]{2,1,0:T(8,128)(2,1)S(1)} collective-permute-done((bf16[4,416,128]{2,1,0:T(8,128)(2,1)}, bf16[4,416,128]{2,1,0:T(8,128)(2,1)S(1)}, u32[]{:S(2)}, u32[]{:S(2)}) %collective-permute-start.25) | collective-permute-done | bytes 426016 | tf_op jit(solution)/shard_map/ppermute | solution.py:1110
  216.5 4.4 %all-gather.5.cloned.1.call-done = bf16[1024,768]{1,0:T(8,128)(2,1)} async-done(((bf16[64,768]{1,0:T(8,128)(2,1)}), bf16[1024,768]{1,0:T(8,128)(2,1)}) %all-gather.5.cloned.1.call-update) | async-done | bytes 1572880 | tf_op jit(solution)/shard_map/all_gather | solution.py:1252
  221.6 53.7 %tokens_back.1 = (bf16[8,1568,768]{2,1,0:T(8,128)(2,1)}, bf16[8,40,768]{2,1,0:T(8,128)(2,1)}, f32[640,768]{1,0:T(8,128)}, f32[640,384]{1,0:T(8,128)}, bf16[640,3...) custom-call(s32[151]{0:T(256)} %plan.1.refs_0_, ...), custom_call_target="tpu_custom_call", output_to_operand_aliasing={{0}: (12, {}), {1}: (13, {})} | custom-call | flops 10000000000 | tf_op jit(solution)/shard_map/tokens_back/pallas_call | solution.py:680
  275.4 37.1 %collective-permute-start.41 = (bf16[640,384]{1,0:T(8,128)(2,1)}, bf16[640,384]{1,0:T(8,128)(2,1)S(1)}, u32[]{:S(2)}, u32[]{:S(2)}) collective-permute-start(bf16[640,384]{1,0:T(8,128)(2,1)} %get-tuple-element.163), channel_id=1, source_target_pairs={{0,4},{4,0},{1,5},{5,1},{2,6},{6,2},{3,7},{7,3},{8,12},{12,8},{9,1... | collective-permute-start | bytes 1474568 | tf_op jit(solution)/shard_map/ppermute | solution.py:1114
  322.2 4.4 %collective-permute-done.29.refs_2_ = bf16[2,192,128]{2,1,0:T(8,128)(2,1)S(1)} collective-permute-done((bf16[2,192,128]{2,1,0:T(8,128)(2,1)}, bf16[2,192,128]{2,1,0:T(8,128)(2,1)S(1)}, u32[]{:S(2)}, u32[]{:S(2)}) %collective-permute-start.29) | collective-permute-done | bytes 98336 | tf_op jit(solution)/shard_map/ppermute | solution.py:1119
  352.7 3.8 collective-permute-start.47
  357.4 5.0 %collective-permute-done.35 = bf16[80,768]{1,0:T(8,128)(2,1)S(1)} collective-permute-done((bf16[80,768]{1,0:T(8,128)(2,1)}, bf16[80,768]{1,0:T(8,128)(2,1)S(1)}, u32[]{:S(2)}, u32[]{:S(2)}) %collective-permute-start.35) | collective-permute-done | bytes 122912 | tf_op jit(solution)/shard_map/ppermute | solution.py:1119
  368.3 3.8 collective-permute-start.46
  374.3 6.5 %collective-permute-done.46.refs_2_ = bf16[160,384]{1,0:T(8,128)(2,1)S(1)} collective-permute-done((bf16[160,384]{1,0:T(8,128)(2,1)}, bf16[160,384]{1,0:T(8,128)(2,1)S(1)}, u32[]{:S(2)}, u32[]{:S(2)}) %collective-permute-start.46) | collective-permute-done | bytes 122912 | tf_op jit(solution)/shard_map/ppermute | solution.py:1119
  403.2 3.8 fusion.2
  (264 shorter events, 138.0 us)
Async XLA Ops:
  7.2 159.1 %all-gather.7.cloned.1.call-start = ((), (), s32[]{:S(2)}) async-start(), calls=%async_computation.1 | async-start | bytes 3760128 | tf_op jit(solution)/shard_map/all_gather | solution.py:1185
  9.1 211.7 %all-gather.5.cloned.1.call-start = ((), (), s32[]{:S(2)}) async-start(), calls=%async_computation | async-start | bytes 1671168 | tf_op jit(solution)/shard_map/all_gather | solution.py:1252
  15.1 49.7 %collective-permute-start.6 = (bf16[1248,768]{1,0:T(8,128)(2,1)}, bf16[1248,768]{1,0:T(8,128)(2,1)S(1)}, u32[]{:S(2)}, u32[]{:S(2)}) collective-permute-start(bf16[1248,768]{1,0:T(8,128)(2,1)} %pack_halves.2), channel_id=1, source_target_pairs={{0,2},{1,3},{2,0},{3,1},{4,6},{5,7},{6,4},{7,5},{8,10},{9,11},{10,... | collective-permute-start | bytes 5750792 | tf_op jit(solution)/shard_map/ppermute | solution.py:1110
  66.1 25.7 %collective-permute-start.7 = (bf16[1248,768]{1,0:T(8,128)(2,1)}, bf16[1248,768]{1,0:T(8,128)(2,1)S(1)}, u32[]{:S(2)}, u32[]{:S(2)}) collective-permute-start(bf16[1248,768]{1,0:T(8,128)(2,1)} %tie.8.refs_10_.refs_9_.refs_14_), channel_id=1, source_target_pairs={{0,4},{4,0},{1,5},{5,1},{2,6},{6,2},{3,7},{7,3},{8,12},{12,8},{9,1... | collective-permute-start | bytes 5750792 | tf_op jit(solution)/shard_map/ppermute | solution.py:1114
  66.5 11.5 %collective-permute-start.3 = (bf16[128,768]{1,0:T(8,128)(2,1)S(1)}, bf16[128,768]{1,0:T(8,128)(2,1)S(1)}, u32[]{:S(2)}, u32[]{:S(2)}) collective-permute-start(bf16[128,768]{1,0:T(8,128)(2,1)S(1)} %copy-done.28), channel_id=1, source_target_pairs={{0,1},{1,0},{2,3},{3,2},{4,5},{5,4},{6,7},{7,6},{8,9},{9,8},{10,11... | collective-permute-start | bytes 589832 | tf_op jit(solution)/shard_map/ppermute | solution.py:1110
  68.0 19.1 %collective-permute-start.5 = (bf16[128,768]{1,0:T(8,128)(2,1)S(1)}, bf16[128,768]{1,0:T(8,128)(2,1)S(1)}, u32[]{:S(2)}, u32[]{:S(2)}) collective-permute-start(bf16[128,768]{1,0:T(8,128)(2,1)S(1)} %copy-done.62), channel_id=1, source_target_pairs={{0,3},{1,2},{2,1},{3,0},{4,7},{5,6},{6,5},{7,4},{8,11},{9,10},{10,... | collective-permute-start | bytes 589832 | tf_op jit(solution)/shard_map/ppermute | solution.py:1110
  69.3 17.8 %collective-permute-start.4 = (bf16[128,768]{1,0:T(8,128)(2,1)S(1)}, bf16[128,768]{1,0:T(8,128)(2,1)S(1)}, u32[]{:S(2)}, u32[]{:S(2)}) collective-permute-start(bf16[128,768]{1,0:T(8,128)(2,1)S(1)} %copy-done.62), channel_id=1, source_target_pairs={{0,2},{1,3},{2,0},{3,1},{4,6},{5,7},{6,4},{7,5},{8,10},{9,11},{10,... | collective-permute-start | bytes 589832 | tf_op jit(solution)/shard_map/ppermute | solution.py:1110
  88.4 28.1 %collective-permute-start.10 = (bf16[768,768]{1,0:T(8,128)(2,1)}, bf16[768,768]{1,0:T(8,128)(2,1)S(1)}, u32[]{:S(2)}, u32[]{:S(2)}) collective-permute-start(bf16[768,768]{1,0:T(8,128)(2,1)} %tie.9), channel_id=1, source_target_pairs={{0,2},{1,3},{2,0},{3,1},{4,6},{5,7},{6,4},{7,5},{8,10},{9,11},{10,... | collective-permute-start | bytes 3538952 | tf_op jit(solution)/shard_map/ppermute | solution.py:1110
  117.5 22.4 %collective-permute-start.13 = (bf16[384,768]{1,0:T(8,128)(2,1)}, bf16[384,768]{1,0:T(8,128)(2,1)S(1)}, u32[]{:S(2)}, u32[]{:S(2)}) collective-permute-start(bf16[384,768]{1,0:T(8,128)(2,1)} %get-tuple-element.122), channel_id=1, source_target_pairs={{0,2},{1,3},{2,0},{3,1},{4,6},{5,7},{6,4},{7,5},{8,10},{9,11},{10,... | collective-permute-start | bytes 1769480 | tf_op jit(solution)/shard_map/ppermute | solution.py:1110
  133.5 24.3 %collective-permute-start.16 = (bf16[384,768]{1,0:T(8,128)(2,1)}, bf16[384,768]{1,0:T(8,128)(2,1)S(1)}, u32[]{:S(2)}, u32[]{:S(2)}) collective-permute-start(bf16[384,768]{1,0:T(8,128)(2,1)} %get-tuple-element.126), channel_id=1, source_target_pairs={{0,2},{1,3},{2,0},{3,1},{4,6},{5,7},{6,4},{7,5},{8,10},{9,11},{10,... | collective-permute-start | bytes 1769480 | tf_op jit(solution)/shard_map/ppermute | solution.py:1110
  149.2 22.7 %collective-permute-start.18 = (bf16[208,128]{1,0:T(8,128)(2,1)}, bf16[208,128]{1,0:T(8,128)(2,1)S(1)}, u32[]{:S(2)}, u32[]{:S(2)}) collective-permute-start(bf16[208,128]{1,0:T(8,128)(2,1)} %tie.12), channel_id=1, source_target_pairs={{0,2},{1,3},{2,0},{3,1},{4,6},{5,7},{6,4},{7,5},{8,10},{9,11},{10,... | collective-permute-start | bytes 159752 | tf_op jit(solution)/shard_map/ppermute | solution.py:1110
  149.7 22.1 %collective-permute-start.19 = (bf16[256,768]{1,0:T(8,128)(2,1)}, bf16[256,768]{1,0:T(8,128)(2,1)S(1)}, u32[]{:S(2)}, u32[]{:S(2)}) collective-permute-start(bf16[256,768]{1,0:T(8,128)(2,1)} %get-tuple-element.131), channel_id=1, source_target_pairs={{0,2},{1,3},{2,0},{3,1},{4,6},{5,7},{6,4},{7,5},{8,10},{9,11},{10,... | collective-permute-start | bytes 1179656 | tf_op jit(solution)/shard_map/ppermute | solution.py:1110
  166.0 22.3 %collective-permute-start.23 = (bf16[256,768]{1,0:T(8,128)(2,1)}, bf16[256,768]{1,0:T(8,128)(2,1)S(1)}, u32[]{:S(2)}, u32[]{:S(2)}) collective-permute-start(bf16[256,768]{1,0:T(8,128)(2,1)} %get-tuple-element.136), channel_id=1, source_target_pairs={{0,2},{1,3},{2,0},{3,1},{4,6},{5,7},{6,4},{7,5},{8,10},{9,11},{10,... | collective-permute-start | bytes 1179656 | tf_op jit(solution)/shard_map/ppermute | solution.py:1110
  182.5 20.3 %collective-permute-start.27 = (bf16[128,768]{1,0:T(8,128)(2,1)}, bf16[128,768]{1,0:T(8,128)(2,1)S(1)}, u32[]{:S(2)}, u32[]{:S(2)}) collective-permute-start(bf16[128,768]{1,0:T(8,128)(2,1)} %get-tuple-element.148.refs_1_), channel_id=1, source_target_pairs={{0,2},{1,3},{2,0},{3,1},{4,6},{5,7},{6,4},{7,5},{8,10},{9,11},{10,... | collective-permute-start | bytes 589832 | tf_op jit(solution)/shard_map/ppermute | solution.py:1110
  191.5 14.2 %collective-permute-start.26 = (bf16[4,416,128]{2,1,0:T(8,128)(2,1)}, bf16[4,416,128]{2,1,0:T(8,128)(2,1)S(1)}, u32[]{:S(2)}, u32[]{:S(2)}) collective-permute-start(bf16[4,416,128]{2,1,0:T(8,128)(2,1)} %stack.95.refs_6_.refs_7_), channel_id=1, source_target_pairs={{0,3},{1,2},{2,1},{3,0},{4,7},{5,6},{6,5},{7,4},{8,11},{9,10},{10,... | collective-permute-start | bytes 1277960 | tf_op jit(solution)/shard_map/ppermute | solution.py:1110
  193.5 21.4 %collective-permute-start.25 = (bf16[4,416,128]{2,1,0:T(8,128)(2,1)}, bf16[4,416,128]{2,1,0:T(8,128)(2,1)S(1)}, u32[]{:S(2)}, u32[]{:S(2)}) collective-permute-start(bf16[4,416,128]{2,1,0:T(8,128)(2,1)} %stack.95.refs_6_.refs_7_), channel_id=1, source_target_pairs={{0,2},{1,3},{2,0},{3,1},{4,6},{5,7},{6,4},{7,5},{8,10},{9,11},{10,... | collective-permute-start | bytes 1277960 | tf_op jit(solution)/shard_map/ppermute | solution.py:1110
  194.6 20.3 %collective-permute-start.24 = (bf16[4,416,128]{2,1,0:T(8,128)(2,1)}, bf16[4,416,128]{2,1,0:T(8,128)(2,1)S(1)}, u32[]{:S(2)}, u32[]{:S(2)}) collective-permute-start(bf16[4,416,128]{2,1,0:T(8,128)(2,1)} %stack.95.refs_6_.refs_7_), channel_id=1, source_target_pairs={{0,1},{1,0},{2,3},{3,2},{4,5},{5,4},{6,7},{7,6},{8,9},{9,8},{10,11... | collective-permute-start | bytes 1277960 | tf_op jit(solution)/shard_map/ppermute | solution.py:1110
  215.7 181.9 %all-reduce.3.cloned.1.call-start = ((), (), s32[]{:S(2)}) async-start(), calls=%async_computation.2 | async-start | bytes 12386304 | tf_op jit(solution)/shard_map/psum | solution.py:1310
  275.4 41.6 %collective-permute-start.41 = (bf16[640,384]{1,0:T(8,128)(2,1)}, bf16[640,384]{1,0:T(8,128)(2,1)S(1)}, u32[]{:S(2)}, u32[]{:S(2)}) collective-permute-start(bf16[640,384]{1,0:T(8,128)(2,1)} %get-tuple-element.163), channel_id=1, source_target_pairs={{0,4},{4,0},{1,5},{5,1},{2,6},{6,2},{3,7},{7,3},{8,12},{12,8},{9,1... | collective-permute-start | bytes 1474568 | tf_op jit(solution)/shard_map/ppermute | solution.py:1114
  314.3 12.3 %collective-permute-start.29 = (bf16[2,192,128]{2,1,0:T(8,128)(2,1)}, bf16[2,192,128]{2,1,0:T(8,128)(2,1)S(1)}, u32[]{:S(2)}, u32[]{:S(2)}) collective-permute-start(bf16[2,192,128]{2,1,0:T(8,128)(2,1)} %get-tuple-element.151), channel_id=1, source_target_pairs={{0,16},{8,24},{16,0},{24,8},{1,17},{9,25},{17,1},{25,9},{2,18},{10... | collective-permute-start | bytes 294920 | tf_op jit(solution)/shard_map/ppermute | solution.py:1119
  314.3 14.0 %collective-permute-start.30 = (bf16[2,192,128]{2,1,0:T(8,128)(2,1)}, bf16[2,192,128]{2,1,0:T(8,128)(2,1)S(1)}, u32[]{:S(2)}, u32[]{:S(2)}) collective-permute-start(bf16[2,192,128]{2,1,0:T(8,128)(2,1)} %get-tuple-element.152), channel_id=1, source_target_pairs={{0,24},{8,0},{16,8},{24,16},{1,25},{9,1},{17,9},{25,17},{2,26},{10... | collective-permute-start | bytes 294920 | tf_op jit(solution)/shard_map/ppermute | solution.py:1119
  320.0 25.4 %collective-permute-start.42 = (bf16[160,384]{1,0:T(8,128)(2,1)}, bf16[160,384]{1,0:T(8,128)(2,1)S(1)}, u32[]{:S(2)}, u32[]{:S(2)}) collective-permute-start(bf16[160,384]{1,0:T(8,128)(2,1)} %get-tuple-element.165), channel_id=1, source_target_pairs={{0,8},{8,16},{16,24},{24,0},{1,9},{9,17},{17,25},{25,1},{2,10},{10... | collective-permute-start | bytes 368648 | tf_op jit(solution)/shard_map/ppermute | solution.py:1119
  334.1 16.0 %collective-permute-start.43 = (bf16[160,384]{1,0:T(8,128)(2,1)}, bf16[160,384]{1,0:T(8,128)(2,1)S(1)}, u32[]{:S(2)}, u32[]{:S(2)}) collective-permute-start(bf16[160,384]{1,0:T(8,128)(2,1)} %get-tuple-element.166), channel_id=1, source_target_pairs={{0,16},{8,24},{16,0},{24,8},{1,17},{9,25},{17,1},{25,9},{2,18},{10... | collective-permute-start | bytes 368648 | tf_op jit(solution)/shard_map/ppermute | solution.py:1119
  337.0 13.2 %collective-permute-start.44 = (bf16[160,384]{1,0:T(8,128)(2,1)}, bf16[160,384]{1,0:T(8,128)(2,1)S(1)}, u32[]{:S(2)}, u32[]{:S(2)}) collective-permute-start(bf16[160,384]{1,0:T(8,128)(2,1)} %get-tuple-element.167), channel_id=1, source_target_pairs={{0,24},{8,0},{16,8},{24,16},{1,25},{9,1},{17,9},{25,17},{2,26},{10... | collective-permute-start | bytes 368648 | tf_op jit(solution)/shard_map/ppermute | solution.py:1119
  343.6 13.8 %collective-permute-start.36 = (bf16[80,768]{1,0:T(8,128)(2,1)}, bf16[80,768]{1,0:T(8,128)(2,1)S(1)}, u32[]{:S(2)}, u32[]{:S(2)}) collective-permute-start(bf16[80,768]{1,0:T(8,128)(2,1)} %latent_back.1), channel_id=1, source_target_pairs={{0,8},{8,16},{16,24},{24,0},{1,9},{9,17},{17,25},{25,1},{2,10},{10... | collective-permute-start | bytes 368648 | tf_op jit(solution)/shard_map/ppermute | solution.py:1119
  344.1 18.3 %collective-permute-start.35 = (bf16[80,768]{1,0:T(8,128)(2,1)}, bf16[80,768]{1,0:T(8,128)(2,1)S(1)}, u32[]{:S(2)}, u32[]{:S(2)}) collective-permute-start(bf16[80,768]{1,0:T(8,128)(2,1)} %latent_back.1), channel_id=1, source_target_pairs={{0,16},{8,24},{16,0},{24,8},{1,17},{9,25},{17,1},{25,9},{2,18},{10... | collective-permute-start | bytes 368648 | tf_op jit(solution)/shard_map/ppermute | solution.py:1119
  345.4 19.2 %collective-permute-start.34 = (bf16[80,768]{1,0:T(8,128)(2,1)}, bf16[80,768]{1,0:T(8,128)(2,1)S(1)}, u32[]{:S(2)}, u32[]{:S(2)}) collective-permute-start(bf16[80,768]{1,0:T(8,128)(2,1)} %latent_back.1), channel_id=1, source_target_pairs={{0,24},{8,0},{16,8},{24,16},{1,25},{9,1},{17,9},{25,17},{2,26},{10... | collective-permute-start | bytes 368648 | tf_op jit(solution)/shard_map/ppermute | solution.py:1119
  352.7 20.0 %collective-permute-start.47 = (bf16[160,384]{1,0:T(8,128)(2,1)}, bf16[160,384]{1,0:T(8,128)(2,1)S(1)}, u32[]{:S(2)}, u32[]{:S(2)}) collective-permute-start(bf16[160,384]{1,0:T(8,128)(2,1)} %share_sum.1.refs_0_), channel_id=1, source_target_pairs={{0,8},{8,16},{16,24},{24,0},{1,9},{9,17},{17,25},{25,1},{2,10},{10... | collective-permute-start | bytes 368648 | tf_op jit(solution)/shard_map/ppermute | solution.py:1119
  364.7 20.2 %collective-permute-start.39 = (bf16[4,80,768]{2,1,0:T(8,128)(2,1)S(1)}, bf16[4,80,768]{2,1,0:T(8,128)(2,1)S(1)}, u32[]{:S(2)}, u32[]{:S(2)}) collective-permute-start(bf16[4,80,768]{2,1,0:T(8,128)(2,1)S(1)} %pad_maximum_fusion.refs_1_), channel_id=1, source_target_pairs={{0,3},{1,2},{2,1},{3,0},{4,7},{5,6},{6,5},{7,4},{8,11},{9,10},{10,... | collective-permute-start | bytes 1474568 | tf_op jit(solution)/shard_map/ppermute | solution.py:1110
  366.0 19.8 %collective-permute-start.38 = (bf16[4,80,768]{2,1,0:T(8,128)(2,1)S(1)}, bf16[4,80,768]{2,1,0:T(8,128)(2,1)S(1)}, u32[]{:S(2)}, u32[]{:S(2)}) collective-permute-start(bf16[4,80,768]{2,1,0:T(8,128)(2,1)S(1)} %pad_maximum_fusion.refs_1_), channel_id=1, source_target_pairs={{0,2},{1,3},{2,0},{3,1},{4,6},{5,7},{6,4},{7,5},{8,10},{9,11},{10,... | collective-permute-start | bytes 1474568 | tf_op jit(solution)/shard_map/ppermute | solution.py:1110
  368.0 17.8 %collective-permute-start.37 = (bf16[4,80,768]{2,1,0:T(8,128)(2,1)S(1)}, bf16[4,80,768]{2,1,0:T(8,128)(2,1)S(1)}, u32[]{:S(2)}, u32[]{:S(2)}) collective-permute-start(bf16[4,80,768]{2,1,0:T(8,128)(2,1)S(1)} %pad_maximum_fusion.refs_1_), channel_id=1, source_target_pairs={{0,1},{1,0},{2,3},{3,2},{4,5},{5,4},{6,7},{7,6},{8,9},{9,8},{10,11... | collective-permute-start | bytes 1474568 | tf_op jit(solution)/shard_map/ppermute | solution.py:1110
  368.3 12.6 %collective-permute-start.46 = (bf16[160,384]{1,0:T(8,128)(2,1)}, bf16[160,384]{1,0:T(8,128)(2,1)S(1)}, u32[]{:S(2)}, u32[]{:S(2)}) collective-permute-start(bf16[160,384]{1,0:T(8,128)(2,1)} %share_sum.1.refs_0_), channel_id=1, source_target_pairs={{0,16},{8,24},{16,0},{24,8},{1,17},{9,25},{17,1},{25,9},{2,18},{10... | collective-permute-start | bytes 368648 | tf_op jit(solution)/shard_map/ppermute | solution.py:1119
  (84 other events, 411.9 us)
Sparse Core Ops, SparseCore 0:
  11.4 88.9 all-gather.6
  157.8 62.9 all-gather.4
  224.1 171.4 all-reduce.2
